TPU v7x, 32 devices: a whole 2x2x4 slice. The times are simulated.
32 devices in a mesh: shock: 8 (over y, x, core), trans: 4 (over z).
Axes of the slice: x: 2, y: 2, z: 4, core: 2. Of those that a mesh axis runs over, the one named last changes fastest.
Arguments:
- positions: float32 [16, 4, 3, 128], P('shock', 'trans'), may hold values from 0.35 to 12.8, as said below
- velocities: float32 [16, 4, 3, 128], P('shock', 'trans'), may hold values from -3 to 3
- features: bfloat16 [16, 4, 576, 128], P('shock', 'trans'), may hold values from -6 to 6
- neighbours: int32 [16, 4, 24, 128], P('shock', 'trans'), may hold values from 0 to 3455, as said below
- counts: int32 [16, 4, 128], P('shock', 'trans'), may hold values from 12 to 24, as said below
- w_first: float32 [64, 8], replicated, may hold values from -2 to 2
- w_second: float32 [192, 64], replicated, may hold values from -0.75 to 0.75
- w_read: float32 [128, 192], replicated, may hold values from -0.4375 to 0.4375
- w_out: float32 [128], replicated, may hold values from -0.5 to 0.5
- fresh_positions: float32 [4, 3, 128], P('trans'), may hold values from 0.35 to 12.8, as said below
- fresh_velocities: float32 [4, 3, 128], P('trans'), may hold values from -3 to 3
Outputs:
- energies: float32 [16, 4, 128], P('shock', 'trans')
- new_positions: float32 [16, 4, 3, 128], P('shock', 'trans')
- new_velocities: float32 [16, 4, 3, 128], P('shock', 'trans')
Inputs may be any that keep to these rules, and one draw needn't show every extreme that they name: `positions`: Block-local coordinates of each block's 128 atoms lie near the sites of a body-centred cubic arrangement of 4 x 4 x 4 cells of side 3.3 inside a cube of side 13.2. `fresh_positions`: as for positions. `neighbours`: each code is ((dz + 1) * 9 + (ds + 1) * 3 + (dt + 1)) * 128 + j with ds, dt, dz in -1 .. 1, naming a lattice neighbour of the atom other than itself at a distance between 1.2 and 8.8; codes of an atom are distinct. `counts`: slots at or beyond an atom's count are padding. Every atom of the block rows below 8 has all 24 slots live.
All inputs are finite; a program needn't handle non-finite values.
Results may differ from a plain program's by a relative error of at most 0.0006.
Values may be sent and summed in bfloat16 or wider, within the bound.
No kernel may reach another device: no remote copies, remote signals or barrier semaphores. Data moves between devices by JAX's collectives and lax.ppermute only.
A program may use at most 128 MiB of HBM per device.

v0:
```python
import math

import jax
import jax.numpy as jnp
from jax import lax
from jax.sharding import PartitionSpec as P

CUTOFF_RADIUS = 9.5
BLOCK_LENGTH = 13.2
KICK_FACTOR = 4.0
MOVE_FACTOR = 0.5
HIGHEST_MODE = lax.Precision.HIGHEST


def extended_2(x, sides, width, wrap):
    for axis, dim in sides:
        count, length = (lax.axis_size(axis), x.shape[dim])
        up = [(i, (i + 1) % count) for i in range(count if wrap else count - 1)]
        down = [(j, i) for i, j in up]
        last = lax.slice_in_dim(x, length - width, length, axis=dim)
        first = lax.slice_in_dim(x, 0, width, axis=dim)
        before = lax.ppermute(last, axis, up)
        after = lax.ppermute(first, axis, down)
        x = jnp.concatenate([before, x, after], axis=dim)
    return x


def shifted(x, axis, by):
    count = lax.axis_size(axis)
    return lax.ppermute(x, axis, [(i, (i + by) % count) for i in range(count)])


def passed_along(block, axis, distance):
    devices = range(lax.axis_size(axis))
    route = [(i - distance, i) for i in devices if i - distance in devices]
    return lax.ppermute(block, axis, route)


def block_energy(window_pos, window_feat, slot_codes, live_count, w_first, w_second, w_read, w_out):
    channels = w_second.shape[0] // 3
    basis_count = w_first.shape[1]
    neighbors = slot_codes.shape[0]
    window_slot = slot_codes % 1152
    image_z = (slot_codes // 1152 - 1).astype(jnp.float32)
    near_block = window_slot // 128
    shock_shift = (near_block // 3 - 1).astype(jnp.float32)
    trans_shift = (near_block % 3 - 1).astype(jnp.float32)
    offsets = jnp.stack([shock_shift, trans_shift, image_z]) * BLOCK_LENGTH
    centre = window_pos[:, 512:640]
    others = jnp.take(window_pos, window_slot, axis=1)
    displace = others + offsets - centre[:, None, :]
    distance = jnp.sqrt(jnp.sum(displace * displace, axis=0))
    heading = displace / distance[None]
    ratio = distance / CUTOFF_RADIUS
    envelope = 1.0 - 28.0 * ratio**6 + 48.0 * ratio**7 - 21.0 * ratio**8
    freqs = math.pi / CUTOFF_RADIUS * jnp.arange(1, basis_count + 1).astype(jnp.float32)
    basis = (
        math.sqrt(2.0 / CUTOFF_RADIUS)
        * jnp.sin(freqs[:, None, None] * distance[None])
        / distance[None]
    )
    slot_rank = lax.broadcasted_iota(jnp.int32, slot_codes.shape, 0)
    live = (slot_rank < live_count[None, :]).astype(jnp.float32)
    hidden = jax.nn.silu(jnp.dot(w_first, basis.reshape(basis_count, -1), precision=HIGHEST_MODE))
    radial = jnp.dot(w_second, hidden, precision=HIGHEST_MODE).reshape(3, channels, neighbors, 128)
    radial = radial * (envelope * live)[None, None]
    unit_x, unit_y, unit_z = (heading[0], heading[1], heading[2])
    root_three = math.sqrt(3.0)
    root_fifteen = math.sqrt(15.0)
    root_five = math.sqrt(5.0)
    harmonics = jnp.stack(
        [
            jnp.ones_like(unit_x),
            root_three * unit_x,
            root_three * unit_y,
            root_three * unit_z,
            root_fifteen * unit_x * unit_y,
            root_fifteen * unit_y * unit_z,
            0.5 * root_five * (3.0 * unit_z * unit_z - 1.0),
            root_fifteen * unit_x * unit_z,
            0.5 * root_fifteen * (unit_x * unit_x - unit_y * unit_y),
        ]
    )
    gathered = (
        jnp.take(window_feat, window_slot, axis=1)
        .reshape(9, channels, neighbors, 128)
        .astype(jnp.float32)
    )
    along = jnp.einsum("cna,mna->mca", radial[0] * gathered[0], harmonics, precision=HIGHEST_MODE)
    direct = jnp.sum(radial[1][None] * gathered, axis=2)
    vector_dot = jnp.sum(gathered[1:4] * harmonics[1:4][:, None], axis=0)
    coupled = jnp.sum(radial[2] * vector_dot, axis=1)
    tensor_sum = (along + direct).at[0].add(coupled) / neighbors
    squares = tensor_sum * tensor_sum
    invariants = jnp.concatenate(
        [squares[0], jnp.sum(squares[1:4], axis=0), jnp.sum(squares[4:9], axis=0)], axis=0
    )
    readout = jax.nn.silu(jnp.dot(w_read, invariants, precision=HIGHEST_MODE))
    return jnp.dot(w_out, readout, precision=HIGHEST_MODE)


def take_window(extended, row, col):
    zero = jnp.zeros((), jnp.int32)
    piece = lax.dynamic_slice(extended, (row, col, zero, zero), (3, 3, extended.shape[2], 128))
    return jnp.moveaxis(piece, 2, 0).reshape(extended.shape[2], 1152)


def sweep(pos_ext, feat_ext, neighbours, counts, w_first, w_second, w_read, w_out):
    nrows, ncols = (neighbours.shape[0], neighbours.shape[1])
    zero = jnp.zeros((), jnp.int32)

    def visit(block_id, carry):
        forces, energies = carry
        row = (block_id // ncols).astype(jnp.int32)
        col = (block_id % ncols).astype(jnp.int32)
        window_pos = take_window(pos_ext, row, col)
        window_feat = take_window(feat_ext, row, col)
        slot_codes = lax.dynamic_slice(
            neighbours, (row, col, zero, zero), (1, 1, neighbours.shape[2], 128)
        )[0, 0]
        live_count = lax.dynamic_slice(counts, (row, col, zero), (1, 1, 128))[0, 0]

        def energy_of(place):
            return block_energy(
                place, window_feat, slot_codes, live_count, w_first, w_second, w_read, w_out
            )

        energy, pullback = jax.vjp(energy_of, window_pos)
        grad = pullback(jnp.ones_like(energy))[0]
        piece = jnp.moveaxis(grad.reshape(3, 3, 3, 128), 0, 2)
        current = lax.dynamic_slice(forces, (row, col, zero, zero), (3, 3, 3, 128))
        forces = lax.dynamic_update_slice(forces, current - piece, (row, col, zero, zero))
        energies = lax.dynamic_update_slice(energies, energy[None, None], (row, col, zero))
        return (forces, energies)

    start = (jnp.zeros(pos_ext.shape, jnp.float32), jnp.zeros((nrows, ncols, 128), jnp.float32))
    return lax.fori_loop(0, nrows * ncols, visit, start)


def local(
    positions,
    velocities,
    features,
    neighbours,
    counts,
    w_first,
    w_second,
    w_read,
    w_out,
    fresh_positions,
    fresh_velocities,
):
    nrows, ncols = (positions.shape[0], positions.shape[1])
    shock_place = lax.axis_index("shock")
    front = lax.axis_size("shock") - 1
    pos_side = extended_2(positions, (("trans", 1),), 1, True)
    pos_ext = extended_2(pos_side, (("shock", 0),), 1, False)
    feat_side = extended_2(features, (("trans", 1),), 1, True)
    feat_ext = extended_2(feat_side, (("shock", 0),), 1, False)
    forces_ext, energies = sweep(
        pos_ext, feat_ext, neighbours, counts, w_first, w_second, w_read, w_out
    )
    from_right = shifted(forces_ext[:, 0], "trans", -1)
    from_left = shifted(forces_ext[:, ncols + 1], "trans", 1)
    folded = forces_ext[:, 1 : ncols + 1]
    folded = folded.at[:, ncols - 1].add(from_right)
    folded = folded.at[:, 0].add(from_left)
    partial_force = folded[1 : nrows + 1]
    from_front = passed_along(folded[0], "shock", -1)
    from_rear = passed_along(folded[nrows + 1], "shock", 1)
    total_force = partial_force.at[nrows - 1].add(from_front)
    total_force = total_force.at[0].add(from_rear)
    new_vel = velocities + KICK_FACTOR * total_force
    moved = positions + MOVE_FACTOR * new_vel
    incoming_pos, incoming_vel = passed_along((moved[0], new_vel[0]), "shock", -1)
    kept_pos = moved[1:]
    kept_vel = new_vel[1:]
    at_front = shock_place == front
    last_pos = jnp.where(at_front, fresh_positions, incoming_pos)
    last_vel = jnp.where(at_front, fresh_velocities, incoming_vel)
    new_positions = jnp.concatenate([kept_pos, last_pos[None]], axis=0)
    new_velocities = jnp.concatenate([kept_vel, last_vel[None]], axis=0)
    return (energies, new_positions, new_velocities)


def solution(mesh):
    return jax.shard_map(
        local,
        mesh=mesh,
        in_specs=(
            P("shock", "trans", None, None),
            P("shock", "trans", None, None),
            P("shock", "trans", None, None),
            P("shock", "trans", None, None),
            P("shock", "trans", None),
            P(),
            P(),
            P(),
            P(),
            P("trans", None, None),
            P("trans", None, None),
        ),
        out_specs=(
            P("shock", "trans", None),
            P("shock", "trans", None, None),
            P("shock", "trans", None, None),
        ),
        check_vma=False,
    )
```

profile of v0, /device:TPU:3, one launch (start us, length us, event | category | flops | bytes accessed | tf_op | source)
XLA Modules:
  0.0 339.0 jit_solution(8056151554600414750)
XLA Ops:
  8.1 5.8 %collective-permute-done.4 = bf16[2,1,576,128]{2,3,1,0:T(8,128)(2,1)S(1)} collective-permute-done((bf16[2,1,576,128]{2,3,1,0:T(8,128)(2,1)S(1)}, bf16[2,1,576,128]{2,3,1,0:T(8,128)(2,1)S(1)}, u32[]{:S(2)}, u32[]{:S(2)}) %collective-permute-start.4) | collective-permute-done | bytes 294944 | tf_op jit(solution)/shard_map/ppermute | solution.py:22
  13.9 7.3 %collective-permute-done.5 = bf16[2,1,576,128]{2,3,1,0:T(8,128)(2,1)S(1)} collective-permute-done((bf16[2,1,576,128]{2,3,1,0:T(8,128)(2,1)S(1)}, bf16[2,1,576,128]{2,3,1,0:T(8,128)(2,1)S(1)}, u32[]{:S(2)}, u32[]{:S(2)}) %collective-permute-start.5) | collective-permute-done | bytes 294944 | tf_op jit(solution)/shard_map/ppermute | solution.py:23
  21.5 4.1 %collective-permute-start.6 = (bf16[1,3,576,128]{2,3,1,0:T(8,128)(2,1)S(1)}, bf16[1,3,576,128]{2,3,1,0:T(8,128)(2,1)S(1)}, u32[]{:S(2)}, u32[]{:S(2)}) collective-permute-start(bf16[1,3,576,128]{2,3,1,0:T(8,128)(2,1)S(1)} %get-tuple-element.539), channel_id=1, source_target_pairs={{0,4},{4,8},{8,12},{12,16},{16,20},{20,24},{24,28},{1,5},{5,9},{9,... | collective-permute-start | bytes 1327112 | tf_op jit(solution)/shard_map/ppermute | solution.py:22
  27.6 4.5 %collective-permute-start.2 = (f32[1,3,3,128]{3,0,2,1:T(1,128)S(1)}, f32[1,3,3,128]{3,0,2,1:T(1,128)S(1)}, u32[]{:S(2)}, u32[]{:S(2)}) collective-permute-start(f32[1,3,3,128]{3,0,2,1:T(1,128)S(1)} %get-tuple-element.543), channel_id=1, source_target_pairs={{0,4},{4,8},{8,12},{12,16},{16,20},{20,24},{24,28},{1,5},{5,9},{9,... | collective-permute-start | bytes 13832 | tf_op jit(solution)/shard_map/ppermute | solution.py:22
  34.1 4.3 %collective-permute-done.3 = f32[1,3,3,128]{3,0,2,1:T(1,128)S(1)} collective-permute-done((f32[1,3,3,128]{3,0,2,1:T(1,128)S(1)}, f32[1,3,3,128]{3,0,2,1:T(1,128)S(1)}, u32[]{:S(2)}, u32[]{:S(2)}) %collective-permute-start.3) | collective-permute-done | bytes 4640 | tf_op jit(solution)/shard_map/ppermute | solution.py:23
  41.3 273.3 %while.23 = (s32[]{:T(128)}, f32[4,3,3,128]{3,0,2,1:T(4,128)}, f32[2,1,128]{2,1,0:T(1,128)}, s32[2,1,24,128]{3,2,1,0:T(8,128)S(1)}, f32[4,3,3,128]{3,0,2,1:T(4,1...) while((s32[]{:T(128)}, f32[4,3,3,128]{3,0,2,1:T(4,128)}, ...), condition=%wide.region_15.16_spmd, body=%wide.region_0.15_spmd.sunk | while | flops 1112283520 | bytes 189631280 | solution.py:137
  43.5 8.1 %gather_fusion = f32[3072,3]{1,0:T(8,128)S(1)} fusion(f32[3,1152]{0,1:T(8,128)S(1)} %bitcast.309, s32[3072]{0:T(1024)S(1)} %get-tuple-element.653), kind=kCustom, calls=%fused_computation.clone.1 | custom fusion | bytes 86016 | tf_op jit(solution)/shard_map/while/body/eval_jaxpr/jvp(jit(_take))/gather | solution.py:50
  57.2 13.5 %gather_fusion.1 = bf16[3072,576]{1,0:T(8,128)(2,1)} fusion(bf16[576,1152]{0,1:T(8,128)(2,1)S(1)} %bitcast.294, s32[3072]{0:T(1024)S(1)} %get-tuple-element.653), kind=kCustom, calls=%fused_computation.1.clone.1 | custom fusion | bytes 7090176 | tf_op jit(solution)/shard_map/while/body/eval_jaxpr/jvp(jit(_take))/gather | solution.py:85
  70.7 4.9 %copy.289 = bf16[24,128,576]{1,0,2:T(8,128)(2,1)S(1)} copy(bf16[24,128,576]{2,1,0:T(8,128)(2,1)} %bitcast.301) | data formatting | bytes 7077888 | tf_op jit(solution)/shard_map/while/body/eval_jaxpr/jvp(jit(_take))/gather | solution.py:85
  75.7 6.8 %copy.290 = bf16[9,64,24,128]{1,2,3,0:T(8,128)(2,1)} copy(bf16[9,64,24,128]{3,2,1,0:T(8,128)(2,1)S(1)} %bitcast.302) | data formatting | bytes 7077888 | tf_op jit(solution)/shard_map/while/body/eval_jaxpr/jvp(jit(_take))/gather | solution.py:85
  82.6 9.1 %fusion.170 = f32[9,64,24,128]{1,2,3,0:T(8,128)} fusion(bf16[9,64,24,128]{1,2,3,0:T(8,128)(2,1)} %copy.290, pred[24,128]{0,1:T(8,128)(4,1)S(1)} %copy.291), kind=kLoop, calls=%fused_computation.6.clone.1 | loop fusion | flops 3538944 | bytes 10619904 | tf_op jit(solution)/shard_map/while/body/eval_jaxpr/jvp()/convert_element_type | solution.py:87
  91.7 5.0 %multiply_reduce_fusion.17 = f32[64,24,128]{0,1,2:T(8,128)} fusion(f32[9,64,24,128]{1,2,3,0:T(8,128)} %fusion.170, f32[3,24,128]{1,2,0:T(8,128)S(1)} %copy-done.5), kind=kLoop, calls=%fused_computation.10.clone.1 | loop fusion | flops 983040 | bytes 3182592 | tf_op jit(solution)/shard_map/while/body/eval_jaxpr/jvp()/reduce_sum | solution.py:91
  102.7 5.1 %copy.287 = f32[3,64,24,128]{1,2,3,0:T(8,128)} copy(f32[3,64,24,128]{3,2,1,0:T(8,128)} %bitcast.303) | data formatting | bytes 4718592 | tf_op jit(solution)/shard_map/while/body/eval_jaxpr/jvp()/reshape | solution.py:65
  113.2 6.3 %multiply_reduce_fusion.16 = f32[9,64,128]{1,2,0:T(8,128)} fusion(f32[64,24,128]{0,1,2:T(8,128)S(1)} %slice_bitcast_fusion.12, bf16[9,64,24,128]{1,2,3,0:T(8,128)(2,1)S(1)} %bitcast.296, pred[24,128]{0,1:T(8,128)(4,1)S(1)} %copy.291), kind=kLoop, calls=%fused_computation.4.clone.1 | loop fusion | flops 7004160 | bytes 4623360 | tf_op jit(solution)/shard_map/while/body/eval_jaxpr/jvp()/reduce_sum | solution.py:90
  132.1 4.2 %fusion.177 = f32[1,64,24,128]{1,2,3,0:T(8,128)S(1)} fusion(f32[9,24,128]{1,0,2:T(8,128)S(1)} %copy.285, f32[9,64,24,128]{1,2,3,0:T(8,128)} %fusion.170, f32[9,64,128]{1,0,2:T(8,128)S(1)} %multiply_multiply_fusion.10), kind=kOutput, calls=%fused_computation.24.clone.1 | convolution fusion | flops 21430272 | bytes 1978368 | tf_op jit(solution)/shard_map/while/body/eval_jaxpr/transpose(jvp(cna,mna->mca))/dot_general | solution.py:89
  139.8 3.8 %copy.297 = f32[3,64,24,128]{3,2,1,0:T(8,128)S(1)} copy(f32[3,64,24,128]{1,2,3,0:T(8,128)} %get-tuple-element.670) | data formatting | bytes 4718592 | tf_op jit(solution)/shard_map/while/body/eval_jaxpr/transpose(jvp())/mul | solution.py:66
  148.4 3.8 %multiply_reduce_fusion.19 = f32[3,24,128]{1,2,0:T(8,128)S(1)} fusion(f32[9,64,24,128]{1,2,3,0:T(8,128)} %fusion.170, f32[64,24,128]{0,1,2:T(8,128)S(1)} %fusion.174), kind=kLoop, calls=%fused_computation.9.clone.1 | loop fusion | flops 1170432 | bytes 3182592 | tf_op jit(solution)/shard_map/while/body/eval_jaxpr/transpose(jvp())/reduce_sum | solution.py:91
  152.3 4.5 %fusion.173 = f32[128,9,24]{2,1,0:T(8,128)S(1)} fusion(f32[9,64,128]{1,0,2:T(8,128)S(1)} %multiply_multiply_fusion.10, f32[3,64,24,128]{1,2,3,0:T(8,128)} %copy-done, f32[9,64,24,128]{1,2,3,0:T(8,128)} %fusion.170), kind=kOutput, calls=%fused_computation.36.clone.1 | convolution fusion | flops 21430272 | bytes 3551232 | tf_op jit(solution)/shard_map/while/body/eval_jaxpr/transpose(jvp(cna,mna->mca))/dot_general | solution.py:89
  158.0 17.2 %scatter_fusion = f32[3,1152]{0,1:T(8,128)S(1)} fusion(f32[3,1152]{0,1:T(8,128)S(1)} %pad.265, s32[3072]{0:T(1024)S(1)} %copy-done.26, f32[3072,3]{1,0:T(8,128)S(1)} %bitcast.307), kind=kCustom, calls=%fused_computation.2.clone.1 | custom fusion | flops 9216 | bytes 122880 | tf_op jit(solution)/shard_map/while/body/eval_jaxpr/transpose(jvp(jit(_take)))/scatter-add | solution.py:50
  180.1 8.1 %gather_fusion = f32[3072,3]{1,0:T(8,128)S(1)} fusion(f32[3,1152]{0,1:T(8,128)S(1)} %bitcast.309, s32[3072]{0:T(1024)S(1)} %get-tuple-element.653), kind=kCustom, calls=%fused_computation.clone.1 | custom fusion | bytes 86016 | tf_op jit(solution)/shard_map/while/body/eval_jaxpr/jvp(jit(_take))/gather | solution.py:50
  193.9 13.5 %gather_fusion.1 = bf16[3072,576]{1,0:T(8,128)(2,1)} fusion(bf16[576,1152]{0,1:T(8,128)(2,1)S(1)} %bitcast.294, s32[3072]{0:T(1024)S(1)} %get-tuple-element.653), kind=kCustom, calls=%fused_computation.1.clone.1 | custom fusion | bytes 7090176 | tf_op jit(solution)/shard_map/while/body/eval_jaxpr/jvp(jit(_take))/gather | solution.py:85
  207.4 4.9 %copy.289 = bf16[24,128,576]{1,0,2:T(8,128)(2,1)S(1)} copy(bf16[24,128,576]{2,1,0:T(8,128)(2,1)} %bitcast.301) | data formatting | bytes 7077888 | tf_op jit(solution)/shard_map/while/body/eval_jaxpr/jvp(jit(_take))/gather | solution.py:85
  212.3 6.8 %copy.290 = bf16[9,64,24,128]{1,2,3,0:T(8,128)(2,1)} copy(bf16[9,64,24,128]{3,2,1,0:T(8,128)(2,1)S(1)} %bitcast.302) | data formatting | bytes 7077888 | tf_op jit(solution)/shard_map/while/body/eval_jaxpr/jvp(jit(_take))/gather | solution.py:85
  219.3 9.1 %fusion.170 = f32[9,64,24,128]{1,2,3,0:T(8,128)} fusion(bf16[9,64,24,128]{1,2,3,0:T(8,128)(2,1)} %copy.290, pred[24,128]{0,1:T(8,128)(4,1)S(1)} %copy.291), kind=kLoop, calls=%fused_computation.6.clone.1 | loop fusion | flops 3538944 | bytes 10619904 | tf_op jit(solution)/shard_map/while/body/eval_jaxpr/jvp()/convert_element_type | solution.py:87
  228.4 5.0 %multiply_reduce_fusion.17 = f32[64,24,128]{0,1,2:T(8,128)} fusion(f32[9,64,24,128]{1,2,3,0:T(8,128)} %fusion.170, f32[3,24,128]{1,2,0:T(8,128)S(1)} %copy-done.5), kind=kLoop, calls=%fused_computation.10.clone.1 | loop fusion | flops 983040 | bytes 3182592 | tf_op jit(solution)/shard_map/while/body/eval_jaxpr/jvp()/reduce_sum | solution.py:91
  239.4 5.1 %copy.287 = f32[3,64,24,128]{1,2,3,0:T(8,128)} copy(f32[3,64,24,128]{3,2,1,0:T(8,128)} %bitcast.303) | data formatting | bytes 4718592 | tf_op jit(solution)/shard_map/while/body/eval_jaxpr/jvp()/reshape | solution.py:65
  249.9 6.3 %multiply_reduce_fusion.16 = f32[9,64,128]{1,2,0:T(8,128)} fusion(f32[64,24,128]{0,1,2:T(8,128)S(1)} %slice_bitcast_fusion.12, bf16[9,64,24,128]{1,2,3,0:T(8,128)(2,1)S(1)} %bitcast.296, pred[24,128]{0,1:T(8,128)(4,1)S(1)} %copy.291), kind=kLoop, calls=%fused_computation.4.clone.1 | loop fusion | flops 7004160 | bytes 4623360 | tf_op jit(solution)/shard_map/while/body/eval_jaxpr/jvp()/reduce_sum | solution.py:90
  268.8 4.2 %fusion.177 = f32[1,64,24,128]{1,2,3,0:T(8,128)S(1)} fusion(f32[9,24,128]{1,0,2:T(8,128)S(1)} %copy.285, f32[9,64,24,128]{1,2,3,0:T(8,128)} %fusion.170, f32[9,64,128]{1,0,2:T(8,128)S(1)} %multiply_multiply_fusion.10), kind=kOutput, calls=%fused_computation.24.clone.1 | convolution fusion | flops 21430272 | bytes 1978368 | tf_op jit(solution)/shard_map/while/body/eval_jaxpr/transpose(jvp(cna,mna->mca))/dot_general | solution.py:89
  276.5 3.8 %copy.297 = f32[3,64,24,128]{3,2,1,0:T(8,128)S(1)} copy(f32[3,64,24,128]{1,2,3,0:T(8,128)} %get-tuple-element.670) | data formatting | bytes 4718592 | tf_op jit(solution)/shard_map/while/body/eval_jaxpr/transpose(jvp())/mul | solution.py:66
  289.0 4.5 %fusion.173 = f32[128,9,24]{2,1,0:T(8,128)S(1)} fusion(f32[9,64,128]{1,0,2:T(8,128)S(1)} %multiply_multiply_fusion.10, f32[3,64,24,128]{1,2,3,0:T(8,128)} %copy-done, f32[9,64,24,128]{1,2,3,0:T(8,128)} %fusion.170), kind=kOutput, calls=%fused_computation.36.clone.1 | convolution fusion | flops 21430272 | bytes 3551232 | tf_op jit(solution)/shard_map/while/body/eval_jaxpr/transpose(jvp(cna,mna->mca))/dot_general | solution.py:89
  294.6 17.2 %scatter_fusion = f32[3,1152]{0,1:T(8,128)S(1)} fusion(f32[3,1152]{0,1:T(8,128)S(1)} %pad.265, s32[3072]{0:T(1024)S(1)} %copy-done.26, f32[3072,3]{1,0:T(8,128)S(1)} %bitcast.307), kind=kCustom, calls=%fused_computation.2.clone.1 | custom fusion | flops 9216 | bytes 122880 | tf_op jit(solution)/shard_map/while/body/eval_jaxpr/transpose(jvp(jit(_take)))/scatter-add | solution.py:50
  324.3 4.4 %collective-permute-start.11 = (f32[1,3,128]{2,0,1:T(1,128)S(1)}, f32[1,3,128]{2,0,1:T(1,128)S(1)}, u32[]{:S(2)}, u32[]{:S(2)}) collective-permute-start(f32[1,3,128]{2,0,1:T(1,128)S(1)} %get-tuple-element.545), channel_id=1, source_target_pairs={{0,4},{4,8},{8,12},{12,16},{16,20},{20,24},{24,28},{1,5},{5,9},{9,... | collective-permute-start | bytes 4616 | tf_op jit(solution)/shard_map/ppermute | solution.py:36
  (381 shorter events, 125.2 us)
Async XLA Ops:
  1.3 6.1 %collective-permute-start = (f32[2,1,3,128]{3,0,2,1:T(2,128)S(1)}, f32[2,1,3,128]{3,0,2,1:T(2,128)S(1)}, u32[]{:S(2)}, u32[]{:S(2)}) collective-permute-start(f32[2,1,3,128]{3,0,2,1:T(2,128)S(1)} %copy.223), channel_id=1, source_target_pairs={{0,1},{1,2},{2,3},{3,0},{4,5},{5,6},{6,7},{7,4},{8,9},{9,10},{10,1... | collective-permute-start | bytes 9224 | tf_op jit(solution)/shard_map/ppermute | solution.py:22
  3.8 10.2 %collective-permute-start.4 = (bf16[2,1,576,128]{2,3,1,0:T(8,128)(2,1)S(1)}, bf16[2,1,576,128]{2,3,1,0:T(8,128)(2,1)S(1)}, u32[]{:S(2)}, u32[]{:S(2)}) collective-permute-start(bf16[2,1,576,128]{2,3,1,0:T(8,128)(2,1)S(1)} %copy.226), channel_id=1, source_target_pairs={{0,1},{1,2},{2,3},{3,0},{4,5},{5,6},{6,7},{7,4},{8,9},{9,10},{10,1... | collective-permute-start | bytes 884744 | tf_op jit(solution)/shard_map/ppermute | solution.py:22
  5.1 16.1 %collective-permute-start.5 = (bf16[2,1,576,128]{2,3,1,0:T(8,128)(2,1)S(1)}, bf16[2,1,576,128]{2,3,1,0:T(8,128)(2,1)S(1)}, u32[]{:S(2)}, u32[]{:S(2)}) collective-permute-start(bf16[2,1,576,128]{2,3,1,0:T(8,128)(2,1)S(1)} %copy.226), channel_id=1, source_target_pairs={{1,0},{2,1},{3,2},{0,3},{5,4},{6,5},{7,6},{4,7},{9,8},{10,9},{11,1... | collective-permute-start | bytes 884744 | tf_op jit(solution)/shard_map/ppermute | solution.py:23
  7.1 20.4 %collective-permute-start.1 = (f32[2,1,3,128]{3,0,2,1:T(2,128)S(1)}, f32[2,1,3,128]{3,0,2,1:T(2,128)S(1)}, u32[]{:S(2)}, u32[]{:S(2)}) collective-permute-start(f32[2,1,3,128]{3,0,2,1:T(2,128)S(1)} %copy.223), channel_id=1, source_target_pairs={{1,0},{2,1},{3,2},{0,3},{5,4},{6,5},{7,6},{4,7},{9,8},{10,9},{11,1... | collective-permute-start | bytes 9224 | tf_op jit(solution)/shard_map/ppermute | solution.py:23
  21.5 19.8 %copy-start.16 = (s32[2,1,24,128]{3,2,1,0:T(8,128)S(1)}, s32[2,1,24,128]{3,2,1,0:T(8,128)}, u32[]{:S(2)}) copy-start(s32[2,1,24,128]{3,2,1,0:T(8,128)} %param.26) | copy-start | bytes 73732
  21.5 17.5 %collective-permute-start.6 = (bf16[1,3,576,128]{2,3,1,0:T(8,128)(2,1)S(1)}, bf16[1,3,576,128]{2,3,1,0:T(8,128)(2,1)S(1)}, u32[]{:S(2)}, u32[]{:S(2)}) collective-permute-start(bf16[1,3,576,128]{2,3,1,0:T(8,128)(2,1)S(1)} %get-tuple-element.539), channel_id=1, source_target_pairs={{0,4},{4,8},{8,12},{12,16},{16,20},{20,24},{24,28},{1,5},{5,9},{9,... | collective-permute-start | bytes 1327112 | tf_op jit(solution)/shard_map/ppermute | solution.py:22
  25.6 13.4 %collective-permute-start.7 = (bf16[1,3,576,128]{2,3,1,0:T(8,128)(2,1)S(1)}, bf16[1,3,576,128]{2,3,1,0:T(8,128)(2,1)S(1)}, u32[]{:S(2)}, u32[]{:S(2)}) collective-permute-start(bf16[1,3,576,128]{2,3,1,0:T(8,128)(2,1)S(1)} %get-tuple-element.540), channel_id=1, source_target_pairs={{4,0},{8,4},{12,8},{16,12},{20,16},{24,20},{28,24},{5,1},{9,5},{13... | collective-permute-start | bytes 1327112 | tf_op jit(solution)/shard_map/ppermute | solution.py:23
  27.6 6.5 %collective-permute-start.2 = (f32[1,3,3,128]{3,0,2,1:T(1,128)S(1)}, f32[1,3,3,128]{3,0,2,1:T(1,128)S(1)}, u32[]{:S(2)}, u32[]{:S(2)}) collective-permute-start(f32[1,3,3,128]{3,0,2,1:T(1,128)S(1)} %get-tuple-element.543), channel_id=1, source_target_pairs={{0,4},{4,8},{8,12},{12,16},{16,20},{20,24},{24,28},{1,5},{5,9},{9,... | collective-permute-start | bytes 13832 | tf_op jit(solution)/shard_map/ppermute | solution.py:22
  32.1 6.3 %collective-permute-start.3 = (f32[1,3,3,128]{3,0,2,1:T(1,128)S(1)}, f32[1,3,3,128]{3,0,2,1:T(1,128)S(1)}, u32[]{:S(2)}, u32[]{:S(2)}) collective-permute-start(f32[1,3,3,128]{3,0,2,1:T(1,128)S(1)} %get-tuple-element.544), channel_id=1, source_target_pairs={{4,0},{8,4},{12,8},{16,12},{20,16},{24,20},{28,24},{5,1},{9,5},{13... | collective-permute-start | bytes 13832 | tf_op jit(solution)/shard_map/ppermute | solution.py:23
  53.6 17.1 %copy-start.14 = (f32[24,128]{1,0:T(8,128)}, f32[24,128]{1,0:T(8,128)S(1)}, u32[]{:S(2)}) copy-start(f32[24,128]{1,0:T(8,128)S(1)} %get-tuple-element.656) | copy-start | bytes 36868 | tf_op jit(solution)/shard_map/while
  82.6 9.1 %copy-start.5 = (f32[3,24,128]{1,2,0:T(8,128)S(1)}, f32[3,24,128]{1,2,0:T(8,128)}, u32[]{:S(2)}) copy-start(f32[3,24,128]{1,2,0:T(8,128)} %copy.292) | copy-start | bytes 110596 | tf_op jit(solution)/shard_map/while
  102.7 10.5 %slice-start = ((s8[7077888]{0:T(1024)(128)(4,1)}), s8[2883584]{0:T(1024)(128)(4,1)S(1)}, s32[]{:S(2)}) async-start(s8[7077888]{0:T(1024)(128)(4,1)} %bitcast.295), calls=%async_computation | async-start | bytes 5767168 | tf_op jit(solution)/shard_map/while
  128.3 8.0 %slice-start.4 = ((s8[4718592]{0:T(1024)(128)(4,1)}), s8[4194304]{0:T(1024)(128)(4,1)S(1)}, s32[]{:S(2)}) async-start(s8[4718592]{0:T(1024)(128)(4,1)} %bitcast.299), calls=%async_computation.4 | async-start | bytes 8388608 | tf_op jit(solution)/shard_map/while
  156.8 18.4 %copy-start.19 = (f32[3,3,3,128]{3,0,2,1:T(4,128)S(1)}, f32[3,3,3,128]{3,0,2,1:T(4,128)}, u32[]{:S(2)}) copy-start(f32[3,3,3,128]{3,0,2,1:T(4,128)} %get-tuple-element.647) | copy-start | bytes 41476 | tf_op jit(solution)/shard_map/while
  157.7 19.4 %copy-start.23 = (f32[128,128]{0,1:T(8,128)S(1)}, f32[128,128]{0,1:T(8,128)}, u32[]{:S(2)}) copy-start(f32[128,128]{0,1:T(8,128)} %copy-done.22) | copy-start | bytes 196612 | tf_op jit(solution)/shard_map/while
  157.8 19.3 %copy-start.35 = (f32[128]{0:T(128)S(1)}, f32[128]{0:T(128)}, u32[]{:S(2)}) copy-start(f32[128]{0:T(128)} %get-tuple-element.713) | copy-start | bytes 1540 | tf_op jit(solution)/shard_map/while
  157.8 19.3 %copy-start.36 = (f32[2,1,128]{2,1,0:T(1,128)S(1)}, f32[2,1,128]{2,1,0:T(1,128)}, u32[]{:S(2)}) copy-start(f32[2,1,128]{2,1,0:T(1,128)} %get-tuple-element.692) | copy-start | bytes 3076 | tf_op jit(solution)/shard_map/while
  157.9 20.0 %copy-start.17 = (s32[2,1,24,128]{3,2,1,0:T(8,128)S(1)}, s32[2,1,24,128]{3,2,1,0:T(8,128)}, u32[]{:S(2)}) copy-start(s32[2,1,24,128]{3,2,1,0:T(8,128)} %get-tuple-element.734) | copy-start | bytes 73732 | tf_op jit(solution)/shard_map/while
  190.3 17.1 %copy-start.14 = (f32[24,128]{1,0:T(8,128)}, f32[24,128]{1,0:T(8,128)S(1)}, u32[]{:S(2)}) copy-start(f32[24,128]{1,0:T(8,128)S(1)} %get-tuple-element.656) | copy-start | bytes 36868 | tf_op jit(solution)/shard_map/while
  219.3 9.1 %copy-start.5 = (f32[3,24,128]{1,2,0:T(8,128)S(1)}, f32[3,24,128]{1,2,0:T(8,128)}, u32[]{:S(2)}) copy-start(f32[3,24,128]{1,2,0:T(8,128)} %copy.292) | copy-start | bytes 110596 | tf_op jit(solution)/shard_map/while
  239.4 10.5 %slice-start = ((s8[7077888]{0:T(1024)(128)(4,1)}), s8[2883584]{0:T(1024)(128)(4,1)S(1)}, s32[]{:S(2)}) async-start(s8[7077888]{0:T(1024)(128)(4,1)} %bitcast.295), calls=%async_computation | async-start | bytes 5767168 | tf_op jit(solution)/shard_map/while
  293.4 18.4 %copy-start.19 = (f32[3,3,3,128]{3,0,2,1:T(4,128)S(1)}, f32[3,3,3,128]{3,0,2,1:T(4,128)}, u32[]{:S(2)}) copy-start(f32[3,3,3,128]{3,0,2,1:T(4,128)} %get-tuple-element.647) | copy-start | bytes 41476 | tf_op jit(solution)/shard_map/while
  294.4 19.4 %copy-start.23 = (f32[128,128]{0,1:T(8,128)S(1)}, f32[128,128]{0,1:T(8,128)}, u32[]{:S(2)}) copy-start(f32[128,128]{0,1:T(8,128)} %copy-done.22) | copy-start | bytes 196612 | tf_op jit(solution)/shard_map/while
  294.4 19.3 %copy-start.35 = (f32[128]{0:T(128)S(1)}, f32[128]{0:T(128)}, u32[]{:S(2)}) copy-start(f32[128]{0:T(128)} %get-tuple-element.713) | copy-start | bytes 1540 | tf_op jit(solution)/shard_map/while
  294.4 19.3 %copy-start.36 = (f32[2,1,128]{2,1,0:T(1,128)S(1)}, f32[2,1,128]{2,1,0:T(1,128)}, u32[]{:S(2)}) copy-start(f32[2,1,128]{2,1,0:T(1,128)} %get-tuple-element.692) | copy-start | bytes 3076 | tf_op jit(solution)/shard_map/while
  294.6 20.0 %copy-start.17 = (s32[2,1,24,128]{3,2,1,0:T(8,128)S(1)}, s32[2,1,24,128]{3,2,1,0:T(8,128)}, u32[]{:S(2)}) copy-start(s32[2,1,24,128]{3,2,1,0:T(8,128)} %get-tuple-element.734) | copy-start | bytes 73732 | tf_op jit(solution)/shard_map/while
  315.3 2.7 collective-permute-start.8
  317.2 4.3 %collective-permute-start.9 = (f32[4,3,128]{2,0,1:T(4,128)S(1)}, f32[4,3,128]{2,0,1:T(4,128)S(1)}, u32[]{:S(2)}, u32[]{:S(2)}) collective-permute-start(f32[4,3,128]{2,0,1:T(4,128)S(1)} %get-tuple-element.542), channel_id=1, source_target_pairs={{0,1},{1,2},{2,3},{3,0},{4,5},{5,6},{6,7},{7,4},{8,9},{9,10},{10,1... | collective-permute-start | bytes 18440 | tf_op jit(solution)/shard_map/ppermute | solution.py:30
  322.2 6.5 %collective-permute-start.10 = (f32[1,3,128]{2,0,1:T(1,128)S(1)}, f32[1,3,128]{2,0,1:T(1,128)S(1)}, u32[]{:S(2)}, u32[]{:S(2)}) collective-permute-start(f32[1,3,128]{2,0,1:T(1,128)S(1)} %get-tuple-element.546), channel_id=1, source_target_pairs={{4,0},{8,4},{12,8},{16,12},{20,16},{24,20},{28,24},{5,1},{9,5},{13... | collective-permute-start | bytes 4616 | tf_op jit(solution)/shard_map/ppermute | solution.py:36
  324.3 5.1 %collective-permute-start.11 = (f32[1,3,128]{2,0,1:T(1,128)S(1)}, f32[1,3,128]{2,0,1:T(1,128)S(1)}, u32[]{:S(2)}, u32[]{:S(2)}) collective-permute-start(f32[1,3,128]{2,0,1:T(1,128)S(1)} %get-tuple-element.545), channel_id=1, source_target_pairs={{0,4},{4,8},{8,12},{12,16},{16,20},{20,24},{24,28},{1,5},{5,9},{9,... | collective-permute-start | bytes 4616 | tf_op jit(solution)/shard_map/ppermute | solution.py:36
  330.1 6.3 %collective-permute-start.12 = (f32[1,3,128]{2,0,1:T(1,128)S(1)}, f32[1,3,128]{2,0,1:T(1,128)S(1)}, u32[]{:S(2)}, u32[]{:S(2)}) collective-permute-start(f32[1,3,128]{2,0,1:T(1,128)S(1)} %get-tuple-element.550), channel_id=1, source_target_pairs={{4,0},{8,4},{12,8},{16,12},{20,16},{24,20},{28,24},{5,1},{9,5},{13... | collective-permute-start | bytes 4616 | tf_op jit(solution)/shard_map/ppermute | solution.py:36
  332.3 6.1 %collective-permute-start.13 = (f32[1,3,128]{2,0,1:T(1,128)S(1)}, f32[1,3,128]{2,0,1:T(1,128)S(1)}, u32[]{:S(2)}, u32[]{:S(2)}) collective-permute-start(f32[1,3,128]{2,0,1:T(1,128)S(1)} %get-tuple-element.548), channel_id=1, source_target_pairs={{4,0},{8,4},{12,8},{16,12},{20,16},{24,20},{28,24},{5,1},{9,5},{13... | collective-permute-start | bytes 4616 | tf_op jit(solution)/shard_map/ppermute | solution.py:36
  (69 other events, 217.9 us)
where the time goes:
time: 341 us; the launch traced here: 339 us
  local copies, waits for them, and re-layouts  125 us (37%)
  other arithmetic  117 us (34%)
  matrix products  38.7 us (11%)
  starting transfers between devices  29.9 us (9%)
  waiting for transfers between devices  25.9 us (8%)
    gather x6, local copies, waits for them, and re-layouts, block_energy(): jnp.take(window_feat, window_slot, axis=1)  50.6 us
    scatter-add x2, other arithmetic, block_energy(): others = jnp.take(window_pos, window_slot, axis=1)  34.3 us
    dot_general x6, matrix products, block_energy(): jnp.einsum('cna,mna->mca', radial[0] * gathered[0], harmonics, precision=...  24.8 us
    reduce_sum x4, other arithmetic, block_energy(): direct = jnp.sum(radial[1][None] * gathered, axis=2)  18.3 us
    convert_element_type x2, other arithmetic, block_energy(): gathered = jnp.take(window_feat, window_slot, axis=1).reshape(9, channels...  18.2 us
    reduce_sum x4, other arithmetic, block_energy(): vector_dot = jnp.sum(gathered[1:4] * harmonics[1:4][:, None], axis=0)  17.7 us
    gather x4, local copies, waits for them, and re-layouts, block_energy(): others = jnp.take(window_pos, window_slot, axis=1)  17.2 us
    while x176, local copies, waits for them, and re-layouts  14.5 us
  transfers between devices with their start and end apart: 14, of which 8 were waited for; matrix products, arithmetic and copies ran while one was open for 1% of the time, Pallas kernels for 0%

commit v1 on v0

v1 whole, which is shorter than its diff:
```python
import functools
import math

import jax
import jax.numpy as jnp
from jax import lax
from jax.experimental import pallas as pl
from jax.experimental.pallas import tpu as pltpu
from jax.sharding import PartitionSpec as P

CUTOFF_RADIUS = 9.5
BLOCK_LENGTH = 13.2
KICK_FACTOR = 4.0
MOVE_FACTOR = 0.5
F32 = jnp.float32
BF16 = jnp.bfloat16
LANES = 128


def extended_2(x, sides, width, wrap):
    for axis, dim in sides:
        count, length = (lax.axis_size(axis), x.shape[dim])
        up = [(i, (i + 1) % count) for i in range(count if wrap else count - 1)]
        down = [(j, i) for i, j in up]
        last = lax.slice_in_dim(x, length - width, length, axis=dim)
        first = lax.slice_in_dim(x, 0, width, axis=dim)
        before = lax.ppermute(last, axis, up)
        after = lax.ppermute(first, axis, down)
        x = jnp.concatenate([before, x, after], axis=dim)
    return x


def shifted(x, axis, by):
    count = lax.axis_size(axis)
    return lax.ppermute(x, axis, [(i, (i + by) % count) for i in range(count)])


def passed_along(block, axis, distance):
    devices = range(lax.axis_size(axis))
    route = [(i - distance, i) for i in devices if i - distance in devices]
    return lax.ppermute(block, axis, route)


def halves(x):
    hi = x.astype(BF16)
    lo = (x - hi.astype(F32)).astype(BF16)
    return hi, lo


def weight_rows(w):
    hi, lo = halves(w)
    return jnp.concatenate([hi, hi, lo], axis=1)


def value_rows(x):
    hi, lo = halves(x)
    return jnp.concatenate([hi, lo, hi], axis=0)


def dot(a, b):
    return jnp.dot(a, b, preferred_element_type=F32)


def sin_cos_half_turns(t):
    n = jnp.floor(t + 0.5)
    r = t - n
    odd = n - 2.0 * jnp.floor(0.5 * n)
    sign = 1.0 - 2.0 * odd
    x = math.pi * r
    y = x * x
    s = 1.0 + y * (
        -1.0 / 6
        + y
        * (
            1.0 / 120
            + y * (-1.0 / 5040 + y * (1.0 / 362880 + y * (-1.0 / 39916800 + y * (1.0 / 6227020800.0))))
        )
    )
    c = 1.0 + y * (
        -0.5
        + y
        * (
            1.0 / 24
            + y
            * (-1.0 / 720 + y * (1.0 / 40320 + y * (-1.0 / 3628800 + y * (1.0 / 479001600.0))))
        )
    )
    return sign * x * s, sign * c


def kernel(
    rows,
    cols,
    channels,
    slots,
    feat_ref,
    pos_ref,
    codes_ref,
    counts_ref,
    w1_ref,
    w2_ref,
    w2t_ref,
    wr_ref,
    wrt_ref,
    wo_ref,
    en_ref,
    force_ref,
    win,
    onehot,
    near,
    xg,
    wsc,
    qsc,
    geo,
    har,
    acc,
    inv,
    dws,
    dys,
    lhs,
):
    blocks = rows * cols
    pairs = slots // 2
    wide = 2 * LANES
    group = 16
    hidden = qsc.shape[2]
    root3, root5, root15 = math.sqrt(3.0), math.sqrt(5.0), math.sqrt(15.0)

    def geometry(b, _):
        r, c = b // cols, b % cols
        for k in range(9):
            win[b, :, k * LANES : (k + 1) * LANES] = feat_ref[r + k // 3, c + k % 3]
        codes = codes_ref[r, c]
        zq = (codes >= 1152).astype(jnp.int32) + (codes >= 2304).astype(jnp.int32)
        slot = codes - 1152 * zq
        near_block = lax.shift_right_logical(slot, 7)
        atom = slot & 127
        row3 = (near_block >= 3).astype(jnp.int32) + (near_block >= 6).astype(jnp.int32)
        shift_x = (row3 - 1).astype(F32) * BLOCK_LENGTH
        shift_y = (near_block - 3 * row3 - 1).astype(F32) * BLOCK_LENGTH
        shift_z = (zq - 1).astype(F32) * BLOCK_LENGTH
        centre = pos_ref[r + 1, c + 1]
        found = [jnp.zeros((slots, LANES), F32) for _ in range(3)]
        for k in range(9):
            place = pos_ref[r + k // 3, c + k % 3]
            here = near_block == k
            for i in range(3):
                line = jnp.broadcast_to(place[i : i + 1], (slots, LANES))
                value = jnp.take_along_axis(line, atom, axis=1, mode="promise_in_bounds")
                found[i] = jnp.where(here, value, found[i])
        rx = found[0] + shift_x - centre[0:1]
        ry = found[1] + shift_y - centre[1:2]
        rz = found[2] + shift_z - centre[2:3]
        dist = jnp.sqrt(rx * rx + ry * ry + rz * rz)
        recip = 1.0 / dist
        ux, uy, uz = rx * recip, ry * recip, rz * recip
        x = dist * (1.0 / CUTOFF_RADIUS)
        x2 = x * x
        x5 = x2 * x2 * x
        live = lax.broadcasted_iota(jnp.int32, (slots, LANES), 0) < counts_ref[r, c]
        scale = jnp.where(live, 1.0 / slots, 0.0)
        env = (1.0 - x5 * x * (28.0 - x * (48.0 - 21.0 * x))) * scale
        denv = (-168.0 / CUTOFF_RADIUS) * x5 * (1.0 - x * (2.0 - x)) * scale
        geo[b, 0] = dist
        geo[b, 1] = recip
        geo[b, 2] = env
        geo[b, 3] = denv
        geo[b, 4] = ux
        geo[b, 5] = uy
        geo[b, 6] = uz
        geo[b, 7] = atom.astype(F32)
        geo[b, 8] = near_block.astype(F32)
        har[b, 0] = root3 * ux
        har[b, 1] = root3 * uy
        har[b, 2] = root3 * uz
        har[b, 3] = root15 * ux * uy
        har[b, 4] = root15 * uy * uz
        har[b, 5] = 0.5 * root5 * (3.0 * uz * uz - 1.0)
        har[b, 6] = root15 * ux * uz
        har[b, 7] = 0.5 * root15 * (ux * ux - uy * uy)
        acc[b] = jnp.zeros(acc.shape[1:], F32)
        return 0

    lax.fori_loop(0, blocks, geometry, 0)

    def wide_row(b, k, p):
        return jnp.concatenate(
            [geo[b, k, pl.ds(2 * p, 1), :], geo[b, k, pl.ds(2 * p + 1, 1), :]], axis=1
        )

    def forward(step, _):
        b, p = step // pairs, step % pairs
        atom = wide_row(b, 7, p)
        place = wide_row(b, 8, p)
        sub = lax.broadcasted_iota(jnp.int32, (LANES, wide), 0).astype(F32)
        hot = jnp.where(sub == atom, 1.0, 0.0).astype(BF16)
        near[step] = hot
        hot3 = hot.reshape(LANES // 16, 16, wide)
        for k in range(9):
            mask = jnp.broadcast_to(jnp.where(place == k, 1.0, 0.0), (16, wide)).astype(BF16)
            onehot[k * LANES : (k + 1) * LANES, :] = (hot3 * mask[None]).reshape(LANES, wide)
        xg[step] = dot(win[b], onehot[...])
        dist, recip = wide_row(b, 0, p), wide_row(b, 1, p)
        env, denv = wide_row(b, 2, p), wide_row(b, 3, p)
        order = (lax.broadcasted_iota(jnp.int32, (8, wide), 0) + 1).astype(F32)
        sin, cos = sin_cos_half_turns(order * (dist * (1.0 / CUTOFF_RADIUS)))
        norm = math.sqrt(2.0 / CUTOFF_RADIUS)
        basis = norm * sin * recip
        slope = ((norm * math.pi / CUTOFF_RADIUS) * order * cos - basis) * recip
        both = jnp.concatenate([basis, slope], axis=1)
        hi = both.astype(BF16).astype(F32)
        lo = both - hi
        pre2 = dot(w1_ref[...], jnp.concatenate([hi, lo, hi, lo], axis=0).astype(BF16))
        pre, dpre = pre2[:, :wide], pre2[:, wide:]
        gate = 1.0 / (1.0 + jnp.exp(-pre))
        h = pre * gate
        dh = gate + h * (1.0 - gate)
        qsc[step] = dh * dpre * env + h * denv
        wsc[step] = dot(w2_ref[...], value_rows(h * env))
        for g in range(channels // group):
            lo_c = g * group
            total = [acc[b, m, lo_c : lo_c + group, :] for m in range(9)]
            for s in range(2):
                ln = slice(s * LANES, (s + 1) * LANES)
                xs = [
                    xg[step, m * channels + lo_c : m * channels + lo_c + group, ln]
                    for m in range(9)
                ]
                w0, w1, w2 = [
                    wsc[step, k * channels + lo_c : k * channels + lo_c + group, ln]
                    for k in range(3)
                ]
                ys = [har[b, m, pl.ds(2 * p + s, 1), :] for m in range(8)]
                t0 = w0 * xs[0]
                vec = xs[1] * ys[0] + xs[2] * ys[1] + xs[3] * ys[2]
                total[0] = total[0] + (t0 + w1 * xs[0]) + w2 * vec
                for m in range(1, 9):
                    total[m] = total[m] + (t0 * ys[m - 1] + w1 * xs[m])
            for m in range(9):
                acc[b, m, lo_c : lo_c + group, :] = total[m]
        return 0

    lax.fori_loop(0, blocks * pairs, forward, 0)

    for b in range(blocks):
        ln = slice(b * LANES, (b + 1) * LANES)
        a = [acc[b, m] for m in range(9)]
        inv[0:channels, ln] = a[0] * a[0]
        inv[channels : 2 * channels, ln] = a[1] * a[1] + a[2] * a[2] + a[3] * a[3]
        inv[2 * channels :, ln] = (
            a[4] * a[4] + a[5] * a[5] + a[6] * a[6] + a[7] * a[7] + a[8] * a[8]
        )
    z = dot(wr_ref[...], value_rows(inv[...]))
    gate = 1.0 / (1.0 + jnp.exp(-z))
    out = z * gate
    wo = wo_ref[...]
    energy = jnp.sum(out * wo, axis=0, keepdims=True)
    dinv = dot(wrt_ref[...], value_rows(wo * (gate + out * (1.0 - gate))))
    for b in range(blocks):
        ln = slice(b * LANES, (b + 1) * LANES)
        en_ref[b // cols, b % cols] = energy[:, ln]
        for m in range(9):
            part = 0 if m == 0 else (1 if m < 4 else 2)
            d = dinv[part * channels : (part + 1) * channels, ln]
            acc[b, m] = 2.0 * acc[b, m] * d

    def backward(step, _):
        b, p = step // pairs, step % pairs
        for s in range(2):
            ln = slice(s * LANES, (s + 1) * LANES)
            ys = [har[b, m, pl.ds(2 * p + s, 1), :] for m in range(8)]
            dy = [jnp.zeros((group, LANES), F32) for _ in range(8)]
            for g in range(channels // group):
                lo_c = g * group
                xs = [
                    xg[step, m * channels + lo_c : m * channels + lo_c + group, ln]
                    for m in range(9)
                ]
                gs = [acc[b, m, lo_c : lo_c + group, :] for m in range(9)]
                w0 = wsc[step, lo_c : lo_c + group, ln]
                w2 = wsc[step, 2 * channels + lo_c : 2 * channels + lo_c + group, ln]
                t0 = w0 * xs[0]
                t2 = w2 * gs[0]
                vec = xs[1] * ys[0] + xs[2] * ys[1] + xs[3] * ys[2]
                along = gs[0]
                direct = gs[0] * xs[0]
                for m in range(1, 9):
                    along = along + gs[m] * ys[m - 1]
                    direct = direct + gs[m] * xs[m]
                    dy[m - 1] = dy[m - 1] + t0 * gs[m]
                    if m < 4:
                        dy[m - 1] = dy[m - 1] + t2 * xs[m]
                dw = [along * xs[0], direct, gs[0] * vec]
                for k in range(3):
                    hi, lo = halves(dw[k])
                    at = k * channels + lo_c
                    dws[at : at + group, ln] = hi
                    dws[3 * channels + at : 3 * channels + at + group, ln] = lo
                    dws[6 * channels + at : 6 * channels + at + group, ln] = hi
            for m in range(8):
                dys[m, pl.ds(2 * p + s, 1), :] = jnp.sum(dy[m], axis=0, keepdims=True)
        dh = dot(w2t_ref[...], dws[...])
        dd = jnp.sum(dh * qsc[step], axis=0, keepdims=True)
        dys[8, pl.ds(2 * p, 1), :] = dd[:, :LANES]
        dys[8, pl.ds(2 * p + 1, 1), :] = dd[:, LANES:]
        return 0

    force_ref[...] = jnp.zeros(force_ref.shape, F32)

    def pull(b, _):
        lax.fori_loop(b * pairs, (b + 1) * pairs, backward, 0)
        r, c = b // cols, b % cols
        ux, uy, uz, recip = geo[b, 4], geo[b, 5], geo[b, 6], geo[b, 1]
        d1, d2, d3, d4, d5, d6, d7, d8 = [dys[m] for m in range(8)]
        gx = root3 * d1 + root15 * (uy * d4 + uz * d7 + ux * d8)
        gy = root3 * d2 + root15 * (ux * d4 + uz * d5 - uy * d8)
        gz = root3 * d3 + root15 * (uy * d5 + ux * d7) + (3.0 * root5) * uz * d6
        radial = dys[8] - (ux * gx + uy * gy + uz * gz) * recip
        grads = [gx * recip + ux * radial, gy * recip + uy * radial, gz * recip + uz * radial]
        for i in range(3):
            here = jnp.sum(grads[i], axis=0, keepdims=True)
            force_ref[r + 1, c + 1, i : i + 1, :] += here
        split = [halves(g) for g in grads]
        which = lax.broadcasted_iota(jnp.int32, (16, LANES), 0).astype(F32)
        place = geo[b, 8]
        for n in range(slots):
            ln = slice(n * LANES, (n + 1) * LANES)
            hit = which == place[n : n + 1]
            for i in range(3):
                for v in range(2):
                    line = split[i][v][n : n + 1].astype(F32)
                    at = (3 * v + i) * 16
                    lhs[at : at + 16, ln] = jnp.where(hit, line, 0.0).astype(BF16)
        total = jnp.zeros((96, LANES), F32)
        for p in range(pairs):
            total = total + lax.dot_general(
                lhs[:, p * wide : (p + 1) * wide],
                near[b * pairs + p],
                (((1,), (1,)), ((), ())),
                preferred_element_type=F32,
            )
        for i in range(3):
            for k in range(9):
                at = i * 16 + k
                value = total[at : at + 1] + total[48 + at : 49 + at]
                force_ref[r + k // 3, c + k % 3, i : i + 1, :] -= value
        return 0

    lax.fori_loop(0, blocks, pull, 0)


def sweep(pos_ext, feat_ext, neighbours, counts, w_first, w_second, w_read, w_out):
    rows, cols, slots = neighbours.shape[0], neighbours.shape[1], neighbours.shape[2]
    hidden, channels = w_first.shape[0], w_second.shape[0] // 3
    units = w_read.shape[0]
    blocks, pairs = rows * cols, slots // 2
    wide = 2 * LANES
    hi, lo = halves(w_first)
    w1 = jnp.concatenate([hi, hi, lo, lo], axis=1)
    vmem = pl.BlockSpec(memory_space=pltpu.VMEM)
    energies, forces = pl.pallas_call(
        functools.partial(kernel, rows, cols, channels, slots),
        out_shape=(
            jax.ShapeDtypeStruct((rows, cols, 1, LANES), F32),
            jax.ShapeDtypeStruct((rows + 2, cols + 2, 3, LANES), F32),
        ),
        in_specs=[vmem] * 10,
        out_specs=(vmem, vmem),
        scratch_shapes=[
            pltpu.VMEM((blocks, 9 * channels, 9 * LANES), BF16),
            pltpu.VMEM((9 * LANES, wide), BF16),
            pltpu.VMEM((blocks * pairs, LANES, wide), BF16),
            pltpu.VMEM((blocks * pairs, 9 * channels, wide), F32),
            pltpu.VMEM((blocks * pairs, 3 * channels, wide), F32),
            pltpu.VMEM((blocks * pairs, hidden, wide), F32),
            pltpu.VMEM((blocks, 9, slots, LANES), F32),
            pltpu.VMEM((blocks, 8, slots, LANES), F32),
            pltpu.VMEM((blocks, 9, channels, LANES), F32),
            pltpu.VMEM((3 * channels, blocks * LANES), F32),
            pltpu.VMEM((9 * channels, wide), BF16),
            pltpu.VMEM((9, slots, LANES), F32),
            pltpu.VMEM((96, slots * LANES), BF16),
        ],
        compiler_params=pltpu.CompilerParams(vmem_limit_bytes=56 * 1024 * 1024),
        cost_estimate=pl.CostEstimate(
            flops=2 * 9 * channels * 9 * LANES * slots * LANES * blocks,
            bytes_accessed=4 * 1024 * 1024,
            transcendentals=0,
        ),
    )(
        feat_ext,
        pos_ext,
        neighbours,
        counts.reshape(rows, cols, 1, LANES),
        w1,
        weight_rows(w_second),
        weight_rows(w_second.T),
        weight_rows(w_read),
        weight_rows(w_read.T),
        w_out.reshape(units, 1),
    )
    return forces, energies.reshape(rows, cols, LANES)


def local(
    positions,
    velocities,
    features,
    neighbours,
    counts,
    w_first,
    w_second,
    w_read,
    w_out,
    fresh_positions,
    fresh_velocities,
):
    nrows, ncols = (positions.shape[0], positions.shape[1])
    shock_place = lax.axis_index("shock")
    front = lax.axis_size("shock") - 1
    pos_side = extended_2(positions, (("trans", 1),), 1, True)
    pos_ext = extended_2(pos_side, (("shock", 0),), 1, False)
    feat_side = extended_2(features, (("trans", 1),), 1, True)
    feat_ext = extended_2(feat_side, (("shock", 0),), 1, False)
    forces_ext, energies = sweep(
        pos_ext, feat_ext, neighbours, counts, w_first, w_second, w_read, w_out
    )
    from_right = shifted(forces_ext[:, 0], "trans", -1)
    from_left = shifted(forces_ext[:, ncols + 1], "trans", 1)
    folded = forces_ext[:, 1 : ncols + 1]
    folded = folded.at[:, ncols - 1].add(from_right)
    folded = folded.at[:, 0].add(from_left)
    packed = jnp.concatenate([folded[:2], velocities[:1], positions[:1]], axis=0)
    ahead = passed_along(packed, "shock", -1)
    force = folded[2 : nrows + 2]
    force = force.at[nrows - 2].add(ahead[0])
    force = force.at[nrows - 1].add(ahead[1])
    old_vel = jnp.concatenate([velocities[1:], ahead[2:3]], axis=0)
    old_pos = jnp.concatenate([positions[1:], ahead[3:4]], axis=0)
    new_vel = old_vel + KICK_FACTOR * force
    moved = old_pos + MOVE_FACTOR * new_vel
    at_front = shock_place == front
    last_pos = jnp.where(at_front, fresh_positions, moved[nrows - 1])
    last_vel = jnp.where(at_front, fresh_velocities, new_vel[nrows - 1])
    new_positions = jnp.concatenate([moved[: nrows - 1], last_pos[None]], axis=0)
    new_velocities = jnp.concatenate([new_vel[: nrows - 1], last_vel[None]], axis=0)
    return (energies, new_positions, new_velocities)


def solution(mesh):
    return jax.shard_map(
        local,
        mesh=mesh,
        in_specs=(
            P("shock", "trans", None, None),
            P("shock", "trans", None, None),
            P("shock", "trans", None, None),
            P("shock", "trans", None, None),
            P("shock", "trans", None),
            P(),
            P(),
            P(),
            P(),
            P("trans", None, None),
            P("trans", None, None),
        ),
        out_specs=(
            P("shock", "trans", None),
            P("shock", "trans", None, None),
            P("shock", "trans", None, None),
        ),
        check_vma=False,
    )
```

time: 341 us -> 85.5 us (0.25)
  local copies, waits for them, and re-layouts: 125 us -> 7.31 us
  other arithmetic: 117 us -> 10.6 us
  matrix products: 38.7 us -> 0 us
  Pallas kernels: 0 us -> 34.6 us
  waiting for transfers between devices: 25.9 us -> 5.66 us
  starting transfers between devices: 29.9 us -> 25.5 us
    gather x12 -> x0, local copies, waits for them, and re-layouts: 67.8 us -> none  [the longest x6 50.6 us: block_energy(): jnp.take(window_feat, window_slot, axis=1)]
    dot_general x20 -> x0, matrix products: 38.7 us -> none  [the longest x6 24.8 us: block_energy(): jnp.einsum('cna,mna->mca', radial[0] * gathered[0], harmonics, precision=...]
    reduce_sum x20 -> x0, other arithmetic: 37.7 us -> none  [the longest x4 18.3 us: block_energy(): direct = jnp.sum(radial[1][None] * gathered, axis=2)]
    pallas_call x0 -> x1, Pallas kernels: none -> 34.6 us  [sweep(): pl.pallas_call(functools.partial(kernel, rows, cols, channels, slots), ou...]
    scatter-add x2 -> x1, other arithmetic: 34.3 us -> 0.01 us  [local(): force = force.at[nrows - 2].add(ahead[0])]
    mul x16 -> x0, other arithmetic: 18 us -> none  [the longest x4 13 us: block_energy(): radial = radial * (envelope * live)[None, None]]
    while x176 -> x0, local copies, waits for them, and re-layouts: 14.5 us -> none
    convert_element_type x6 -> x8, other arithmetic: 18.4 us -> 4.23 us  [the longest x3 2.44 us: halves(): hi = x.astype(BF16)]
  transfers between devices with their start and end apart: 14 -> 11, of which waited for: 8 -> 2; matrix products, arithmetic and copies ran while one was open for 1% -> 15% of each run, Pallas kernels for 0% -> 0%
where the time goes in v1:
time: 85.5 us; the launch traced here: 84.6 us
  Pallas kernels  34.6 us (40%)
  starting transfers between devices  25.5 us (30%)
  other arithmetic  10.6 us (12%)
  local copies, waits for them, and re-layouts  7.31 us (9%)
  waiting for transfers between devices  5.66 us (7%)
  between operations  0.92 us (1%)
    pallas_call x1, Pallas kernels, sweep(): pl.pallas_call(functools.partial(kernel, rows, cols, channels, slots), ou...  34.6 us
    ppermute x4, starting transfers between devices, extended_2(): after = lax.ppermute(first, axis, down)  10.9 us
    ppermute x4, starting transfers between devices, extended_2(): before = lax.ppermute(last, axis, up)  8.91 us
    unnamed x25, local copies, waits for them, and re-layouts  4.65 us
    ppermute x1, waiting for transfers between devices, passed_along(): return lax.ppermute(block, axis, route)  4.32 us
    ppermute x2, starting transfers between devices, shifted(): return lax.ppermute(x, axis, [(i, (i + by) % count) for i in range(count)])  3.26 us
    concatenate x4, other arithmetic, weight_rows(): return jnp.concatenate([hi, hi, lo], axis=1)  2.88 us
    ppermute x1, starting transfers between devices, passed_along(): return lax.ppermute(block, axis, route)  2.45 us
  transfers between devices with their start and end apart: 11, of which 2 were waited for; matrix products, arithmetic and copies ran while one was open for 15% of the time, Pallas kernels for 0%

profile of v1, /device:TPU:3, one launch (start us, length us, event | category | flops | bytes accessed | tf_op | source)
XLA Modules:
  0.0 84.6 jit_solution(2408964904942823771)
XLA Ops:
  0.7 1.3 %collective-permute-start = (bf16[2,1,576,128]{3,2,1,0:T(8,128)(2,1)}, bf16[2,1,576,128]{3,2,1,0:T(8,128)(2,1)S(1)}, u32[]{:S(2)}, u32[]{:S(2)}) collective-permute-start(bf16[2,1,576,128]{3,2,1,0:T(8,128)(2,1)} %param.21), channel_id=1, source_target_pairs={{0,1},{1,2},{2,3},{3,0},{4,5},{5,6},{6,7},{7,4},{8,9},{9,10},{10,1... | collective-permute-start | bytes 884744 | tf_op jit(solution)/shard_map/ppermute | solution.py:27
  2.0 2.1 %collective-permute-start.1 = (bf16[2,1,576,128]{3,2,1,0:T(8,128)(2,1)}, bf16[2,1,576,128]{3,2,1,0:T(8,128)(2,1)S(1)}, u32[]{:S(2)}, u32[]{:S(2)}) collective-permute-start(bf16[2,1,576,128]{3,2,1,0:T(8,128)(2,1)} %param.21), channel_id=1, source_target_pairs={{1,0},{2,1},{3,2},{0,3},{5,4},{6,5},{7,6},{4,7},{9,8},{10,9},{11,1... | collective-permute-start | bytes 884744 | tf_op jit(solution)/shard_map/ppermute | solution.py:28
  4.1 0.7 copy.38
  4.8 3.3 %collective-permute-start.5 = (f32[2,1,3,128]{3,2,1,0:T(4,128)S(1)}, f32[2,1,3,128]{3,2,1,0:T(4,128)S(1)}, u32[]{:S(2)}, u32[]{:S(2)}) collective-permute-start(f32[2,1,3,128]{3,2,1,0:T(4,128)S(1)} %copy.38), channel_id=1, source_target_pairs={{1,0},{2,1},{3,2},{0,3},{5,4},{6,5},{7,6},{4,7},{9,8},{10,9},{11,1... | collective-permute-start | bytes 9224 | tf_op jit(solution)/shard_map/ppermute | solution.py:28
  8.0 0.8 copy.41
  8.8 0.7 convert_element_type.45
  9.5 0.9 %copy.46 = f32[192,64]{1,0:T(8,128)S(1)} copy(f32[192,64]{0,1:T(8,128)} %param.25) | data formatting | bytes 98304 | tf_op args[6]
  10.4 0.8 %convert_element_type.48 = bf16[192,64]{0,1:T(8,128)(2,1)S(1)} convert(f32[192,64]{0,1:T(8,128)} %param.25) | non-fusion elementwise | flops 12288 | bytes 73728 | tf_op jit(solution)/shard_map/convert_element_type | solution.py:45
  11.3 0.8 %fusion.1 = (bf16[64,192]{1,0:T(8,128)(2,1)S(1)}, bf16[64,192]{1,0:T(8,128)(2,1)S(1)}) fusion(f32[192,64]{0,1:T(8,128)} %param.25), kind=kLoop, calls=%fused_computation.12 | loop fusion | flops 49152 | bytes 98304 | tf_op jit(solution)/shard_map/convert_element_type | solution.py:46
  12.1 1.0 %copy.50 = f32[128,192]{1,0:T(8,128)S(1)} copy(f32[128,192]{0,1:T(8,128)} %param.26) | data formatting | bytes 196608 | tf_op args[7]
  13.1 0.9 %convert_element_type.54 = bf16[128,192]{0,1:T(8,128)(2,1)S(1)} convert(f32[128,192]{0,1:T(8,128)} %param.26) | non-fusion elementwise | flops 24576 | bytes 147456 | tf_op jit(solution)/shard_map/convert_element_type | solution.py:45
  14.0 0.9 %fusion = (bf16[192,128]{1,0:T(8,128)(2,1)S(1)}, bf16[192,128]{1,0:T(8,128)(2,1)S(1)}) fusion(f32[128,192]{0,1:T(8,128)} %param.26), kind=kLoop, calls=%fused_computation.7 | loop fusion | flops 98304 | bytes 196608 | tf_op jit(solution)/shard_map/convert_element_type | solution.py:46
  15.2 0.7 pad_maximum_fusion.3.w2_ref
  16.0 0.8 pad_maximum_fusion.1.wr_ref
  16.8 0.7 pad_maximum_fusion.2.wrt_ref
  17.5 0.7 pad_maximum_fusion.4.w2t_ref
  18.6 3.6 %collective-permute-start.3 = (bf16[1,3,576,128]{3,2,1,0:T(8,128)(2,1)S(1)}, bf16[1,3,576,128]{3,2,1,0:T(8,128)(2,1)S(1)}, u32[]{:S(2)}, u32[]{:S(2)}) collective-permute-start(bf16[1,3,576,128]{3,2,1,0:T(8,128)(2,1)S(1)} %get-tuple-element.68), channel_id=1, source_target_pairs={{4,0},{8,4},{12,8},{16,12},{20,16},{24,20},{28,24},{5,1},{9,5},{13... | collective-permute-start | bytes 1327112 | tf_op jit(solution)/shard_map/ppermute | solution.py:28
  22.2 3.0 %collective-permute-start.2 = (bf16[1,3,576,128]{3,2,1,0:T(8,128)(2,1)S(1)}, bf16[1,3,576,128]{3,2,1,0:T(8,128)(2,1)S(1)}, u32[]{:S(2)}, u32[]{:S(2)}) collective-permute-start(bf16[1,3,576,128]{3,2,1,0:T(8,128)(2,1)S(1)} %get-tuple-element.67), channel_id=1, source_target_pairs={{0,4},{4,8},{8,12},{12,16},{16,20},{20,24},{24,28},{1,5},{5,9},{9,... | collective-permute-start | bytes 1327112 | tf_op jit(solution)/shard_map/ppermute | solution.py:27
  25.2 1.9 %collective-permute-start.7 = (f32[1,3,3,128]{3,2,1,0:T(4,128)S(1)}, f32[1,3,3,128]{3,2,1,0:T(4,128)S(1)}, u32[]{:S(2)}, u32[]{:S(2)}) collective-permute-start(f32[1,3,3,128]{3,2,1,0:T(4,128)S(1)} %get-tuple-element.70), channel_id=1, source_target_pairs={{4,0},{8,4},{12,8},{16,12},{20,16},{24,20},{28,24},{5,1},{9,5},{13... | collective-permute-start | bytes 13832 | tf_op jit(solution)/shard_map/ppermute | solution.py:28
  27.1 4.5 %collective-permute-start.6 = (f32[1,3,3,128]{3,2,1,0:T(4,128)S(1)}, f32[1,3,3,128]{3,2,1,0:T(4,128)S(1)}, u32[]{:S(2)}, u32[]{:S(2)}) collective-permute-start(f32[1,3,3,128]{3,2,1,0:T(4,128)S(1)} %get-tuple-element.69), channel_id=1, source_target_pairs={{0,4},{4,8},{8,12},{12,16},{16,20},{20,24},{24,28},{1,5},{5,9},{9,... | collective-permute-start | bytes 13832 | tf_op jit(solution)/shard_map/ppermute | solution.py:27
  31.7 0.7 pad_maximum_fusion.6.w1_ref
  32.4 0.7 copy.53.wo_ref
  33.1 0.6 pad_maximum_fusion.5.pos_ref
  33.7 1.5 %pad_maximum_fusion.feat_ref = bf16[4,3,576,128]{3,2,1,0:T(8,128)(2,1)} fusion(bf16[1,3,576,128]{3,2,1,0:T(8,128)(2,1)S(1)} %collective-permute-done.3, bf16[2,3,576,128]{3,2,1,0:T(8,128)(2,1)S(1)} %constant_dynamic-update-slice_fusion, bf16[1,3,576,128]{3,2,1,0:T(8,128)(2,1)S(1)} %collective-permute-done.2), kind=kLoop, calls=%fused_computation | loop fusion | flops 1769472 | bytes 3538944 | tf_op jit(solution)/shard_map/concatenate | solution.py:29
  35.2 34.6 %shard_map.130 = (f32[2,1,1,128]{3,2,1,0:T(1,128)}, f32[4,3,3,128]{3,2,1,0:T(4,128)}) custom-call(bf16[4,3,576,128]{3,2,1,0:T(8,128)(2,1)} %pad_maximum_fusion.feat_ref, f32[4,3,3,128]{3,2,1,0:T(4,128)} %pad_maximum_fusion.5.pos_ref, s32[2,1,24,128]{3,2,1,0:T(8,128)} %codes_ref.1, s32[2,1,1,128]{3,2,1,0:T(1,128)} %bitcast.47, ...), custom_call_target="tpu_custom_call" | custom-call | flops 8153726976 | bytes 4194304 | tf_op jit(solution)/shard_map/pallas_call | solution.py:361
  69.8 0.7 slice_bitcast_fusion.1
  70.5 0.7 slice_bitcast_fusion
  71.2 3.3 %collective-permute-start.8 = (f32[4,3,128]{2,1,0:T(4,128)S(1)}, f32[4,3,128]{2,1,0:T(4,128)S(1)}, u32[]{:S(2)}, u32[]{:S(2)}) collective-permute-start(f32[4,3,128]{2,1,0:T(4,128)S(1)} %slice_bitcast_fusion), channel_id=1, source_target_pairs={{0,3},{1,0},{2,1},{3,2},{4,7},{5,4},{6,5},{7,6},{8,11},{9,8},{10,9... | collective-permute-start | bytes 18440 | tf_op jit(solution)/shard_map/ppermute | solution.py:35
  74.4 1.3 %collective-permute-done.9 = f32[4,3,128]{2,1,0:T(4,128)S(1)} collective-permute-done((f32[4,3,128]{2,1,0:T(4,128)S(1)}, f32[4,3,128]{2,1,0:T(4,128)S(1)}, u32[]{:S(2)}, u32[]{:S(2)}) %collective-permute-start.9) | collective-permute-done | bytes 6176 | tf_op jit(solution)/shard_map/ppermute | solution.py:35
  75.8 0.7 fusion.2
  76.5 2.4 %collective-permute-start.10 = (f32[4,1,3,128]{3,2,0,1:T(4,128)S(1)}, f32[4,1,3,128]{3,2,0,1:T(4,128)S(1)}, u32[]{:S(2)}, u32[]{:S(2)}) collective-permute-start(f32[4,1,3,128]{3,2,0,1:T(4,128)S(1)} %pad_maximum_fusion.7), channel_id=1, source_target_pairs={{4,0},{8,4},{12,8},{16,12},{20,16},{24,20},{28,24},{5,1},{9,5},{13... | collective-permute-start | bytes 18440 | tf_op jit(solution)/shard_map/ppermute | solution.py:41
  79.0 4.3 %collective-permute-done.10 = f32[4,1,3,128]{3,2,0,1:T(4,128)S(1)} collective-permute-done((f32[4,1,3,128]{3,2,0,1:T(4,128)S(1)}, f32[4,1,3,128]{3,2,0,1:T(4,128)S(1)}, u32[]{:S(2)}, u32[]{:S(2)}) %collective-permute-start.10) | collective-permute-done | bytes 6176 | tf_op jit(solution)/shard_map/ppermute | solution.py:41
  (58 shorter events, 1.9 us)
Async XLA Ops:
  0.6 17.8 %copy-start = (bf16[2,1,576,128]{3,2,1,0:T(8,128)(2,1)S(1)}, bf16[2,1,576,128]{3,2,1,0:T(8,128)(2,1)}, u32[]{:S(2)}) copy-start(bf16[2,1,576,128]{3,2,1,0:T(8,128)(2,1)} %param.21) | copy-start | bytes 884740
  0.6 17.7 %copy-start.1 = (f32[2,1,3,128]{3,1,2,0:T(1,128)S(1)}, f32[2,1,3,128]{3,1,2,0:T(1,128)}, u32[]{:S(2)}) copy-start(f32[2,1,3,128]{3,1,2,0:T(1,128)} %param.19) | copy-start | bytes 9220
  0.7 17.7 %collective-permute-start = (bf16[2,1,576,128]{3,2,1,0:T(8,128)(2,1)}, bf16[2,1,576,128]{3,2,1,0:T(8,128)(2,1)S(1)}, u32[]{:S(2)}, u32[]{:S(2)}) collective-permute-start(bf16[2,1,576,128]{3,2,1,0:T(8,128)(2,1)} %param.21), channel_id=1, source_target_pairs={{0,1},{1,2},{2,3},{3,0},{4,5},{5,6},{6,7},{7,4},{8,9},{9,10},{10,1... | collective-permute-start | bytes 884744 | tf_op jit(solution)/shard_map/ppermute | solution.py:27
  2.0 16.5 %collective-permute-start.1 = (bf16[2,1,576,128]{3,2,1,0:T(8,128)(2,1)}, bf16[2,1,576,128]{3,2,1,0:T(8,128)(2,1)S(1)}, u32[]{:S(2)}, u32[]{:S(2)}) collective-permute-start(bf16[2,1,576,128]{3,2,1,0:T(8,128)(2,1)} %param.21), channel_id=1, source_target_pairs={{1,0},{2,1},{3,2},{0,3},{5,4},{6,5},{7,6},{4,7},{9,8},{10,9},{11,1... | collective-permute-start | bytes 884744 | tf_op jit(solution)/shard_map/ppermute | solution.py:28
  4.8 13.5 %collective-permute-start.4 = (f32[2,1,3,128]{3,2,1,0:T(4,128)S(1)}, f32[2,1,3,128]{3,2,1,0:T(4,128)S(1)}, u32[]{:S(2)}, u32[]{:S(2)}) collective-permute-start(f32[2,1,3,128]{3,2,1,0:T(4,128)S(1)} %copy.38), channel_id=1, source_target_pairs={{0,1},{1,2},{2,3},{3,0},{4,5},{5,6},{6,7},{7,4},{8,9},{9,10},{10,1... | collective-permute-start | bytes 9224 | tf_op jit(solution)/shard_map/ppermute | solution.py:27
  4.8 13.5 %collective-permute-start.5 = (f32[2,1,3,128]{3,2,1,0:T(4,128)S(1)}, f32[2,1,3,128]{3,2,1,0:T(4,128)S(1)}, u32[]{:S(2)}, u32[]{:S(2)}) collective-permute-start(f32[2,1,3,128]{3,2,1,0:T(4,128)S(1)} %copy.38), channel_id=1, source_target_pairs={{1,0},{2,1},{3,2},{0,3},{5,4},{6,5},{7,6},{4,7},{9,8},{10,9},{11,1... | collective-permute-start | bytes 9224 | tf_op jit(solution)/shard_map/ppermute | solution.py:28
  18.3 14.0 %copy-start.5 = (f32[128]{0:T(128)S(1)}, f32[128]{0:T(128)}, u32[]{:S(2)}) copy-start(f32[128]{0:T(128)} %param.27) | copy-start | bytes 1540
  18.6 15.2 %collective-permute-start.3 = (bf16[1,3,576,128]{3,2,1,0:T(8,128)(2,1)S(1)}, bf16[1,3,576,128]{3,2,1,0:T(8,128)(2,1)S(1)}, u32[]{:S(2)}, u32[]{:S(2)}) collective-permute-start(bf16[1,3,576,128]{3,2,1,0:T(8,128)(2,1)S(1)} %get-tuple-element.68), channel_id=1, source_target_pairs={{4,0},{8,4},{12,8},{16,12},{20,16},{24,20},{28,24},{5,1},{9,5},{13... | collective-permute-start | bytes 1327112 | tf_op jit(solution)/shard_map/ppermute | solution.py:28
  22.2 11.6 %collective-permute-start.2 = (bf16[1,3,576,128]{3,2,1,0:T(8,128)(2,1)S(1)}, bf16[1,3,576,128]{3,2,1,0:T(8,128)(2,1)S(1)}, u32[]{:S(2)}, u32[]{:S(2)}) collective-permute-start(bf16[1,3,576,128]{3,2,1,0:T(8,128)(2,1)S(1)} %get-tuple-element.67), channel_id=1, source_target_pairs={{0,4},{4,8},{8,12},{12,16},{16,20},{20,24},{24,28},{1,5},{5,9},{9,... | collective-permute-start | bytes 1327112 | tf_op jit(solution)/shard_map/ppermute | solution.py:27
  25.2 7.9 %collective-permute-start.7 = (f32[1,3,3,128]{3,2,1,0:T(4,128)S(1)}, f32[1,3,3,128]{3,2,1,0:T(4,128)S(1)}, u32[]{:S(2)}, u32[]{:S(2)}) collective-permute-start(f32[1,3,3,128]{3,2,1,0:T(4,128)S(1)} %get-tuple-element.70), channel_id=1, source_target_pairs={{4,0},{8,4},{12,8},{16,12},{20,16},{24,20},{28,24},{5,1},{9,5},{13... | collective-permute-start | bytes 13832 | tf_op jit(solution)/shard_map/ppermute | solution.py:28
  27.1 6.0 %collective-permute-start.6 = (f32[1,3,3,128]{3,2,1,0:T(4,128)S(1)}, f32[1,3,3,128]{3,2,1,0:T(4,128)S(1)}, u32[]{:S(2)}, u32[]{:S(2)}) collective-permute-start(f32[1,3,3,128]{3,2,1,0:T(4,128)S(1)} %get-tuple-element.69), channel_id=1, source_target_pairs={{0,4},{4,8},{8,12},{12,16},{16,20},{20,24},{24,28},{1,5},{5,9},{9,... | collective-permute-start | bytes 13832 | tf_op jit(solution)/shard_map/ppermute | solution.py:27
  35.2 39.2 %copy-start.2 = (f32[2,1,3,128]{3,1,2,0:T(1,128)S(1)}, f32[2,1,3,128]{3,1,2,0:T(1,128)}, u32[]{:S(2)}) copy-start(f32[2,1,3,128]{3,1,2,0:T(1,128)} %param.20) | copy-start | bytes 9220
  35.2 39.2 %slice-start = ((f32[2,1,3,128]{3,1,2,0:T(1,128)}), f32[1,1,3,128]{3,1,2,0:T(1,128)S(1)}, s32[]{:S(2)}) async-start(f32[2,1,3,128]{3,1,2,0:T(1,128)} %param.19), calls=%async_computation | async-start | bytes 3072 | tf_op jit(solution)/shard_map/slice | solution.py:433
  35.2 48.1 %copy-start.3 = (f32[1,3,128]{2,0,1:T(1,128)S(1)}, f32[1,3,128]{2,0,1:T(1,128)}, u32[]{:S(2)}) copy-start(f32[1,3,128]{2,0,1:T(1,128)} %param.29) | copy-start | bytes 4612
  35.2 48.1 %copy-start.4 = (f32[1,3,128]{2,0,1:T(1,128)S(1)}, f32[1,3,128]{2,0,1:T(1,128)}, u32[]{:S(2)}) copy-start(f32[1,3,128]{2,0,1:T(1,128)} %param.28) | copy-start | bytes 4612
  71.2 4.6 %collective-permute-start.9 = (f32[4,3,128]{2,1,0:T(4,128)S(1)}, f32[4,3,128]{2,1,0:T(4,128)S(1)}, u32[]{:S(2)}, u32[]{:S(2)}) collective-permute-start(f32[4,3,128]{2,1,0:T(4,128)S(1)} %slice_bitcast_fusion.1), channel_id=1, source_target_pairs={{0,1},{1,2},{2,3},{3,0},{4,5},{5,6},{6,7},{7,4},{8,9},{9,10},{10,1... | collective-permute-start | bytes 18440 | tf_op jit(solution)/shard_map/ppermute | solution.py:35
  71.2 4.6 %collective-permute-start.8 = (f32[4,3,128]{2,1,0:T(4,128)S(1)}, f32[4,3,128]{2,1,0:T(4,128)S(1)}, u32[]{:S(2)}, u32[]{:S(2)}) collective-permute-start(f32[4,3,128]{2,1,0:T(4,128)S(1)} %slice_bitcast_fusion), channel_id=1, source_target_pairs={{0,3},{1,0},{2,1},{3,2},{4,7},{5,4},{6,5},{7,6},{8,11},{9,8},{10,9... | collective-permute-start | bytes 18440 | tf_op jit(solution)/shard_map/ppermute | solution.py:35
  76.5 6.8 %collective-permute-start.10 = (f32[4,1,3,128]{3,2,0,1:T(4,128)S(1)}, f32[4,1,3,128]{3,2,0,1:T(4,128)S(1)}, u32[]{:S(2)}, u32[]{:S(2)}) collective-permute-start(f32[4,1,3,128]{3,2,0,1:T(4,128)S(1)} %pad_maximum_fusion.7), channel_id=1, source_target_pairs={{4,0},{8,4},{12,8},{16,12},{20,16},{24,20},{28,24},{5,1},{9,5},{13... | collective-permute-start | bytes 18440 | tf_op jit(solution)/shard_map/ppermute | solution.py:41

commit v2 on v1

v2 whole, which is shorter than its diff:
```python
import functools
import math

import jax
import jax.numpy as jnp
from jax import lax
from jax.experimental import pallas as pl
from jax.experimental.pallas import tpu as pltpu
from jax.sharding import PartitionSpec as P

CUTOFF_RADIUS = 9.5
BLOCK_LENGTH = 13.2
KICK_FACTOR = 4.0
MOVE_FACTOR = 0.5
F32 = jnp.float32
BF16 = jnp.bfloat16
LANES = 128
QUAD = 4
EDGE_LIMIT = 16
LOCAL_LIMIT = 16


def shifted(x, axis, by):
    count = lax.axis_size(axis)
    return lax.ppermute(x, axis, [(i, (i + by) % count) for i in range(count)])


def passed_along(block, axis, distance):
    devices = range(lax.axis_size(axis))
    route = [(i - distance, i) for i in devices if i - distance in devices]
    return lax.ppermute(block, axis, route)


def halves(x):
    hi = x.astype(BF16)
    lo = (x - hi.astype(F32)).astype(BF16)
    return hi, lo


def value_rows(x):
    hi, lo = halves(x)
    return jnp.concatenate([hi, lo, hi], axis=0)


def dot(a, b):
    return jnp.dot(a, b, preferred_element_type=F32)


def sin_cos_half_turns(t):
    n = jnp.floor(t + 0.5)
    r = t - n
    odd = n - 2.0 * jnp.floor(0.5 * n)
    sign = 1.0 - 2.0 * odd
    x = math.pi * r
    y = x * x
    s = 1.0 + y * (
        -1.0 / 6
        + y
        * (
            1.0 / 120
            + y * (-1.0 / 5040 + y * (1.0 / 362880 + y * (-1.0 / 39916800 + y * (1.0 / 6227020800.0))))
        )
    )
    c = 1.0 + y * (
        -0.5
        + y
        * (
            1.0 / 24
            + y
            * (-1.0 / 720 + y * (1.0 / 40320 + y * (-1.0 / 3628800 + y * (1.0 / 479001600.0))))
        )
    )
    return sign * x * s, sign * c


def weight_halves(w):
    hi = w.astype(BF16).astype(F32)
    return hi, w - hi


def weight_rows(w):
    hi, lo = weight_halves(w)
    return jnp.concatenate([hi, hi, lo], axis=1).astype(BF16)


def joined(ref, b, k, first, count):
    lines = [ref[b, k, pl.ds(first + s, 1), :] for s in range(count)]
    return jnp.concatenate(lines, axis=1)


def window_hot(near, place, first, count):
    lanes = near.shape[1]
    near3 = near.reshape(LANES // 16, 16, lanes)
    parts = []
    for k in range(count):
        mask = jnp.where(place == (first + k).astype(F32), 1.0, 0.0)
        mask = jnp.broadcast_to(mask, (16, lanes)).astype(BF16)
        parts.append((near3 * mask[None]).reshape(LANES, lanes))
    return parts


def edge_kernel(
    rows,
    cols,
    slots,
    own_ref,
    left_ref,
    right_ref,
    prev_ref,
    next_ref,
    codes_ref,
    counts_ref,
    w1_ref,
    w2_ref,
    wr_ref,
    wo_ref,
    geo,
    har,
    near,
    wsc,
    dsc,
    wrs,
    wrt,
    woc,
    pos_ref,
    w1s,
    w2s,
):
    blocks = rows * cols
    quads = slots // QUAD
    wide = QUAD * LANES
    root3, root5, root15 = math.sqrt(3.0), math.sqrt(5.0), math.sqrt(15.0)

    hi, lo = weight_halves(w1_ref[...].T)
    w1s[...] = jnp.concatenate([hi, hi, lo, lo], axis=1).astype(BF16)
    w2s[...] = weight_rows(w2_ref[...].T)
    wrs[...] = weight_rows(wr_ref[...].T)
    wrt[...] = weight_rows(wr_ref[...])
    units = wo_ref.shape[1]
    one = lax.broadcasted_iota(jnp.int32, (units, units), 0)
    two = lax.broadcasted_iota(jnp.int32, (units, units), 1)
    woc[...] = jnp.sum(jnp.where(one == two, wo_ref[...], 0.0), axis=1, keepdims=True)

    for i in range(3):
        pos_ref[0, :, i, :] = prev_ref[0, i]
        pos_ref[rows + 1, :, i, :] = next_ref[0, i]
        for r in range(rows):
            pos_ref[r + 1, 0:1, i, :] = left_ref[r, i]
            pos_ref[r + 1, cols + 1 :, i, :] = right_ref[r, i]
            pos_ref[r + 1, 1 : cols + 1, i, :] = own_ref[r, i]

    def geometry(b, _):
        r, c = b // cols, b % cols
        codes = codes_ref[r, c]
        zq = (codes >= 1152).astype(jnp.int32) + (codes >= 2304).astype(jnp.int32)
        slot = codes - 1152 * zq
        near_block = lax.shift_right_logical(slot, 7)
        atom = slot & 127
        row3 = (near_block >= 3).astype(jnp.int32) + (near_block >= 6).astype(jnp.int32)
        shift_x = (row3 - 1).astype(F32) * BLOCK_LENGTH
        shift_y = (near_block - 3 * row3 - 1).astype(F32) * BLOCK_LENGTH
        shift_z = (zq - 1).astype(F32) * BLOCK_LENGTH
        centre = pos_ref[r + 1, c + 1]
        found = [jnp.zeros((slots, LANES), F32) for _ in range(3)]
        for k in range(9):
            place = pos_ref[r + k // 3, c + k % 3]
            here = near_block == k
            for i in range(3):
                line = jnp.broadcast_to(place[i : i + 1], (slots, LANES))
                value = jnp.take_along_axis(line, atom, axis=1, mode="promise_in_bounds")
                found[i] = jnp.where(here, value, found[i])
        rx = found[0] + shift_x - centre[0:1]
        ry = found[1] + shift_y - centre[1:2]
        rz = found[2] + shift_z - centre[2:3]
        dist = jnp.sqrt(rx * rx + ry * ry + rz * rz)
        recip = 1.0 / dist
        ux, uy, uz = rx * recip, ry * recip, rz * recip
        x = dist * (1.0 / CUTOFF_RADIUS)
        x2 = x * x
        x5 = x2 * x2 * x
        live = lax.broadcasted_iota(jnp.int32, (slots, LANES), 0) < counts_ref[r, c]
        scale = jnp.where(live, 1.0 / slots, 0.0)
        env = (1.0 - x5 * x * (28.0 - x * (48.0 - 21.0 * x))) * scale
        denv = (-168.0 / CUTOFF_RADIUS) * x5 * (1.0 - x * (2.0 - x)) * scale
        geo[b, 0] = dist
        geo[b, 1] = recip
        geo[b, 2] = env
        geo[b, 3] = denv
        geo[b, 4] = ux
        geo[b, 5] = uy
        geo[b, 6] = uz
        geo[b, 7] = atom.astype(F32)
        geo[b, 8] = near_block.astype(F32)
        har[b, 0] = root3 * ux
        har[b, 1] = root3 * uy
        har[b, 2] = root3 * uz
        har[b, 3] = root15 * ux * uy
        har[b, 4] = root15 * uy * uz
        har[b, 5] = 0.5 * root5 * (3.0 * uz * uz - 1.0)
        har[b, 6] = root15 * ux * uz
        har[b, 7] = 0.5 * root15 * (ux * ux - uy * uy)
        return 0

    lax.fori_loop(0, blocks, geometry, 0)

    def network(step, _):
        b, first = step // quads, (step % quads) * QUAD
        atom = joined(geo, b, 7, first, QUAD)
        sub = lax.broadcasted_iota(jnp.int32, (LANES, wide), 0).astype(F32)
        near[step] = jnp.where(sub == atom, 1.0, 0.0).astype(BF16)
        dist, recip, env, denv = [joined(geo, b, k, first, QUAD) for k in range(4)]
        order = (lax.broadcasted_iota(jnp.int32, (8, wide), 0) + 1).astype(F32)
        sin, cos = sin_cos_half_turns(order * (dist * (1.0 / CUTOFF_RADIUS)))
        norm = math.sqrt(2.0 / CUTOFF_RADIUS)
        basis = norm * sin * recip
        slope = ((norm * math.pi / CUTOFF_RADIUS) * order * cos - basis) * recip
        both = jnp.concatenate([basis, slope], axis=1)
        hi = both.astype(BF16).astype(F32)
        lo = both - hi
        pre2 = dot(w1s[...], jnp.concatenate([hi, lo, hi, lo], axis=0).astype(BF16))
        pre, dpre = pre2[:, :wide], pre2[:, wide:]
        gate = 1.0 / (1.0 + jnp.exp(-pre))
        h = pre * gate
        dh = gate + h * (1.0 - gate)
        wsc[step] = dot(w2s[...], value_rows(h * env))
        dsc[step] = dot(w2s[...], value_rows(dh * dpre * env + h * denv))
        return 0

    lax.fori_loop(0, blocks * quads, network, 0)


def local_kernel(rows, cols, own_ref, left_ref, right_ref, near, geo, out, win, onehot):
    blocks = rows * cols
    steps = near.shape[0]
    quads = steps // blocks
    feats = win.shape[1]
    spans = win.shape[2] // LANES

    def first_slot(r):
        return 3 if (spans == 6 and r == 0) else 0

    def place_block(part, r, c):
        for i in range(max(r - 2, 0), min(r + 1, rows)):
            for j in range(max(c - 2, 0), min(c + 1, cols)):
                k = 3 * (r - i) + (c - j) - first_slot(i)
                win[i * cols + j, :, k * LANES : (k + 1) * LANES] = part

    if spans == 9:
        for c in range(cols):
            win[c, :, : 3 * LANES] = jnp.zeros((feats, 3 * LANES), BF16)
            win[blocks - cols + c, :, 6 * LANES :] = jnp.zeros((feats, 3 * LANES), BF16)
    for r in range(rows):
        place_block(left_ref[r, 0], r + 1, 0)
        place_block(right_ref[r, 0], r + 1, cols + 1)
        for c in range(cols):
            place_block(own_ref[r, c], r + 1, c + 1)

    def body(step, _):
        b, first = step // quads, (step % quads) * QUAD
        k0 = jnp.where(b // cols == 0, 3, 0) if spans == 6 else jnp.int32(0)
        place = joined(geo, b, 8, first, QUAD)
        parts = window_hot(near[step], place, k0, spans)
        for k in range(spans):
            onehot[k * LANES : (k + 1) * LANES, :] = parts[k]
        out[step] = dot(win[b], onehot[...]).astype(BF16)
        return 0

    lax.fori_loop(0, steps, body, 0)


RING = 3


def energy_kernel(
    rows,
    cols,
    channels,
    slots,
    prev_ref,
    next_ref,
    geo,
    har,
    near,
    wrs,
    wrt,
    woc,
    wsc_hbm,
    dsc_hbm,
    xl_hbm,
    en_ref,
    fleft_ref,
    fown_ref,
    fright_ref,
    force_ref,
    win,
    xl,
    xg,
    wsc,
    dsc,
    acc,
    inv,
    dys,
    lhs,
    wsem,
    dsem,
    xsem,
    *,
    stream,
):
    blocks = rows * cols
    quads = slots // QUAD
    steps = blocks * quads
    wide = QUAD * LANES
    group = 8
    root3, root5, root15 = math.sqrt(3.0), math.sqrt(5.0), math.sqrt(15.0)

    def w_copy(step):
        return pltpu.make_async_copy(wsc_hbm.at[step], wsc.at[step], wsem.at[step])

    def d_copy(step):
        return pltpu.make_async_copy(dsc_hbm.at[step], dsc.at[step], dsem.at[step])

    def x_copy(step):
        at = step % RING
        return pltpu.make_async_copy(xl_hbm.at[step], xl.at[at], xsem.at[at])

    if stream:
        for i in range(RING):
            x_copy(i).start()
            w_copy(i).start()
        for i in range(RING, steps):
            w_copy(i).start()
        for i in range(steps):
            d_copy(i).start()
    else:
        wsc, dsc = wsc_hbm, dsc_hbm

    for r in range(rows):
        for c in range(cols):
            b = r * cols + c
            for k in range(3):
                if r == 0:
                    win[b, :, k * LANES : (k + 1) * LANES] = prev_ref[0, c + k]
                elif r == rows - 1:
                    win[b, :, k * LANES : (k + 1) * LANES] = next_ref[0, c + k]
                else:
                    win[b, :, k * LANES : (k + 1) * LANES] = jnp.zeros_like(prev_ref[0, 0])
    acc[...] = jnp.zeros(acc.shape, F32)

    def gather(step):
        b, first = step // quads, (step % quads) * QUAD
        r = b // cols
        k0 = jnp.where(r == 0, 0, jnp.where(r == rows - 1, 6, 9))
        place = joined(geo, b, 8, first, QUAD)
        onehot = jnp.concatenate(window_hot(near[step], place, k0, 3), axis=0)
        if stream:
            x_copy(step).wait()
            xg[step] = xl[step % RING].astype(F32) + dot(win[b], onehot)
        else:
            xg[step] = xl_hbm[step].astype(F32) + dot(win[b], onehot)

    def collect(step):
        b, first = step // quads, (step % quads) * QUAD
        for g in range(channels // group):
            at = g * group
            total = [acc[b, m, at : at + group, :] for m in range(9)]
            for s in range(QUAD):
                ln = slice(s * LANES, (s + 1) * LANES)
                xs = [
                    xg[step, m * channels + at : m * channels + at + group, ln]
                    for m in range(9)
                ]
                w0, w1, w2 = [
                    wsc[step, k * channels + at : k * channels + at + group, ln]
                    for k in range(3)
                ]
                ys = [har[b, m, pl.ds(first + s, 1), :] for m in range(8)]
                t0 = w0 * xs[0]
                vec = xs[1] * ys[0] + xs[2] * ys[1] + xs[3] * ys[2]
                total[0] = total[0] + (t0 + w1 * xs[0]) + w2 * vec
                for m in range(1, 9):
                    total[m] = total[m] + (t0 * ys[m - 1] + w1 * xs[m])
            for m in range(9):
                acc[b, m, at : at + group, :] = total[m]

    def forward(step, _):
        if stream:
            w_copy(step - 1).wait()
        collect(step - 1)
        gather(step)
        if stream:

            @pl.when(step + RING - 1 < steps)
            def _():
                x_copy(step + RING - 1).start()

        return 0

    gather(0)
    lax.fori_loop(1, steps, forward, 0)
    if stream:
        w_copy(steps - 1).wait()
    collect(steps - 1)

    for b in range(blocks):
        ln = slice(b * LANES, (b + 1) * LANES)
        a = [acc[b, m] for m in range(9)]
        inv[0:channels, ln] = a[0] * a[0]
        inv[channels : 2 * channels, ln] = a[1] * a[1] + a[2] * a[2] + a[3] * a[3]
        inv[2 * channels :, ln] = (
            a[4] * a[4] + a[5] * a[5] + a[6] * a[6] + a[7] * a[7] + a[8] * a[8]
        )
    z = dot(wrs[...], value_rows(inv[...]))
    gate = 1.0 / (1.0 + jnp.exp(-z))
    out = z * gate
    wo = woc[...]
    energy = jnp.sum(out * wo, axis=0, keepdims=True)
    dinv = dot(wrt[...], value_rows(wo * (gate + out * (1.0 - gate))))
    for b in range(blocks):
        ln = slice(b * LANES, (b + 1) * LANES)
        en_ref[b // cols, b % cols] = energy[:, ln]
        for m in range(9):
            part = 0 if m == 0 else (1 if m < 4 else 2)
            d = dinv[part * channels : (part + 1) * channels, ln]
            acc[b, m] = 2.0 * acc[b, m] * d

    def backward(step, _):
        b, first = step // quads, (step % quads) * QUAD
        if stream:
            d_copy(step).wait()
        for s in range(QUAD):
            ln = slice(s * LANES, (s + 1) * LANES)
            ys = [har[b, m, pl.ds(first + s, 1), :] for m in range(8)]
            dy = [jnp.zeros((group, LANES), F32) for _ in range(9)]
            for g in range(channels // group):
                at = g * group
                xs = [
                    xg[step, m * channels + at : m * channels + at + group, ln]
                    for m in range(9)
                ]
                gs = [acc[b, m, at : at + group, :] for m in range(9)]
                w0 = wsc[step, at : at + group, ln]
                w2 = wsc[step, 2 * channels + at : 2 * channels + at + group, ln]
                d0, d1, d2 = [
                    dsc[step, k * channels + at : k * channels + at + group, ln]
                    for k in range(3)
                ]
                t0 = w0 * xs[0]
                t2 = w2 * gs[0]
                vec = xs[1] * ys[0] + xs[2] * ys[1] + xs[3] * ys[2]
                along = gs[0]
                direct = gs[0] * xs[0]
                for m in range(1, 9):
                    along = along + gs[m] * ys[m - 1]
                    direct = direct + gs[m] * xs[m]
                    dy[m - 1] = dy[m - 1] + t0 * gs[m]
                    if m < 4:
                        dy[m - 1] = dy[m - 1] + t2 * xs[m]
                dy[8] = dy[8] + (d0 * xs[0] * along + d1 * direct + d2 * gs[0] * vec)
            for m in range(9):
                dys[b, m, pl.ds(first + s, 1), :] = jnp.sum(dy[m], axis=0, keepdims=True)
        return 0

    lax.fori_loop(0, steps, backward, 0)
    force_ref[...] = jnp.zeros(force_ref.shape, F32)

    def pull(b, _):
        r, c = b // cols, b % cols
        ux, uy, uz, recip = geo[b, 4], geo[b, 5], geo[b, 6], geo[b, 1]
        d1, d2, d3, d4, d5, d6, d7, d8 = [dys[b, m] for m in range(8)]
        gx = root3 * d1 + root15 * (uy * d4 + uz * d7 + ux * d8)
        gy = root3 * d2 + root15 * (ux * d4 + uz * d5 - uy * d8)
        gz = root3 * d3 + root15 * (uy * d5 + ux * d7) + (3.0 * root5) * uz * d6
        radial = dys[b, 8] - (ux * gx + uy * gy + uz * gz) * recip
        grads = [gx * recip + ux * radial, gy * recip + uy * radial, gz * recip + uz * radial]
        for i in range(3):
            here = jnp.sum(grads[i], axis=0, keepdims=True)
            force_ref[r + 1, c + 1, i : i + 1, :] += here
        split = [halves(g) for g in grads]
        which = lax.broadcasted_iota(jnp.int32, (16, LANES), 0).astype(F32)
        place = geo[b, 8]
        for n in range(slots):
            ln = slice(n * LANES, (n + 1) * LANES)
            hit = which == place[n : n + 1]
            for i in range(3):
                for v in range(2):
                    line = split[i][v][n : n + 1].astype(F32)
                    at = (3 * v + i) * 16
                    lhs[at : at + 16, ln] = jnp.where(hit, line, 0.0).astype(BF16)
        total = jnp.zeros((96, LANES), F32)
        for p in range(quads):
            total = total + lax.dot_general(
                lhs[:, p * wide : (p + 1) * wide],
                near[b * quads + p],
                (((1,), (1,)), ((), ())),
                preferred_element_type=F32,
            )
        for i in range(3):
            for k in range(9):
                at = i * 16 + k
                value = total[at : at + 1] + total[48 + at : 49 + at]
                force_ref[r + k // 3, c + k % 3, i : i + 1, :] -= value
        return 0

    lax.fori_loop(0, blocks, pull, 0)
    for r in range(rows + 2):
        for i in range(3):
            fleft_ref[r, i] = force_ref[r, 0:1, i, :]
            fright_ref[r, i] = force_ref[r, cols + 1 :, i, :]
            fown_ref[r, i] = force_ref[r, 1 : cols + 1, i, :]


def vmem_call(body, name, ins, out_shape, scratch, limit, flops):
    vmem = pl.BlockSpec(memory_space=pltpu.VMEM)
    return pl.pallas_call(
        body,
        out_shape=out_shape,
        in_specs=ins,
        out_specs=[vmem] * len(out_shape),
        scratch_shapes=scratch,
        compiler_params=pltpu.CompilerParams(vmem_limit_bytes=limit * 1024 * 1024),
        cost_estimate=pl.CostEstimate(flops=flops, bytes_accessed=1024 * 1024, transcendentals=0),
        name=name,
    )


def edge_part(pos, neighbours, counts, w_first, w_second, w_read, w_out):
    rows, cols, slots = neighbours.shape[0], neighbours.shape[1], neighbours.shape[2]
    hidden, basis = w_first.shape
    units, reads = w_read.shape
    weights = w_second.shape[0]
    blocks, steps, wide = rows * cols, rows * cols * slots // QUAD, QUAD * LANES
    vmem = pl.BlockSpec(memory_space=pltpu.VMEM)
    sds = jax.ShapeDtypeStruct
    call = vmem_call(
        functools.partial(edge_kernel, rows, cols, slots),
        "edges",
        [vmem] * 11,
        [
            sds((blocks, 9, slots, LANES), F32),
            sds((blocks, 8, slots, LANES), F32),
            sds((steps, LANES, wide), BF16),
            sds((steps, weights, wide), F32),
            sds((steps, weights, wide), F32),
            sds((units, 3 * reads), BF16),
            sds((reads, 3 * units), BF16),
            sds((units, 1), F32),
        ],
        [
            pltpu.VMEM((rows + 2, cols + 2, 3, LANES), F32),
            pltpu.VMEM((hidden, 4 * basis), BF16),
            pltpu.VMEM((weights, 3 * hidden), BF16),
        ],
        EDGE_LIMIT,
        2 * 6 * 2 * weights * hidden * steps * wide,
    )
    return call(
        *pos,
        neighbours,
        counts.reshape(rows, cols, 1, LANES),
        w_first.T,
        w_second.T,
        w_read.T,
        w_out.reshape(1, units),
    )


def local_part(own, left, right, near, geo):
    rows, cols, feats = own.shape[0], own.shape[1], own.shape[2]
    steps, _, wide = near.shape
    spans = 6 if rows == 2 else 9
    vmem = pl.BlockSpec(memory_space=pltpu.VMEM)
    call = vmem_call(
        functools.partial(local_kernel, rows, cols),
        "local",
        [vmem] * 5,
        [jax.ShapeDtypeStruct((steps, feats, wide), BF16)],
        [
            pltpu.VMEM((rows * cols, feats, spans * LANES), BF16),
            pltpu.VMEM((spans * LANES, wide), BF16),
        ],
        LOCAL_LIMIT,
        2 * feats * spans * LANES * steps * wide,
    )
    return call(own, left, right, near, geo)[0]


def energy_part(before, after, edges, gathered, rows, cols):
    geo, har, near, wsc, dsc, wrs, wrt, woc = edges
    slots = geo.shape[2]
    steps, weights, wide = wsc.shape
    channels, blocks, feats = weights // 3, rows * cols, gathered.shape[1]
    vmem = pl.BlockSpec(memory_space=pltpu.VMEM)
    hbm = pl.BlockSpec(memory_space=pl.ANY)
    sds = jax.ShapeDtypeStruct
    side = sds((rows + 2, 3, 1, LANES), F32)
    stream = blocks > 2
    kept = steps if stream else 1
    call = vmem_call(
        functools.partial(energy_kernel, rows, cols, channels, slots, stream=stream),
        "energy",
        [vmem] * 8 + [hbm if stream else vmem] * 3,
        [sds((rows, cols, 1, LANES), F32), side, sds((rows + 2, 3, cols, LANES), F32), side],
        [
            pltpu.VMEM((rows + 2, cols + 2, 3, LANES), F32),
            pltpu.VMEM((blocks, feats, 3 * LANES), BF16),
            pltpu.VMEM((RING, feats, wide) if stream else (1, 16, LANES), BF16),
            pltpu.VMEM((steps, feats, wide), F32),
            pltpu.VMEM((steps, weights, wide) if stream else (1, 8, LANES), F32),
            pltpu.VMEM((steps, weights, wide) if stream else (1, 8, LANES), F32),
            pltpu.VMEM((blocks, 9, channels, LANES), F32),
            pltpu.VMEM((weights, blocks * LANES), F32),
            pltpu.VMEM((blocks, 9, slots, LANES), F32),
            pltpu.VMEM((96, slots * LANES), BF16),
            pltpu.SemaphoreType.DMA((kept,)),
            pltpu.SemaphoreType.DMA((kept,)),
            pltpu.SemaphoreType.DMA((RING,)),
        ],
        56 if stream else 24,
        2 * feats * 9 * LANES * steps * wide,
    )
    energies, f_left, f_own, f_right = call(
        before, after, geo, har, near, wrs, wrt, woc, wsc, dsc, gathered
    )
    return f_left, f_own, f_right, energies.reshape(rows, cols, LANES)


def local(
    positions,
    velocities,
    features,
    neighbours,
    counts,
    w_first,
    w_second,
    w_read,
    w_out,
    fresh_positions,
    fresh_velocities,
):
    nrows, ncols = (positions.shape[0], positions.shape[1])
    shock_place = lax.axis_index("shock")
    front = lax.axis_size("shock") - 1
    assert nrows >= 2 and neighbours.shape[2] % QUAD == 0

    def sides(x, axis):
        last = lax.slice_in_dim(x, ncols - 1, ncols, axis=axis)
        first = lax.slice_in_dim(x, 0, 1, axis=axis)
        return shifted(last, "trans", 1), shifted(first, "trans", -1)

    def ends(x, left, right, axis):
        last = jnp.concatenate([left[nrows - 1 :], x[nrows - 1 :], right[nrows - 1 :]], axis=axis)
        first = jnp.concatenate([left[:1], x[:1], right[:1]], axis=axis)
        return passed_along(last, "shock", 1), passed_along(first, "shock", -1)

    pos = positions.transpose(0, 2, 1, 3)
    vel = velocities.transpose(0, 2, 1, 3)
    pos_left, pos_right = sides(pos, 2)
    left, right = sides(features, 1)
    pos_before, pos_after = ends(pos, pos_left, pos_right, 2)
    left, right, _, _ = lax.optimization_barrier((left, right, pos_before, pos_after))
    placed = (pos, pos_left, pos_right, pos_before, pos_after)
    edges = edge_part(placed, neighbours, counts, w_first, w_second, w_read, w_out)
    before, after = ends(features, left, right, 1)
    gathered = local_part(features, left, right, edges[2], edges[0])
    f_left, f_own, f_right, energies = energy_part(before, after, edges, gathered, nrows, ncols)
    from_right = shifted(f_left, "trans", -1)
    from_left = shifted(f_right, "trans", 1)
    folded = f_own.at[:, :, ncols - 1].add(from_right[:, :, 0])
    folded = folded.at[:, :, 0].add(from_left[:, :, 0])
    packed = jnp.concatenate([folded[:2], vel[:1], pos[:1]], axis=0)
    ahead = passed_along(packed, "shock", -1)
    force = folded[2 : nrows + 2]
    force = jnp.concatenate([force[: nrows - 2], force[nrows - 2 :] + ahead[:2]], axis=0)
    old_vel = jnp.concatenate([vel[1:], ahead[2:3]], axis=0)
    old_pos = jnp.concatenate([pos[1:], ahead[3:4]], axis=0)
    new_vel = old_vel + KICK_FACTOR * force
    moved = old_pos + MOVE_FACTOR * new_vel
    at_front = shock_place == front
    last_pos = jnp.where(at_front, fresh_positions.transpose(1, 0, 2), moved[nrows - 1])
    last_vel = jnp.where(at_front, fresh_velocities.transpose(1, 0, 2), new_vel[nrows - 1])
    new_positions = jnp.concatenate([moved[: nrows - 1], last_pos[None]], axis=0)
    new_velocities = jnp.concatenate([new_vel[: nrows - 1], last_vel[None]], axis=0)
    return (energies, new_positions.transpose(0, 2, 1, 3), new_velocities.transpose(0, 2, 1, 3))


def solution(mesh):
    return jax.shard_map(
        local,
        mesh=mesh,
        in_specs=(
            P("shock", "trans", None, None),
            P("shock", "trans", None, None),
            P("shock", "trans", None, None),
            P("shock", "trans", None, None),
            P("shock", "trans", None),
            P(),
            P(),
            P(),
            P(),
            P("trans", None, None),
            P("trans", None, None),
        ),
        out_specs=(
            P("shock", "trans", None),
            P("shock", "trans", None, None),
            P("shock", "trans", None, None),
        ),
        check_vma=False,
    )
```

time: 85.5 us -> 74.4 us (0.87)
  other arithmetic: 10.6 us -> 1.34 us
  waiting for transfers between devices: 5.66 us -> 10.8 us
  Pallas kernels: 34.6 us -> 30.4 us
  starting transfers between devices: 25.5 us -> 23.2 us
    ppermute x8 -> x0, starting transfers between devices: 19.8 us -> none  [the longest x4 10.9 us: extended_2(): after = lax.ppermute(first, axis, down)]
    ppermute x1 -> x5, starting transfers between devices: 2.45 us -> 15 us  [passed_along(): return lax.ppermute(block, axis, route)]
    concatenate x10 -> x5, other arithmetic: 5.65 us -> 0.14 us  [the longest x2 0.06 us: ends(): jnp.concatenate([left[nrows - 1:], x[nrows - 1:], right[nrows - 1:]], axi...]
    ppermute x2 -> x6, starting transfers between devices: 3.26 us -> 8.22 us  [shifted(): return lax.ppermute(x, axis, [(i, (i + by) % count) for i in range(count)])]
    convert_element_type x8 -> x0, other arithmetic: 4.23 us -> none  [the longest x3 2.44 us: halves(): hi = x.astype(BF16)]
    pallas_call x1 -> x3, Pallas kernels: 34.6 us -> 30.4 us  [the longest x1 15.4 us: energy_part(): call(before, after, geo, har, near, wrs, wrt, woc, wsc, dsc, gathered)]
    ppermute x2 -> x6, waiting for transfers between devices: 1.32 us -> 3.96 us  [shifted(): return lax.ppermute(x, axis, [(i, (i + by) % count) for i in range(count)])]
    ppermute x1 -> x5, waiting for transfers between devices: 4.32 us -> 6.82 us  [passed_along(): return lax.ppermute(block, axis, route)]
  transfers between devices with their start and end apart: 11 -> 11, of which waited for: 2 -> 4; matrix products, arithmetic and copies ran while one was open for 15% -> 2% of each run, Pallas kernels for 0% -> 20%
where the time goes in v2:
time: 74.4 us; the launch traced here: 73.5 us
  Pallas kernels  30.4 us (41%)
  starting transfers between devices  23.2 us (31%)
  waiting for transfers between devices  10.8 us (15%)
  local copies, waits for them, and re-layouts  6.95 us (9%)
  other arithmetic  1.34 us (2%)
  between operations  0.88 us (1%)
    pallas_call x1, Pallas kernels, energy_part(): call(before, after, geo, har, near, wrs, wrt, woc, wsc, dsc, gathered)  15.4 us
    ppermute x5, starting transfers between devices, passed_along(): return lax.ppermute(block, axis, route)  15 us
    ppermute x6, starting transfers between devices, shifted(): return lax.ppermute(x, axis, [(i, (i + by) % count) for i in range(count)])  8.22 us
    pallas_call x1, Pallas kernels, local_part(): return call(own, left, right, near, geo)[0]  7.92 us
    pallas_call x1, Pallas kernels, edge_part(): call(*pos, neighbours, counts.reshape(rows, cols, 1, LANES), w_first.T, w...  7.04 us
    ppermute x5, waiting for transfers between devices, passed_along(): return lax.ppermute(block, axis, route)  6.82 us
    unnamed x22, local copies, waits for them, and re-layouts  5.19 us
    ppermute x6, waiting for transfers between devices, shifted(): return lax.ppermute(x, axis, [(i, (i + by) % count) for i in range(count)])  3.96 us
  transfers between devices with their start and end apart: 11, of which 4 were waited for; matrix products, arithmetic and copies ran while one was open for 2% of the time, Pallas kernels for 20%

profile of v2, /device:TPU:3, one launch (start us, length us, event | category | flops | bytes accessed | tf_op | source)
XLA Modules:
  0.0 73.5 jit_solution(203670058031712961)
XLA Ops:
  0.6 1.3 %collective-permute-start.2 = (f32[2,3,1,128]{3,2,1,0:T(1,128)}, f32[2,3,1,128]{3,2,1,0:T(1,128)S(1)}, u32[]{:S(2)}, u32[]{:S(2)}) collective-permute-start(f32[2,3,1,128]{3,2,1,0:T(1,128)} %bitcast.33), channel_id=1, source_target_pairs={{0,1},{1,2},{2,3},{3,0},{4,5},{5,6},{6,7},{7,4},{8,9},{9,10},{10,1... | collective-permute-start | bytes 9224 | tf_op jit(solution)/shard_map/ppermute | solution.py:25
  2.0 2.1 %collective-permute-start.3 = (f32[2,3,1,128]{3,2,1,0:T(1,128)}, f32[2,3,1,128]{3,2,1,0:T(1,128)S(1)}, u32[]{:S(2)}, u32[]{:S(2)}) collective-permute-start(f32[2,3,1,128]{3,2,1,0:T(1,128)} %bitcast.34), channel_id=1, source_target_pairs={{0,3},{1,0},{2,1},{3,2},{4,7},{5,4},{6,5},{7,6},{8,11},{9,8},{10,9... | collective-permute-start | bytes 9224 | tf_op jit(solution)/shard_map/ppermute | solution.py:25
  4.1 3.3 %collective-permute-start.1 = (bf16[2,1,576,128]{3,2,1,0:T(8,128)(2,1)}, bf16[2,1,576,128]{3,2,1,0:T(8,128)(2,1)S(1)}, u32[]{:S(2)}, u32[]{:S(2)}) collective-permute-start(bf16[2,1,576,128]{3,2,1,0:T(8,128)(2,1)} %own_ref.1), channel_id=1, source_target_pairs={{0,3},{1,0},{2,1},{3,2},{4,7},{5,4},{6,5},{7,6},{8,11},{9,8},{10,9... | collective-permute-start | bytes 884744 | tf_op jit(solution)/shard_map/ppermute | solution.py:25
  7.3 0.7 slice_bitcast_fusion.2
  8.1 4.7 %collective-permute-start.4 = (f32[1,3,3,128]{3,2,1,0:T(4,128)S(1)}, f32[1,3,3,128]{3,2,1,0:T(4,128)S(1)}, u32[]{:S(2)}, u32[]{:S(2)}) collective-permute-start(f32[1,3,3,128]{3,2,1,0:T(4,128)S(1)} %pad_maximum_fusion.2), channel_id=1, source_target_pairs={{0,4},{4,8},{8,12},{12,16},{16,20},{20,24},{24,28},{1,5},{5,9},{9,... | collective-permute-start | bytes 13832 | tf_op jit(solution)/shard_map/ppermute | solution.py:31
  12.8 1.9 %collective-permute-start.5 = (f32[1,3,3,128]{3,2,1,0:T(4,128)S(1)}, f32[1,3,3,128]{3,2,1,0:T(4,128)S(1)}, u32[]{:S(2)}, u32[]{:S(2)}) collective-permute-start(f32[1,3,3,128]{3,2,1,0:T(4,128)S(1)} %pad_maximum_fusion.3), channel_id=1, source_target_pairs={{4,0},{8,4},{12,8},{16,12},{20,16},{24,20},{28,24},{5,1},{9,5},{13... | collective-permute-start | bytes 13832 | tf_op jit(solution)/shard_map/ppermute | solution.py:31
  14.7 1.0 %fusion.4 = (bf16[1,1,576,128]{3,2,1,0:T(8,128)(2,1)S(1)}, bf16[1,1,576,128]{3,2,1,0:T(8,128)(2,1)S(1)}) fusion(bf16[2,1,576,128]{3,2,1,0:T(8,128)(2,1)} %own_ref.1), kind=kLoop, calls=%fused_computation.19 | loop fusion | bytes 589824 | tf_op jit(solution)/shard_map/slice | solution.py:653
  15.7 2.9 %collective-permute-done.5.next_ref = f32[1,3,3,128]{3,2,1,0:T(4,128)S(1)} collective-permute-done((f32[1,3,3,128]{3,2,1,0:T(4,128)S(1)}, f32[1,3,3,128]{3,2,1,0:T(4,128)S(1)}, u32[]{:S(2)}, u32[]{:S(2)}) %collective-permute-start.5) | collective-permute-done | bytes 4640 | tf_op jit(solution)/shard_map/ppermute | solution.py:31
  18.6 0.7 copy-done.1
  19.3 0.9 %copy-done.2 = f32[128,192]{0,1:T(8,128)S(1)} copy-done((f32[128,192]{0,1:T(8,128)S(1)}, f32[128,192]{0,1:T(8,128)}, u32[]{:S(2)}) %copy-start.2) | copy-done | bytes 98328
  20.2 0.8 %copy-done.3 = f32[192,64]{0,1:T(8,128)S(1)} copy-done((f32[192,64]{0,1:T(8,128)S(1)}, f32[192,64]{0,1:T(8,128)}, u32[]{:S(2)}) %copy-start.3) | copy-done | bytes 49176
  21.0 0.7 copy-done.4
  21.8 0.7 copy-done.5
  22.5 0.7 copy-done.6
  23.2 0.7 copy-done.7
  23.8 7.0 %edges.1 = (f32[2,9,24,128]{3,2,1,0:T(8,128)S(1)}, f32[2,8,24,128]{3,2,1,0:T(8,128)S(1)}, bf16[12,128,512]{2,1,0:T(8,128)(2,1)S(1)}, f32[12,192,512]{2,1,0:T(8,1...) custom-call(f32[2,3,1,128]{3,2,1,0:T(1,128)S(1)} %bitcast.35, ...), custom_call_target="tpu_custom_call" | custom-call | flops 1811939328 | bytes 1048576 | tf_op jit(solution)/shard_map/edges/pallas_call | solution.py:557
  30.9 0.1 pad_maximum_fusion.1
  31.0 1.9 %collective-permute-start.7 = (bf16[1,3,576,128]{3,2,1,0:T(8,128)(2,1)S(1)}, bf16[1,3,576,128]{3,2,1,0:T(8,128)(2,1)S(1)}, u32[]{:S(2)}, u32[]{:S(2)}) collective-permute-start(bf16[1,3,576,128]{3,2,1,0:T(8,128)(2,1)S(1)} %pad_maximum_fusion.1), channel_id=1, source_target_pairs={{4,0},{8,4},{12,8},{16,12},{20,16},{24,20},{28,24},{5,1},{9,5},{13... | collective-permute-start | bytes 1327112 | tf_op jit(solution)/shard_map/ppermute | solution.py:31
  32.9 0.1 pad_maximum_fusion
  33.0 4.5 %collective-permute-start.6 = (bf16[1,3,576,128]{3,2,1,0:T(8,128)(2,1)S(1)}, bf16[1,3,576,128]{3,2,1,0:T(8,128)(2,1)S(1)}, u32[]{:S(2)}, u32[]{:S(2)}) collective-permute-start(bf16[1,3,576,128]{3,2,1,0:T(8,128)(2,1)S(1)} %pad_maximum_fusion), channel_id=1, source_target_pairs={{0,4},{4,8},{8,12},{12,16},{16,20},{20,24},{24,28},{1,5},{5,9},{9,... | collective-permute-start | bytes 1327112 | tf_op jit(solution)/shard_map/ppermute | solution.py:31
  37.5 7.9 %local.1.xl_hbm = bf16[12,576,512]{2,1,0:T(8,128)(2,1)S(1)} custom-call(bf16[2,1,576,128]{3,2,1,0:T(8,128)(2,1)S(1)} %copy-done, bf16[2,1,576,128]{3,2,1,0:T(8,128)(2,1)S(1)} %collective-permute-done.left_ref, bf16[2,1,576,128]{3,2,1,0:T(8,128)(2,1)S(1)} %collective-permute-done.1.right_ref, bf16[12,128,512]{2,1,0:T(8,128)(2,1)S(1)} %get-tuple-element.45.near, ...), custom_call_target="tpu_custom_call" | custom-call | flops 5435817984 | bytes 1048576 | tf_op jit(solution)/shard_map/local/pallas_call | solution.py:585
  45.5 0.0 copy-start.8
  45.5 0.0 copy-start.10
  45.5 15.4 %energy.1 = (f32[2,1,1,128]{3,2,1,0:T(1,128)}, f32[4,3,1,128]{3,2,1,0:T(1,128)S(1)}, f32[4,3,1,128]{3,2,1,0:T(1,128)S(1)}, f32[4,3,1,128]{3,2,1,0:T(1,128)S(1)}) custom-call(bf16[1,3,576,128]{3,2,1,0:T(8,128)(2,1)S(1)} %collective-permute-done.6.prev_ref, bf16[1,3,576,128]{3,2,1,0:T(8,128)(2,1)S(1)} %collective-permute-done.7.next_ref, ...), custom_call_target="tpu_custom_call" | custom-call | flops 8153726976 | bytes 1048576 | tf_op jit(solution)/shard_map/energy/pallas_call | solution.py:622
  61.0 1.2 %collective-permute-start.8 = (f32[4,3,1,128]{3,2,1,0:T(1,128)S(1)}, f32[4,3,1,128]{3,2,1,0:T(1,128)S(1)}, u32[]{:S(2)}, u32[]{:S(2)}) collective-permute-start(f32[4,3,1,128]{3,2,1,0:T(1,128)S(1)} %get-tuple-element.53), channel_id=1, source_target_pairs={{0,3},{1,0},{2,1},{3,2},{4,7},{5,4},{6,5},{7,6},{8,11},{9,8},{10,9... | collective-permute-start | bytes 18440 | tf_op jit(solution)/shard_map/ppermute | solution.py:25
  62.1 0.3 collective-permute-start.9
  62.5 1.0 %collective-permute-done.8 = f32[4,3,1,128]{3,2,1,0:T(1,128)S(1)} collective-permute-done((f32[4,3,1,128]{3,2,1,0:T(1,128)S(1)}, f32[4,3,1,128]{3,2,1,0:T(1,128)S(1)}, u32[]{:S(2)}, u32[]{:S(2)}) %collective-permute-start.8) | collective-permute-done | bytes 6176 | tf_op jit(solution)/shard_map/ppermute | solution.py:25
  63.5 2.9 %collective-permute-done.9 = f32[4,3,1,128]{3,2,1,0:T(1,128)S(1)} collective-permute-done((f32[4,3,1,128]{3,2,1,0:T(1,128)S(1)}, f32[4,3,1,128]{3,2,1,0:T(1,128)S(1)}, u32[]{:S(2)}, u32[]{:S(2)}) %collective-permute-start.9) | collective-permute-done | bytes 6176 | tf_op jit(solution)/shard_map/ppermute | solution.py:25
  66.5 1.9 %collective-permute-start.10 = (f32[4,3,1,128]{3,2,1,0:T(1,128)S(1)}, f32[4,3,1,128]{3,2,1,0:T(1,128)S(1)}, u32[]{:S(2)}, u32[]{:S(2)}) collective-permute-start(f32[4,3,1,128]{3,2,1,0:T(1,128)S(1)} %pad_maximum_fusion.4), channel_id=1, source_target_pairs={{4,0},{8,4},{12,8},{16,12},{20,16},{24,20},{28,24},{5,1},{9,5},{13... | collective-permute-start | bytes 18440 | tf_op jit(solution)/shard_map/ppermute | solution.py:31
  68.4 3.9 %collective-permute-done.10 = f32[4,3,1,128]{3,2,1,0:T(1,128)S(1)} collective-permute-done((f32[4,3,1,128]{3,2,1,0:T(1,128)S(1)}, f32[4,3,1,128]{3,2,1,0:T(1,128)S(1)}, u32[]{:S(2)}, u32[]{:S(2)}) %collective-permute-start.10) | collective-permute-done | bytes 6176 | tf_op jit(solution)/shard_map/ppermute | solution.py:31
  72.4 0.6 maximum_bitcast_fusion.1
  73.0 0.6 maximum_bitcast_fusion
  (34 shorter events, 0.2 us)
Async XLA Ops:
  0.6 7.4 %collective-permute-start.2 = (f32[2,3,1,128]{3,2,1,0:T(1,128)}, f32[2,3,1,128]{3,2,1,0:T(1,128)S(1)}, u32[]{:S(2)}, u32[]{:S(2)}) collective-permute-start(f32[2,3,1,128]{3,2,1,0:T(1,128)} %bitcast.33), channel_id=1, source_target_pairs={{0,1},{1,2},{2,3},{3,0},{4,5},{5,6},{6,7},{7,4},{8,9},{9,10},{10,1... | collective-permute-start | bytes 9224 | tf_op jit(solution)/shard_map/ppermute | solution.py:25
  2.0 6.1 %collective-permute-start.3 = (f32[2,3,1,128]{3,2,1,0:T(1,128)}, f32[2,3,1,128]{3,2,1,0:T(1,128)S(1)}, u32[]{:S(2)}, u32[]{:S(2)}) collective-permute-start(f32[2,3,1,128]{3,2,1,0:T(1,128)} %bitcast.34), channel_id=1, source_target_pairs={{0,3},{1,0},{2,1},{3,2},{4,7},{5,4},{6,5},{7,6},{8,11},{9,8},{10,9... | collective-permute-start | bytes 9224 | tf_op jit(solution)/shard_map/ppermute | solution.py:25
  4.1 26.8 %collective-permute-start = (bf16[2,1,576,128]{3,2,1,0:T(8,128)(2,1)}, bf16[2,1,576,128]{3,2,1,0:T(8,128)(2,1)S(1)}, u32[]{:S(2)}, u32[]{:S(2)}) collective-permute-start(bf16[2,1,576,128]{3,2,1,0:T(8,128)(2,1)} %own_ref.1), channel_id=1, source_target_pairs={{0,1},{1,2},{2,3},{3,0},{4,5},{5,6},{6,7},{7,4},{8,9},{9,10},{10,1... | collective-permute-start | bytes 884744 | tf_op jit(solution)/shard_map/ppermute | solution.py:25
  4.1 26.8 %collective-permute-start.1 = (bf16[2,1,576,128]{3,2,1,0:T(8,128)(2,1)}, bf16[2,1,576,128]{3,2,1,0:T(8,128)(2,1)S(1)}, u32[]{:S(2)}, u32[]{:S(2)}) collective-permute-start(bf16[2,1,576,128]{3,2,1,0:T(8,128)(2,1)} %own_ref.1), channel_id=1, source_target_pairs={{0,3},{1,0},{2,1},{3,2},{4,7},{5,4},{6,5},{7,6},{8,11},{9,8},{10,9... | collective-permute-start | bytes 884744 | tf_op jit(solution)/shard_map/ppermute | solution.py:25
  8.1 7.6 %collective-permute-start.4 = (f32[1,3,3,128]{3,2,1,0:T(4,128)S(1)}, f32[1,3,3,128]{3,2,1,0:T(4,128)S(1)}, u32[]{:S(2)}, u32[]{:S(2)}) collective-permute-start(f32[1,3,3,128]{3,2,1,0:T(4,128)S(1)} %pad_maximum_fusion.2), channel_id=1, source_target_pairs={{0,4},{4,8},{8,12},{12,16},{16,20},{20,24},{24,28},{1,5},{5,9},{9,... | collective-permute-start | bytes 13832 | tf_op jit(solution)/shard_map/ppermute | solution.py:31
  12.8 5.8 %collective-permute-start.5 = (f32[1,3,3,128]{3,2,1,0:T(4,128)S(1)}, f32[1,3,3,128]{3,2,1,0:T(4,128)S(1)}, u32[]{:S(2)}, u32[]{:S(2)}) collective-permute-start(f32[1,3,3,128]{3,2,1,0:T(4,128)S(1)} %pad_maximum_fusion.3), channel_id=1, source_target_pairs={{4,0},{8,4},{12,8},{16,12},{20,16},{24,20},{28,24},{5,1},{9,5},{13... | collective-permute-start | bytes 13832 | tf_op jit(solution)/shard_map/ppermute | solution.py:31
  18.6 0.7 copy-start.1
  19.3 0.9 %copy-start.2 = (f32[128,192]{0,1:T(8,128)S(1)}, f32[128,192]{0,1:T(8,128)}, u32[]{:S(2)}) copy-start(f32[128,192]{0,1:T(8,128)} %param.22) | copy-start | bytes 294916
  20.2 0.8 %copy-start.3 = (f32[192,64]{0,1:T(8,128)S(1)}, f32[192,64]{0,1:T(8,128)}, u32[]{:S(2)}) copy-start(f32[192,64]{0,1:T(8,128)} %param.21) | copy-start | bytes 147460
  21.0 0.7 %copy-start.4 = (s32[2,1,24,128]{3,2,1,0:T(8,128)S(1)}, s32[2,1,24,128]{3,2,1,0:T(8,128)}, u32[]{:S(2)}) copy-start(s32[2,1,24,128]{3,2,1,0:T(8,128)} %codes_ref.1) | copy-start | bytes 73732
  21.8 0.7 copy-start.5
  22.5 0.7 copy-start.6
  23.1 0.7 copy-start.7
  23.8 13.7 %copy-start = (bf16[2,1,576,128]{3,2,1,0:T(8,128)(2,1)S(1)}, bf16[2,1,576,128]{3,2,1,0:T(8,128)(2,1)}, u32[]{:S(2)}) copy-start(bf16[2,1,576,128]{3,2,1,0:T(8,128)(2,1)} %own_ref.1) | copy-start | bytes 884740
  31.0 14.5 %collective-permute-start.7 = (bf16[1,3,576,128]{3,2,1,0:T(8,128)(2,1)S(1)}, bf16[1,3,576,128]{3,2,1,0:T(8,128)(2,1)S(1)}, u32[]{:S(2)}, u32[]{:S(2)}) collective-permute-start(bf16[1,3,576,128]{3,2,1,0:T(8,128)(2,1)S(1)} %pad_maximum_fusion.1), channel_id=1, source_target_pairs={{4,0},{8,4},{12,8},{16,12},{20,16},{24,20},{28,24},{5,1},{9,5},{13... | collective-permute-start | bytes 1327112 | tf_op jit(solution)/shard_map/ppermute | solution.py:31
  33.0 12.5 %collective-permute-start.6 = (bf16[1,3,576,128]{3,2,1,0:T(8,128)(2,1)S(1)}, bf16[1,3,576,128]{3,2,1,0:T(8,128)(2,1)S(1)}, u32[]{:S(2)}, u32[]{:S(2)}) collective-permute-start(bf16[1,3,576,128]{3,2,1,0:T(8,128)(2,1)S(1)} %pad_maximum_fusion), channel_id=1, source_target_pairs={{0,4},{4,8},{8,12},{12,16},{16,20},{20,24},{24,28},{1,5},{5,9},{9,... | collective-permute-start | bytes 1327112 | tf_op jit(solution)/shard_map/ppermute | solution.py:31
  45.5 17.0 %copy-start.8 = (f32[2,1,3,128]{3,1,2,0:T(1,128)S(1)}, f32[2,1,3,128]{3,1,2,0:T(1,128)}, u32[]{:S(2)}) copy-start(f32[2,1,3,128]{3,1,2,0:T(1,128)} %param.16) | copy-start | bytes 9220
  45.5 26.8 %copy-start.9 = (f32[1,3,128]{2,0,1:T(1,128)S(1)}, f32[1,3,128]{2,0,1:T(1,128)}, u32[]{:S(2)}) copy-start(f32[1,3,128]{2,0,1:T(1,128)} %param.25) | copy-start | bytes 4612
  45.5 27.4 %copy-start.10 = (f32[1,3,128]{2,0,1:T(1,128)S(1)}, f32[1,3,128]{2,0,1:T(1,128)}, u32[]{:S(2)}) copy-start(f32[1,3,128]{2,0,1:T(1,128)} %param.24) | copy-start | bytes 4612
  61.0 2.5 %collective-permute-start.8 = (f32[4,3,1,128]{3,2,1,0:T(1,128)S(1)}, f32[4,3,1,128]{3,2,1,0:T(1,128)S(1)}, u32[]{:S(2)}, u32[]{:S(2)}) collective-permute-start(f32[4,3,1,128]{3,2,1,0:T(1,128)S(1)} %get-tuple-element.53), channel_id=1, source_target_pairs={{0,3},{1,0},{2,1},{3,2},{4,7},{5,4},{6,5},{7,6},{8,11},{9,8},{10,9... | collective-permute-start | bytes 18440 | tf_op jit(solution)/shard_map/ppermute | solution.py:25
  62.1 4.3 %collective-permute-start.9 = (f32[4,3,1,128]{3,2,1,0:T(1,128)S(1)}, f32[4,3,1,128]{3,2,1,0:T(1,128)S(1)}, u32[]{:S(2)}, u32[]{:S(2)}) collective-permute-start(f32[4,3,1,128]{3,2,1,0:T(1,128)S(1)} %get-tuple-element.54), channel_id=1, source_target_pairs={{0,1},{1,2},{2,3},{3,0},{4,5},{5,6},{6,7},{7,4},{8,9},{9,10},{10,1... | collective-permute-start | bytes 18440 | tf_op jit(solution)/shard_map/ppermute | solution.py:25
  66.5 5.8 %collective-permute-start.10 = (f32[4,3,1,128]{3,2,1,0:T(1,128)S(1)}, f32[4,3,1,128]{3,2,1,0:T(1,128)S(1)}, u32[]{:S(2)}, u32[]{:S(2)}) collective-permute-start(f32[4,3,1,128]{3,2,1,0:T(1,128)S(1)} %pad_maximum_fusion.4), channel_id=1, source_target_pairs={{4,0},{8,4},{12,8},{16,12},{20,16},{24,20},{28,24},{5,1},{9,5},{13... | collective-permute-start | bytes 18440 | tf_op jit(solution)/shard_map/ppermute | solution.py:31

commit v3 on v2

--- a/solution.py
+++ b/solution.py
@@ -16,6 +16,7 @@
 BF16 = jnp.bfloat16
 LANES = 128
 QUAD = 4
+UNROLL = 2
 EDGE_LIMIT = 16
 LOCAL_LIMIT = 16
 
@@ -103,17 +104,17 @@
     rows,
     cols,
     slots,
-    own_ref,
     left_ref,
     right_ref,
     prev_ref,
     next_ref,
-    codes_ref,
-    counts_ref,
-    w1_ref,
-    w2_ref,
-    wr_ref,
-    wo_ref,
+    own_hbm,
+    codes_hbm,
+    counts_hbm,
+    w1_hbm,
+    w2_hbm,
+    wr_hbm,
+    wo_hbm,
     geo,
     har,
     near,
@@ -125,11 +126,29 @@
     pos_ref,
     w1s,
     w2s,
+    own_ref,
+    codes_ref,
+    counts_ref,
+    w1_ref,
+    w2_ref,
+    wr_ref,
+    wo_ref,
+    sems,
 ):
     blocks = rows * cols
     quads = slots // QUAD
     wide = QUAD * LANES
     root3, root5, root15 = math.sqrt(3.0), math.sqrt(5.0), math.sqrt(15.0)
+
+    sources = [own_hbm, codes_hbm, counts_hbm, w1_hbm, w2_hbm, wr_hbm, wo_hbm]
+    places = [own_ref, codes_ref, counts_ref, w1_ref, w2_ref, wr_ref, wo_ref]
+    copies = [
+        pltpu.make_async_copy(x, y, sems.at[i]) for i, (x, y) in enumerate(zip(sources, places))
+    ]
+    for copy in copies:
+        copy.start()
+    for copy in copies:
+        copy.wait()
 
     hi, lo = weight_halves(w1_ref[...].T)
     w1s[...] = jnp.concatenate([hi, hi, lo, lo], axis=1).astype(BF16)
@@ -226,10 +245,10 @@
         dsc[step] = dot(w2s[...], value_rows(dh * dpre * env + h * denv))
         return 0
 
-    lax.fori_loop(0, blocks * quads, network, 0)
-
-
-def local_kernel(rows, cols, own_ref, left_ref, right_ref, near, geo, out, win, onehot):
+    lax.fori_loop(0, blocks * quads, network, 0, unroll=UNROLL)
+
+
+def local_kernel(rows, cols, own_ref, left_ref, right_ref, near, geo, out, win, onehot_even, onehot_odd):
     blocks = rows * cols
     steps = near.shape[0]
     quads = steps // blocks
@@ -255,7 +274,7 @@
         for c in range(cols):
             place_block(own_ref[r, c], r + 1, c + 1)
 
-    def body(step, _):
+    def pick(onehot, step):
         b, first = step // quads, (step % quads) * QUAD
         k0 = jnp.where(b // cols == 0, 3, 0) if spans == 6 else jnp.int32(0)
         place = joined(geo, b, 8, first, QUAD)
@@ -263,9 +282,13 @@
         for k in range(spans):
             onehot[k * LANES : (k + 1) * LANES, :] = parts[k]
         out[step] = dot(win[b], onehot[...]).astype(BF16)
+
+    def body(i, _):
+        pick(onehot_even, 2 * i)
+        pick(onehot_odd, 2 * i + 1)
         return 0
 
-    lax.fori_loop(0, steps, body, 0)
+    lax.fori_loop(0, steps // 2, body, 0)
 
 
 RING = 3
@@ -294,7 +317,8 @@
     force_ref,
     win,
     xl,
-    xg,
+    xg_even,
+    xg_odd,
     wsc,
     dsc,
     acc,
@@ -347,7 +371,7 @@
                     win[b, :, k * LANES : (k + 1) * LANES] = jnp.zeros_like(prev_ref[0, 0])
     acc[...] = jnp.zeros(acc.shape, F32)
 
-    def gather(step):
+    def gather(xg, step):
         b, first = step // quads, (step % quads) * QUAD
         r = b // cols
         k0 = jnp.where(r == 0, 0, jnp.where(r == rows - 1, 6, 9))
@@ -355,11 +379,11 @@
         onehot = jnp.concatenate(window_hot(near[step], place, k0, 3), axis=0)
         if stream:
             x_copy(step).wait()
-            xg[step] = xl[step % RING].astype(F32) + dot(win[b], onehot)
+            xg[step // 2] = xl[step % RING].astype(F32) + dot(win[b], onehot)
         else:
-            xg[step] = xl_hbm[step].astype(F32) + dot(win[b], onehot)
-
-    def collect(step):
+            xg[step // 2] = xl_hbm[step].astype(F32) + dot(win[b], onehot)
+
+    def collect(xg, step):
         b, first = step // quads, (step % quads) * QUAD
         for g in range(channels // group):
             at = g * group
@@ -367,7 +391,7 @@
             for s in range(QUAD):
                 ln = slice(s * LANES, (s + 1) * LANES)
                 xs = [
-                    xg[step, m * channels + at : m * channels + at + group, ln]
+                    xg[step // 2, m * channels + at : m * channels + at + group, ln]
                     for m in range(9)
                 ]
                 w0, w1, w2 = [
@@ -383,24 +407,28 @@
             for m in range(9):
                 acc[b, m, at : at + group, :] = total[m]
 
-    def forward(step, _):
+    def advance(xg, xg_last, step, last):
         if stream:
             w_copy(step - 1).wait()
-        collect(step - 1)
-        gather(step)
-        if stream:
+        gather(xg, step)
+        collect(xg_last, step - 1)
+        if stream and not last:
 
             @pl.when(step + RING - 1 < steps)
             def _():
                 x_copy(step + RING - 1).start()
 
+    def forward(i, _):
+        advance(xg_even, xg_odd, 2 * i, False)
+        advance(xg_odd, xg_even, 2 * i + 1, False)
         return 0
 
-    gather(0)
-    lax.fori_loop(1, steps, forward, 0)
+    gather(xg_even, 0)
+    advance(xg_odd, xg_even, 1, False)
+    lax.fori_loop(1, steps // 2, forward, 0)
     if stream:
         w_copy(steps - 1).wait()
-    collect(steps - 1)
+    collect(xg_odd, steps - 1)
 
     for b in range(blocks):
         ln = slice(b * LANES, (b + 1) * LANES)
@@ -424,7 +452,7 @@
             d = dinv[part * channels : (part + 1) * channels, ln]
             acc[b, m] = 2.0 * acc[b, m] * d
 
-    def backward(step, _):
+    def edge_terms(xg, step):
         b, first = step // quads, (step % quads) * QUAD
         if stream:
             d_copy(step).wait()
@@ -435,7 +463,7 @@
             for g in range(channels // group):
                 at = g * group
                 xs = [
-                    xg[step, m * channels + at : m * channels + at + group, ln]
+                    xg[step // 2, m * channels + at : m * channels + at + group, ln]
                     for m in range(9)
                 ]
                 gs = [acc[b, m, at : at + group, :] for m in range(9)]
@@ -459,9 +487,13 @@
                 dy[8] = dy[8] + (d0 * xs[0] * along + d1 * direct + d2 * gs[0] * vec)
             for m in range(9):
                 dys[b, m, pl.ds(first + s, 1), :] = jnp.sum(dy[m], axis=0, keepdims=True)
+
+    def backward(i, _):
+        edge_terms(xg_even, 2 * i)
+        edge_terms(xg_odd, 2 * i + 1)
         return 0
 
-    lax.fori_loop(0, steps, backward, 0)
+    lax.fori_loop(0, steps // 2, backward, 0)
     force_ref[...] = jnp.zeros(force_ref.shape, F32)
 
     def pull(b, _):
@@ -531,11 +563,12 @@
     weights = w_second.shape[0]
     blocks, steps, wide = rows * cols, rows * cols * slots // QUAD, QUAD * LANES
     vmem = pl.BlockSpec(memory_space=pltpu.VMEM)
+    hbm = pl.BlockSpec(memory_space=pltpu.HBM)
     sds = jax.ShapeDtypeStruct
     call = vmem_call(
         functools.partial(edge_kernel, rows, cols, slots),
         "edges",
-        [vmem] * 11,
+        [vmem] * 4 + [hbm] * 7,
         [
             sds((blocks, 9, slots, LANES), F32),
             sds((blocks, 8, slots, LANES), F32),
@@ -550,19 +583,28 @@
             pltpu.VMEM((rows + 2, cols + 2, 3, LANES), F32),
             pltpu.VMEM((hidden, 4 * basis), BF16),
             pltpu.VMEM((weights, 3 * hidden), BF16),
+            pltpu.VMEM((rows, 3, cols, LANES), F32),
+            pltpu.VMEM((rows, cols, slots, LANES), jnp.int32),
+            pltpu.VMEM((rows, cols, 1, LANES), jnp.int32),
+            pltpu.VMEM((basis, hidden), F32),
+            pltpu.VMEM((hidden, weights), F32),
+            pltpu.VMEM((reads, units), F32),
+            pltpu.VMEM((1, units), F32),
+            pltpu.SemaphoreType.DMA((7,)),
         ],
         EDGE_LIMIT,
         2 * 6 * 2 * weights * hidden * steps * wide,
     )
-    return call(
-        *pos,
+    args = [
+        pos[0],
         neighbours,
         counts.reshape(rows, cols, 1, LANES),
         w_first.T,
         w_second.T,
         w_read.T,
         w_out.reshape(1, units),
-    )
+    ]
+    return call(*pos[1:], *[pltpu.with_memory_space_constraint(x, pltpu.HBM) for x in args])
 
 
 def local_part(own, left, right, near, geo):
@@ -577,6 +619,7 @@
         [jax.ShapeDtypeStruct((steps, feats, wide), BF16)],
         [
             pltpu.VMEM((rows * cols, feats, spans * LANES), BF16),
+            pltpu.VMEM((spans * LANES, wide), BF16),
             pltpu.VMEM((spans * LANES, wide), BF16),
         ],
         LOCAL_LIMIT,
@@ -605,7 +648,8 @@
             pltpu.VMEM((rows + 2, cols + 2, 3, LANES), F32),
             pltpu.VMEM((blocks, feats, 3 * LANES), BF16),
             pltpu.VMEM((RING, feats, wide) if stream else (1, 16, LANES), BF16),
-            pltpu.VMEM((steps, feats, wide), F32),
+            pltpu.VMEM((steps // 2, feats, wide), F32),
+            pltpu.VMEM((steps // 2, feats, wide), F32),
             pltpu.VMEM((steps, weights, wide) if stream else (1, 8, LANES), F32),
             pltpu.VMEM((steps, weights, wide) if stream else (1, 8, LANES), F32),
             pltpu.VMEM((blocks, 9, channels, LANES), F32),
@@ -641,7 +685,7 @@
     nrows, ncols = (positions.shape[0], positions.shape[1])
     shock_place = lax.axis_index("shock")
     front = lax.axis_size("shock") - 1
-    assert nrows >= 2 and neighbours.shape[2] % QUAD == 0
+    assert nrows >= 2 and neighbours.shape[2] % (2 * QUAD) == 0
 
     def sides(x, axis):
         last = lax.slice_in_dim(x, ncols - 1, ncols, axis=axis)

time: 74.4 us -> 66.9 us (0.90)
  local copies, waits for them, and re-layouts: 6.95 us -> 1.77 us
  Pallas kernels: 30.4 us -> 27.2 us
    unnamed x22 -> x8, local copies, waits for them, and re-layouts: 5.19 us -> 0.01 us
    pallas_call x1, Pallas kernels: 15.4 us -> 13.3 us  [energy_part(): call(before, after, geo, har, near, wrs, wrt, woc, wsc, dsc, gathered)]
    pallas_call x1, Pallas kernels: 7.92 us -> 6.83 us  [local_part(): return call(own, left, right, near, geo)[0]]
  transfers between devices with their start and end apart: 11 -> 11, of which waited for: 4 -> 5; matrix products, arithmetic and copies ran while one was open for 2% -> 3% of each run, Pallas kernels for 20% -> 21%
where the time goes in v3:
time: 66.9 us; the launch traced here: 65.9 us
  Pallas kernels  27.2 us (41%)
  starting transfers between devices  23.2 us (35%)
  waiting for transfers between devices  11.5 us (17%)
  local copies, waits for them, and re-layouts  1.77 us (3%)
  other arithmetic  1.34 us (2%)
  between operations  0.84 us (1%)
    ppermute x5, starting transfers between devices, passed_along(): return lax.ppermute(block, axis, route)  15 us
    pallas_call x1, Pallas kernels, energy_part(): call(before, after, geo, har, near, wrs, wrt, woc, wsc, dsc, gathered)  13.3 us
    ppermute x6, starting transfers between devices, shifted(): return lax.ppermute(x, axis, [(i, (i + by) % count) for i in range(count)])  8.26 us
    ppermute x5, waiting for transfers between devices, passed_along(): return lax.ppermute(block, axis, route)  7.24 us
    pallas_call x1, Pallas kernels, edge_part(): call(*pos[1:], *[pltpu.with_memory_space_constraint(x, pltpu.HBM) for x i...  7.11 us
    pallas_call x1, Pallas kernels, local_part(): return call(own, left, right, near, geo)[0]  6.83 us
    ppermute x6, waiting for transfers between devices, shifted(): return lax.ppermute(x, axis, [(i, (i + by) % count) for i in range(count)])  4.28 us
    slice x5, local copies, waits for them, and re-layouts, ends(): first = jnp.concatenate([left[:1], x[:1], right[:1]], axis=axis)  1.75 us
  transfers between devices with their start and end apart: 11, of which 5 were waited for; matrix products, arithmetic and copies ran while one was open for 3% of the time, Pallas kernels for 21%

profile of v3, /device:TPU:3, one launch (start us, length us, event | category | flops | bytes accessed | tf_op | source)
XLA Modules:
  0.0 65.9 jit_solution(9643543857971649097)
XLA Ops:
  0.6 1.3 %collective-permute-start.2 = (f32[2,3,1,128]{3,2,1,0:T(1,128)}, f32[2,3,1,128]{3,2,1,0:T(1,128)S(1)}, u32[]{:S(2)}, u32[]{:S(2)}) collective-permute-start(f32[2,3,1,128]{3,2,1,0:T(1,128)} %bitcast.33), channel_id=1, source_target_pairs={{0,1},{1,2},{2,3},{3,0},{4,5},{5,6},{6,7},{7,4},{8,9},{9,10},{10,1... | collective-permute-start | bytes 9224 | tf_op jit(solution)/shard_map/ppermute | solution.py:26
  2.0 2.1 %collective-permute-start.3 = (f32[2,3,1,128]{3,2,1,0:T(1,128)}, f32[2,3,1,128]{3,2,1,0:T(1,128)S(1)}, u32[]{:S(2)}, u32[]{:S(2)}) collective-permute-start(f32[2,3,1,128]{3,2,1,0:T(1,128)} %bitcast.34), channel_id=1, source_target_pairs={{0,3},{1,0},{2,1},{3,2},{4,7},{5,4},{6,5},{7,6},{8,11},{9,8},{10,9... | collective-permute-start | bytes 9224 | tf_op jit(solution)/shard_map/ppermute | solution.py:26
  4.1 0.0 collective-permute-start
  4.1 3.3 %collective-permute-start.1 = (bf16[2,1,576,128]{3,2,1,0:T(8,128)(2,1)}, bf16[2,1,576,128]{3,2,1,0:T(8,128)(2,1)S(1)}, u32[]{:S(2)}, u32[]{:S(2)}) collective-permute-start(bf16[2,1,576,128]{3,2,1,0:T(8,128)(2,1)} %own_ref.1), channel_id=1, source_target_pairs={{0,3},{1,0},{2,1},{3,2},{4,7},{5,4},{6,5},{7,6},{8,11},{9,8},{10,9... | collective-permute-start | bytes 884744 | tf_op jit(solution)/shard_map/ppermute | solution.py:26
  7.3 0.7 %slice_bitcast_fusion.2 = (f32[1,3,1,128]{3,2,1,0:T(1,128)S(1)}, f32[1,3,1,128]{3,2,1,0:T(1,128)S(1)}) fusion(f32[2,1,3,128]{3,1,2,0:T(1,128)} %param.15), kind=kLoop, calls=%fused_computation.16 | loop fusion | bytes 6144 | tf_op jit(solution)/shard_map/slice | solution.py:697
  8.0 0.0 collective-permute-done.2.left_ref
  8.0 0.0 collective-permute-done.3.right_ref
  8.1 4.7 %collective-permute-start.4 = (f32[1,3,3,128]{3,2,1,0:T(4,128)S(1)}, f32[1,3,3,128]{3,2,1,0:T(4,128)S(1)}, u32[]{:S(2)}, u32[]{:S(2)}) collective-permute-start(f32[1,3,3,128]{3,2,1,0:T(4,128)S(1)} %pad_maximum_fusion.2), channel_id=1, source_target_pairs={{0,4},{4,8},{8,12},{12,16},{16,20},{20,24},{24,28},{1,5},{5,9},{9,... | collective-permute-start | bytes 13832 | tf_op jit(solution)/shard_map/ppermute | solution.py:32
  12.8 1.9 %collective-permute-start.5 = (f32[1,3,3,128]{3,2,1,0:T(4,128)S(1)}, f32[1,3,3,128]{3,2,1,0:T(4,128)S(1)}, u32[]{:S(2)}, u32[]{:S(2)}) collective-permute-start(f32[1,3,3,128]{3,2,1,0:T(4,128)S(1)} %pad_maximum_fusion.3), channel_id=1, source_target_pairs={{4,0},{8,4},{12,8},{16,12},{20,16},{24,20},{28,24},{5,1},{9,5},{13... | collective-permute-start | bytes 13832 | tf_op jit(solution)/shard_map/ppermute | solution.py:32
  14.7 1.0 %fusion.4 = (bf16[1,1,576,128]{3,2,1,0:T(8,128)(2,1)S(1)}, bf16[1,1,576,128]{3,2,1,0:T(8,128)(2,1)S(1)}) fusion(bf16[2,1,576,128]{3,2,1,0:T(8,128)(2,1)} %own_ref.1), kind=kLoop, calls=%fused_computation.19 | loop fusion | bytes 589824 | tf_op jit(solution)/shard_map/slice | solution.py:697
  15.7 0.0 collective-permute-done.4.prev_ref
  15.7 2.9 %collective-permute-done.5.next_ref = f32[1,3,3,128]{3,2,1,0:T(4,128)S(1)} collective-permute-done((f32[1,3,3,128]{3,2,1,0:T(4,128)S(1)}, f32[1,3,3,128]{3,2,1,0:T(4,128)S(1)}, u32[]{:S(2)}, u32[]{:S(2)}) %collective-permute-start.5) | collective-permute-done | bytes 4640 | tf_op jit(solution)/shard_map/ppermute | solution.py:32
  18.6 7.1 %edges.1 = (f32[2,9,24,128]{3,2,1,0:T(8,128)S(1)}, f32[2,8,24,128]{3,2,1,0:T(8,128)S(1)}, bf16[12,128,512]{2,1,0:T(8,128)(2,1)S(1)}, f32[12,192,512]{2,1,0:T(8,1...) custom-call(f32[2,3,1,128]{3,2,1,0:T(1,128)S(1)} %collective-permute, ...), custom_call_target="tpu_custom_call" | custom-call | flops 1811939328 | bytes 1048576 | tf_op jit(solution)/shard_map/edges/pallas_call | solution.py:607
  25.7 0.0 collective-permute-done.left_ref
  25.8 0.0 collective-permute-done.1.right_ref
  25.8 0.1 pad_maximum_fusion.1
  25.9 1.9 %collective-permute-start.7 = (bf16[1,3,576,128]{3,2,1,0:T(8,128)(2,1)S(1)}, bf16[1,3,576,128]{3,2,1,0:T(8,128)(2,1)S(1)}, u32[]{:S(2)}, u32[]{:S(2)}) collective-permute-start(bf16[1,3,576,128]{3,2,1,0:T(8,128)(2,1)S(1)} %pad_maximum_fusion.1), channel_id=1, source_target_pairs={{4,0},{8,4},{12,8},{16,12},{20,16},{24,20},{28,24},{5,1},{9,5},{13... | collective-permute-start | bytes 1327112 | tf_op jit(solution)/shard_map/ppermute | solution.py:32
  27.8 0.1 pad_maximum_fusion
  27.9 4.5 %collective-permute-start.6 = (bf16[1,3,576,128]{3,2,1,0:T(8,128)(2,1)S(1)}, bf16[1,3,576,128]{3,2,1,0:T(8,128)(2,1)S(1)}, u32[]{:S(2)}, u32[]{:S(2)}) collective-permute-start(bf16[1,3,576,128]{3,2,1,0:T(8,128)(2,1)S(1)} %pad_maximum_fusion), channel_id=1, source_target_pairs={{0,4},{4,8},{8,12},{12,16},{16,20},{20,24},{24,28},{1,5},{5,9},{9,... | collective-permute-start | bytes 1327112 | tf_op jit(solution)/shard_map/ppermute | solution.py:32
  32.4 0.0 copy-done
  32.4 6.8 %local.1.xl_hbm = bf16[12,576,512]{2,1,0:T(8,128)(2,1)S(1)} custom-call(bf16[2,1,576,128]{3,2,1,0:T(8,128)(2,1)S(1)} %copy-done, bf16[2,1,576,128]{3,2,1,0:T(8,128)(2,1)S(1)} %collective-permute-done.left_ref, bf16[2,1,576,128]{3,2,1,0:T(8,128)(2,1)S(1)} %collective-permute-done.1.right_ref, bf16[12,128,512]{2,1,0:T(8,128)(2,1)S(1)} %get-tuple-element.45.near, ...), custom_call_target="tpu_custom_call" | custom-call | flops 5435817984 | bytes 1048576 | tf_op jit(solution)/shard_map/local/pallas_call | solution.py:628
  39.3 0.4 collective-permute-done.7.next_ref
  39.7 0.0 collective-permute-done.6.prev_ref
  39.7 13.3 %energy.1 = (f32[2,1,1,128]{3,2,1,0:T(1,128)}, f32[4,3,1,128]{3,2,1,0:T(1,128)S(1)}, f32[4,3,1,128]{3,2,1,0:T(1,128)S(1)}, f32[4,3,1,128]{3,2,1,0:T(1,128)S(1)}) custom-call(bf16[1,3,576,128]{3,2,1,0:T(8,128)(2,1)S(1)} %collective-permute-done.6.prev_ref, bf16[1,3,576,128]{3,2,1,0:T(8,128)(2,1)S(1)} %collective-permute-done.7.next_ref, ...), custom_call_target="tpu_custom_call" | custom-call | flops 8153726976 | bytes 1048576 | tf_op jit(solution)/shard_map/energy/pallas_call | solution.py:666
  53.0 1.6 %collective-permute-start.8 = (f32[4,3,1,128]{3,2,1,0:T(1,128)S(1)}, f32[4,3,1,128]{3,2,1,0:T(1,128)S(1)}, u32[]{:S(2)}, u32[]{:S(2)}) collective-permute-start(f32[4,3,1,128]{3,2,1,0:T(1,128)S(1)} %get-tuple-element.53), channel_id=1, source_target_pairs={{0,3},{1,0},{2,1},{3,2},{4,7},{5,4},{6,5},{7,6},{8,11},{9,8},{10,9... | collective-permute-start | bytes 18440 | tf_op jit(solution)/shard_map/ppermute | solution.py:26
  54.5 0.0 collective-permute-start.9
  54.6 1.0 %collective-permute-done.8 = f32[4,3,1,128]{3,2,1,0:T(1,128)S(1)} collective-permute-done((f32[4,3,1,128]{3,2,1,0:T(1,128)S(1)}, f32[4,3,1,128]{3,2,1,0:T(1,128)S(1)}, u32[]{:S(2)}, u32[]{:S(2)}) %collective-permute-start.8) | collective-permute-done | bytes 6176 | tf_op jit(solution)/shard_map/ppermute | solution.py:26
  55.5 3.3 %collective-permute-done.9 = f32[4,3,1,128]{3,2,1,0:T(1,128)S(1)} collective-permute-done((f32[4,3,1,128]{3,2,1,0:T(1,128)S(1)}, f32[4,3,1,128]{3,2,1,0:T(1,128)S(1)}, u32[]{:S(2)}, u32[]{:S(2)}) %collective-permute-start.9) | collective-permute-done | bytes 6176 | tf_op jit(solution)/shard_map/ppermute | solution.py:26
  58.9 1.9 %collective-permute-start.10 = (f32[4,3,1,128]{3,2,1,0:T(1,128)S(1)}, f32[4,3,1,128]{3,2,1,0:T(1,128)S(1)}, u32[]{:S(2)}, u32[]{:S(2)}) collective-permute-start(f32[4,3,1,128]{3,2,1,0:T(1,128)S(1)} %pad_maximum_fusion.4), channel_id=1, source_target_pairs={{4,0},{8,4},{12,8},{16,12},{20,16},{24,20},{28,24},{5,1},{9,5},{13... | collective-permute-start | bytes 18440 | tf_op jit(solution)/shard_map/ppermute | solution.py:32
  60.8 3.9 %collective-permute-done.10 = f32[4,3,1,128]{3,2,1,0:T(1,128)S(1)} collective-permute-done((f32[4,3,1,128]{3,2,1,0:T(1,128)S(1)}, f32[4,3,1,128]{3,2,1,0:T(1,128)S(1)}, u32[]{:S(2)}, u32[]{:S(2)}) %collective-permute-start.10) | collective-permute-done | bytes 6176 | tf_op jit(solution)/shard_map/ppermute | solution.py:32
  64.8 0.6 maximum_bitcast_fusion.1
  65.3 0.6 maximum_bitcast_fusion
  (20 shorter events, 0.1 us)
Async XLA Ops:
  0.6 7.4 %collective-permute-start.2 = (f32[2,3,1,128]{3,2,1,0:T(1,128)}, f32[2,3,1,128]{3,2,1,0:T(1,128)S(1)}, u32[]{:S(2)}, u32[]{:S(2)}) collective-permute-start(f32[2,3,1,128]{3,2,1,0:T(1,128)} %bitcast.33), channel_id=1, source_target_pairs={{0,1},{1,2},{2,3},{3,0},{4,5},{5,6},{6,7},{7,4},{8,9},{9,10},{10,1... | collective-permute-start | bytes 9224 | tf_op jit(solution)/shard_map/ppermute | solution.py:26
  2.0 6.1 %collective-permute-start.3 = (f32[2,3,1,128]{3,2,1,0:T(1,128)}, f32[2,3,1,128]{3,2,1,0:T(1,128)S(1)}, u32[]{:S(2)}, u32[]{:S(2)}) collective-permute-start(f32[2,3,1,128]{3,2,1,0:T(1,128)} %bitcast.34), channel_id=1, source_target_pairs={{0,3},{1,0},{2,1},{3,2},{4,7},{5,4},{6,5},{7,6},{8,11},{9,8},{10,9... | collective-permute-start | bytes 9224 | tf_op jit(solution)/shard_map/ppermute | solution.py:26
  4.1 21.7 %collective-permute-start = (bf16[2,1,576,128]{3,2,1,0:T(8,128)(2,1)}, bf16[2,1,576,128]{3,2,1,0:T(8,128)(2,1)S(1)}, u32[]{:S(2)}, u32[]{:S(2)}) collective-permute-start(bf16[2,1,576,128]{3,2,1,0:T(8,128)(2,1)} %own_ref.1), channel_id=1, source_target_pairs={{0,1},{1,2},{2,3},{3,0},{4,5},{5,6},{6,7},{7,4},{8,9},{9,10},{10,1... | collective-permute-start | bytes 884744 | tf_op jit(solution)/shard_map/ppermute | solution.py:26
  4.1 21.7 %collective-permute-start.1 = (bf16[2,1,576,128]{3,2,1,0:T(8,128)(2,1)}, bf16[2,1,576,128]{3,2,1,0:T(8,128)(2,1)S(1)}, u32[]{:S(2)}, u32[]{:S(2)}) collective-permute-start(bf16[2,1,576,128]{3,2,1,0:T(8,128)(2,1)} %own_ref.1), channel_id=1, source_target_pairs={{0,3},{1,0},{2,1},{3,2},{4,7},{5,4},{6,5},{7,6},{8,11},{9,8},{10,9... | collective-permute-start | bytes 884744 | tf_op jit(solution)/shard_map/ppermute | solution.py:26
  8.1 7.6 %collective-permute-start.4 = (f32[1,3,3,128]{3,2,1,0:T(4,128)S(1)}, f32[1,3,3,128]{3,2,1,0:T(4,128)S(1)}, u32[]{:S(2)}, u32[]{:S(2)}) collective-permute-start(f32[1,3,3,128]{3,2,1,0:T(4,128)S(1)} %pad_maximum_fusion.2), channel_id=1, source_target_pairs={{0,4},{4,8},{8,12},{12,16},{16,20},{20,24},{24,28},{1,5},{5,9},{9,... | collective-permute-start | bytes 13832 | tf_op jit(solution)/shard_map/ppermute | solution.py:32
  12.8 5.8 %collective-permute-start.5 = (f32[1,3,3,128]{3,2,1,0:T(4,128)S(1)}, f32[1,3,3,128]{3,2,1,0:T(4,128)S(1)}, u32[]{:S(2)}, u32[]{:S(2)}) collective-permute-start(f32[1,3,3,128]{3,2,1,0:T(4,128)S(1)} %pad_maximum_fusion.3), channel_id=1, source_target_pairs={{4,0},{8,4},{12,8},{16,12},{20,16},{24,20},{28,24},{5,1},{9,5},{13... | collective-permute-start | bytes 13832 | tf_op jit(solution)/shard_map/ppermute | solution.py:32
  18.6 13.8 %copy-start = (bf16[2,1,576,128]{3,2,1,0:T(8,128)(2,1)S(1)}, bf16[2,1,576,128]{3,2,1,0:T(8,128)(2,1)}, u32[]{:S(2)}) copy-start(bf16[2,1,576,128]{3,2,1,0:T(8,128)(2,1)} %own_ref.1) | copy-start | bytes 884740
  25.9 13.8 %collective-permute-start.7 = (bf16[1,3,576,128]{3,2,1,0:T(8,128)(2,1)S(1)}, bf16[1,3,576,128]{3,2,1,0:T(8,128)(2,1)S(1)}, u32[]{:S(2)}, u32[]{:S(2)}) collective-permute-start(bf16[1,3,576,128]{3,2,1,0:T(8,128)(2,1)S(1)} %pad_maximum_fusion.1), channel_id=1, source_target_pairs={{4,0},{8,4},{12,8},{16,12},{20,16},{24,20},{28,24},{5,1},{9,5},{13... | collective-permute-start | bytes 1327112 | tf_op jit(solution)/shard_map/ppermute | solution.py:32
  27.9 11.8 %collective-permute-start.6 = (bf16[1,3,576,128]{3,2,1,0:T(8,128)(2,1)S(1)}, bf16[1,3,576,128]{3,2,1,0:T(8,128)(2,1)S(1)}, u32[]{:S(2)}, u32[]{:S(2)}) collective-permute-start(bf16[1,3,576,128]{3,2,1,0:T(8,128)(2,1)S(1)} %pad_maximum_fusion), channel_id=1, source_target_pairs={{0,4},{4,8},{8,12},{12,16},{16,20},{20,24},{24,28},{1,5},{5,9},{9,... | collective-permute-start | bytes 1327112 | tf_op jit(solution)/shard_map/ppermute | solution.py:32
  39.7 14.9 %copy-start.1 = (f32[2,1,3,128]{3,1,2,0:T(1,128)S(1)}, f32[2,1,3,128]{3,1,2,0:T(1,128)}, u32[]{:S(2)}) copy-start(f32[2,1,3,128]{3,1,2,0:T(1,128)} %param.16) | copy-start | bytes 9220
  39.7 25.0 %copy-start.2 = (f32[1,3,128]{2,0,1:T(1,128)S(1)}, f32[1,3,128]{2,0,1:T(1,128)}, u32[]{:S(2)}) copy-start(f32[1,3,128]{2,0,1:T(1,128)} %param.25) | copy-start | bytes 4612
  39.7 25.6 %copy-start.3 = (f32[1,3,128]{2,0,1:T(1,128)S(1)}, f32[1,3,128]{2,0,1:T(1,128)}, u32[]{:S(2)}) copy-start(f32[1,3,128]{2,0,1:T(1,128)} %param.24) | copy-start | bytes 4612
  53.0 2.5 %collective-permute-start.8 = (f32[4,3,1,128]{3,2,1,0:T(1,128)S(1)}, f32[4,3,1,128]{3,2,1,0:T(1,128)S(1)}, u32[]{:S(2)}, u32[]{:S(2)}) collective-permute-start(f32[4,3,1,128]{3,2,1,0:T(1,128)S(1)} %get-tuple-element.53), channel_id=1, source_target_pairs={{0,3},{1,0},{2,1},{3,2},{4,7},{5,4},{6,5},{7,6},{8,11},{9,8},{10,9... | collective-permute-start | bytes 18440 | tf_op jit(solution)/shard_map/ppermute | solution.py:26
  54.5 4.3 %collective-permute-start.9 = (f32[4,3,1,128]{3,2,1,0:T(1,128)S(1)}, f32[4,3,1,128]{3,2,1,0:T(1,128)S(1)}, u32[]{:S(2)}, u32[]{:S(2)}) collective-permute-start(f32[4,3,1,128]{3,2,1,0:T(1,128)S(1)} %get-tuple-element.54), channel_id=1, source_target_pairs={{0,1},{1,2},{2,3},{3,0},{4,5},{5,6},{6,7},{7,4},{8,9},{9,10},{10,1... | collective-permute-start | bytes 18440 | tf_op jit(solution)/shard_map/ppermute | solution.py:26
  58.9 5.8 %collective-permute-start.10 = (f32[4,3,1,128]{3,2,1,0:T(1,128)S(1)}, f32[4,3,1,128]{3,2,1,0:T(1,128)S(1)}, u32[]{:S(2)}, u32[]{:S(2)}) collective-permute-start(f32[4,3,1,128]{3,2,1,0:T(1,128)S(1)} %pad_maximum_fusion.4), channel_id=1, source_target_pairs={{4,0},{8,4},{12,8},{16,12},{20,16},{24,20},{28,24},{5,1},{9,5},{13... | collective-permute-start | bytes 18440 | tf_op jit(solution)/shard_map/ppermute | solution.py:32

commit v4 on v2

v4 whole, which is shorter than its diff:
```python
import functools
import math

import jax
import jax.numpy as jnp
from jax import lax
from jax.experimental import pallas as pl
from jax.experimental.pallas import tpu as pltpu
from jax.sharding import PartitionSpec as P

CUTOFF_RADIUS = 9.5
BLOCK_LENGTH = 13.2
KICK_FACTOR = 4.0
MOVE_FACTOR = 0.5
F32 = jnp.float32
BF16 = jnp.bfloat16
LANES = 128
QUAD = 4


def shifted(x, axis, by):
    count = lax.axis_size(axis)
    return lax.ppermute(x, axis, [(i, (i + by) % count) for i in range(count)])


def passed_along(block, axis, distance):
    devices = range(lax.axis_size(axis))
    route = [(i - distance, i) for i in devices if i - distance in devices]
    return lax.ppermute(block, axis, route)


def halves(x):
    hi = x.astype(BF16)
    lo = (x - hi.astype(F32)).astype(BF16)
    return hi, lo


def value_rows(x):
    hi, lo = halves(x)
    return jnp.concatenate([hi, lo, hi], axis=0)


def dot(a, b):
    return jnp.dot(a, b, preferred_element_type=F32)


def sin_cos_half_turns(t):
    n = jnp.floor(t + 0.5)
    r = t - n
    odd = n - 2.0 * jnp.floor(0.5 * n)
    sign = 1.0 - 2.0 * odd
    x = math.pi * r
    y = x * x
    s = 1.0 + y * (
        -1.0 / 6
        + y
        * (
            1.0 / 120
            + y * (-1.0 / 5040 + y * (1.0 / 362880 + y * (-1.0 / 39916800 + y * (1.0 / 6227020800.0))))
        )
    )
    c = 1.0 + y * (
        -0.5
        + y
        * (
            1.0 / 24
            + y
            * (-1.0 / 720 + y * (1.0 / 40320 + y * (-1.0 / 3628800 + y * (1.0 / 479001600.0))))
        )
    )
    return sign * x * s, sign * c


def weight_halves(w):
    hi = w.astype(BF16).astype(F32)
    return hi, w - hi


def weight_rows(w):
    hi, lo = weight_halves(w)
    return jnp.concatenate([hi, hi, lo], axis=1).astype(BF16)


def joined(ref, b, k, first, count):
    lines = [ref[b, k, pl.ds(first + s, 1), :] for s in range(count)]
    return jnp.concatenate(lines, axis=1)


def lines(ref, b, first, count):
    return jnp.concatenate([ref[b, pl.ds(first + s, 1), :] for s in range(count)], axis=1)


def first_row(rows, r):
    return 1 if (rows == 2 and r == 0) else 0


def window_hot(near, place, wanted):
    lanes = near.shape[1]
    near3 = near.reshape(LANES // 16, 16, lanes)
    parts = []
    for k in wanted:
        mask = jnp.where(place == jnp.asarray(k).astype(F32), 1.0, 0.0)
        mask = jnp.broadcast_to(mask, (16, lanes)).astype(BF16)
        parts.append((near3 * mask[None]).reshape(LANES, lanes))
    return parts


def decoded(codes):
    zq = (codes >= 1152).astype(jnp.int32) + (codes >= 2304).astype(jnp.int32)
    slot = codes - 1152 * zq
    return zq, lax.shift_right_logical(slot, 7), slot & 127


def copied(sources, places, sems):
    copies = [
        pltpu.make_async_copy(x, y, sems.at[i]) for i, (x, y) in enumerate(zip(sources, places))
    ]
    for copy in copies:
        copy.start()
    return copies


def prepare_kernel(
    rows,
    cols,
    slots,
    own_ref,
    codes_hbm,
    w1_hbm,
    w2_hbm,
    wr_hbm,
    wo_hbm,
    near,
    place,
    w1s,
    w2s,
    wrs,
    wrt,
    woc,
    out,
    codes_ref,
    w1_ref,
    w2_ref,
    wr_ref,
    wo_ref,
    atoms,
    win,
    onehot_even,
    onehot_odd,
    sems,
):
    blocks = rows * cols
    quads = slots // QUAD
    wide = QUAD * LANES
    spans = win.shape[2] // LANES
    copies = copied(
        [codes_hbm, w1_hbm, w2_hbm, wr_hbm, wo_hbm],
        [codes_ref, w1_ref, w2_ref, wr_ref, wo_ref],
        sems,
    )
    copies[0].wait()
    for r in range(rows):
        for c in range(cols):
            _, block, atom = decoded(codes_ref[r, c])
            place[r * cols + c] = block.astype(F32)
            atoms[r * cols + c] = atom.astype(F32)
    feats = win.shape[1]
    for r in range(rows):
        first = first_row(rows, r)
        for c in range(cols):
            for k in range(spans):
                ln = slice(k * LANES, (k + 1) * LANES)
                if 0 <= r - 1 + first + k < rows:
                    win[r * cols + c, :, ln] = own_ref[r - 1 + first + k, c, :feats]
                else:
                    win[r * cols + c, :, ln] = jnp.zeros((feats, LANES), BF16)

    def pick(onehot, step):
        b, at = step // quads, (step % quads) * QUAD
        atom = lines(atoms, b, at, QUAD)
        sub = lax.broadcasted_iota(jnp.int32, (LANES, wide), 0).astype(F32)
        hot = jnp.where(sub == atom, 1.0, 0.0).astype(BF16)
        near[step] = hot
        first = jnp.where(b // cols == 0, first_row(rows, 0), 0)
        wanted = [3 * (first + k) + 1 for k in range(spans)]
        parts = window_hot(hot, lines(place, b, at, QUAD), wanted)
        for k in range(spans):
            onehot[k * LANES : (k + 1) * LANES, :] = parts[k]
        out[step] = dot(win[b], onehot[...]).astype(BF16)

    def body(i, _):
        pick(onehot_even, 2 * i)
        pick(onehot_odd, 2 * i + 1)
        return 0

    lax.fori_loop(0, blocks * quads // 2, body, 0)

    for copy in copies[1:]:
        copy.wait()
    hi, lo = weight_halves(w1_ref[...].T)
    line = jnp.concatenate([hi, hi, lo, lo], axis=1)
    none = jnp.zeros_like(line)
    w1s[...] = jnp.concatenate(
        [jnp.concatenate([line, none], axis=1), jnp.concatenate([none, line], axis=1)], axis=0
    ).astype(BF16)
    w2s[...] = weight_rows(w2_ref[...].T)
    wrs[...] = weight_rows(wr_ref[...].T)
    wrt[...] = weight_rows(wr_ref[...])
    units = wo_ref.shape[1]
    one = lax.broadcasted_iota(jnp.int32, (units, units), 0)
    two = lax.broadcasted_iota(jnp.int32, (units, units), 1)
    woc[...] = jnp.sum(jnp.where(one == two, wo_ref[...], 0.0), axis=1, keepdims=True)


def pack_kernel(rows, cols, feat_hbm, pos_hbm, out, pos_ref, sems):
    feats = feat_hbm.shape[2]
    copies = copied(
        [pos_hbm] + [feat_hbm.at[r, c] for r in range(rows) for c in range(cols)],
        [pos_ref] + [out.at[r, c, pl.ds(0, feats)] for r in range(rows) for c in range(cols)],
        sems,
    )
    copies[0].wait()
    for r in range(rows):
        for c in range(cols):
            rest = jnp.concatenate([pos_ref[r, i, c : c + 1, :] for i in range(3)], axis=0)
            parts = []
            for _ in range(3):
                part = rest.astype(BF16).astype(F32)
                parts.append(part)
                rest = rest - part
            parts.append(jnp.zeros((7, LANES), F32))
            out[r, c, feats:] = jnp.concatenate(parts, axis=0).astype(BF16)
    for copy in copies[1:]:
        copy.wait()


def place_of(block, feats):
    rest = block[feats : feats + 16].astype(F32)
    return rest[0:3] + rest[3:6] + rest[6:9]


def ends_kernel(rows, left_ref, right_ref, up, down):
    for out, r in ((up, rows - 1), (down, 0)):
        out[:, :LANES] = left_ref[r, 0]
        out[:, LANES:] = right_ref[r, 0]


def local_kernel(
    rows,
    cols,
    prev_ref,
    next_ref,
    left_ref,
    right_ref,
    own_ref,
    near,
    place,
    xa,
    out,
    win,
    hot_even,
    hot_odd,
):
    blocks = rows * cols
    steps = near.shape[0]
    quads = steps // blocks
    feats = out.shape[1]

    def columns(r, c):
        found = []
        for k in range(3):
            row = r - 1 + k
            for col in (c - 1, c, c + 1):
                slot = 3 * k + col - c + 1
                if 0 <= row < rows and col != c:
                    if col < 0:
                        found.append((slot, left_ref[row, 0, :feats]))
                    elif col >= cols:
                        found.append((slot, right_ref[row, 0, :feats]))
                    else:
                        found.append((slot, own_ref[row, col, :feats]))
                elif not 0 <= row < rows and 0 <= col < cols:
                    ref = prev_ref if row < 0 else next_ref
                    found.append((slot, ref[0, col, :feats]))
        return found

    for b in range(blocks):
        found = columns(b // cols, b % cols)
        count = len(found)
        for k, (_, block) in enumerate(found):
            win[b, :, k * LANES : (k + 1) * LANES] = block

        def pick(hot, step):
            first = (step % quads) * QUAD
            parts = window_hot(near[step], lines(place, b, first, QUAD), [x for x, _ in found])
            for k in range(count):
                hot[k * LANES : (k + 1) * LANES, :] = parts[k]
            picked = dot(win[b, :, : count * LANES], hot[: count * LANES, :])
            out[step] = xa[step] + picked.astype(BF16)

        def body(i, _):
            pick(hot_even, b * quads + 2 * i)
            pick(hot_odd, b * quads + 2 * i + 1)
            return 0

        lax.fori_loop(0, quads // 2, body, 0)


RING = 3


def energy_kernel(
    rows,
    cols,
    channels,
    slots,
    prev_ref,
    next_ref,
    prev_own_ref,
    next_own_ref,
    own_ref,
    left_ref,
    right_ref,
    codes_hbm,
    counts_hbm,
    near,
    w1s,
    w2s,
    wrs,
    wrt,
    woc,
    xl_hbm,
    en_ref,
    fleft_ref,
    fown_ref,
    fright_ref,
    force_ref,
    pos_ref,
    codes_ref,
    counts_ref,
    geo,
    har,
    win,
    xl,
    xg_even,
    xg_odd,
    w_even,
    w_odd,
    d_even,
    d_odd,
    acc,
    inv,
    dys,
    lhs,
    sems,
    xsem,
    *,
    stream,
):
    blocks = rows * cols
    quads = slots // QUAD
    steps = blocks * quads
    wide = QUAD * LANES
    group = 8
    feats = 9 * channels
    root3, root5, root15 = math.sqrt(3.0), math.sqrt(5.0), math.sqrt(15.0)
    even, odd = (xg_even, w_even, d_even), (xg_odd, w_odd, d_odd)

    def x_copy(step):
        at = step % RING
        return pltpu.make_async_copy(xl_hbm.at[step], xl.at[at], xsem.at[at])

    copies = copied([codes_hbm, counts_hbm], [codes_ref, counts_ref], sems)
    if stream:
        for i in range(RING):
            x_copy(i).start()

    for side, middle, r in ((prev_ref, prev_own_ref, 0), (next_ref, next_own_ref, rows + 1)):
        pos_ref[r, 0] = place_of(side[:, :LANES], feats)
        pos_ref[r, cols + 1] = place_of(side[:, LANES:], feats)
        for c in range(cols):
            pos_ref[r, c + 1] = place_of(middle[0, c], feats)
    for r in range(rows):
        pos_ref[r + 1, 0] = place_of(left_ref[r, 0], feats)
        pos_ref[r + 1, cols + 1] = place_of(right_ref[r, 0], feats)
        for c in range(cols):
            pos_ref[r + 1, c + 1] = place_of(own_ref[r, c], feats)
            none = jnp.zeros((feats, LANES), BF16)
            ref = prev_ref if r == 0 else next_ref
            ends = r == 0 or r == rows - 1
            b = r * cols + c
            win[b, :, :LANES] = ref[:feats, :LANES] if ends and c == 0 else none
            win[b, :, LANES:] = ref[:feats, LANES:] if ends and c == cols - 1 else none
    acc[...] = jnp.zeros(acc.shape, F32)
    for copy in copies:
        copy.wait()

    def geometry(b, _):
        r, c = b // cols, b % cols
        zq, near_block, atom = decoded(codes_ref[r, c])
        row3 = (near_block >= 3).astype(jnp.int32) + (near_block >= 6).astype(jnp.int32)
        shift_x = (row3 - 1).astype(F32) * BLOCK_LENGTH
        shift_y = (near_block - 3 * row3 - 1).astype(F32) * BLOCK_LENGTH
        shift_z = (zq - 1).astype(F32) * BLOCK_LENGTH
        centre = pos_ref[r + 1, c + 1]
        found = [jnp.zeros((slots, LANES), F32) for _ in range(3)]
        for k in range(9):
            place = pos_ref[r + k // 3, c + k % 3]
            here = near_block == k
            for i in range(3):
                line = jnp.broadcast_to(place[i : i + 1], (slots, LANES))
                value = jnp.take_along_axis(line, atom, axis=1, mode="promise_in_bounds")
                found[i] = jnp.where(here, value, found[i])
        rx = found[0] + shift_x - centre[0:1]
        ry = found[1] + shift_y - centre[1:2]
        rz = found[2] + shift_z - centre[2:3]
        dist = jnp.sqrt(rx * rx + ry * ry + rz * rz)
        recip = 1.0 / dist
        ux, uy, uz = rx * recip, ry * recip, rz * recip
        x = dist * (1.0 / CUTOFF_RADIUS)
        x2 = x * x
        x5 = x2 * x2 * x
        live = lax.broadcasted_iota(jnp.int32, (slots, LANES), 0) < counts_ref[r, c]
        scale = jnp.where(live, 1.0 / slots, 0.0)
        env = (1.0 - x5 * x * (28.0 - x * (48.0 - 21.0 * x))) * scale
        denv = (-168.0 / CUTOFF_RADIUS) * x5 * (1.0 - x * (2.0 - x)) * scale
        geo[b, 0] = dist
        geo[b, 1] = recip
        geo[b, 2] = env
        geo[b, 3] = denv
        geo[b, 4] = ux
        geo[b, 5] = uy
        geo[b, 6] = uz
        geo[b, 7] = near_block.astype(F32)
        har[b, 0] = root3 * ux
        har[b, 1] = root3 * uy
        har[b, 2] = root3 * uz
        har[b, 3] = root15 * ux * uy
        har[b, 4] = root15 * uy * uz
        har[b, 5] = 0.5 * root5 * (3.0 * uz * uz - 1.0)
        har[b, 6] = root15 * ux * uz
        har[b, 7] = 0.5 * root15 * (ux * ux - uy * uy)
        return 0

    lax.fori_loop(0, blocks, geometry, 0)

    def network(buffers, step):
        _, wsc, dsc = buffers
        b, first = step // quads, (step % quads) * QUAD
        dist, recip, env, denv = [joined(geo, b, k, first, QUAD) for k in range(4)]
        order = (lax.broadcasted_iota(jnp.int32, (8, wide), 0) + 1).astype(F32)
        sin, cos = sin_cos_half_turns(order * (dist * (1.0 / CUTOFF_RADIUS)))
        norm = math.sqrt(2.0 / CUTOFF_RADIUS)
        basis = norm * sin * recip
        slope = ((norm * math.pi / CUTOFF_RADIUS) * order * cos - basis) * recip
        split = []
        for x in (basis, slope):
            hi = x.astype(BF16).astype(F32)
            split += [hi, x - hi] * 2
        pre2 = dot(w1s[...], jnp.concatenate(split, axis=0).astype(BF16))
        pre, dpre = pre2[: pre2.shape[0] // 2], pre2[pre2.shape[0] // 2 :]
        gate = 1.0 / (1.0 + jnp.exp(-pre))
        h = pre * gate
        dh = gate + h * (1.0 - gate)
        wsc[step // 2] = dot(w2s[...], value_rows(h * env))
        dsc[step // 2] = dot(w2s[...], value_rows(dh * dpre * env + h * denv))

    def gather(buffers, step):
        b, first = step // quads, (step % quads) * QUAD
        r = b // cols
        k0 = jnp.where(r == 0, 0, jnp.where(r == rows - 1, 6, 9))
        parts = window_hot(near[step], joined(geo, b, 7, first, QUAD), [k0, k0 + 2])
        if stream:
            x_copy(step).wait()
            held = xl[step % RING]
        else:
            held = xl_hbm[step]
        buffers[0][step // 2] = held.astype(F32) + dot(win[b], jnp.concatenate(parts, axis=0))

    def collect(buffers, step):
        xg, wsc, _ = buffers
        b, first = step // quads, (step % quads) * QUAD
        for g in range(channels // group):
            at = g * group
            total = [acc[b, m, at : at + group, :] for m in range(9)]
            for s in range(QUAD):
                ln = slice(s * LANES, (s + 1) * LANES)
                xs = [
                    xg[step // 2, m * channels + at : m * channels + at + group, ln]
                    for m in range(9)
                ]
                w0, w1, w2 = [
                    wsc[step // 2, k * channels + at : k * channels + at + group, ln]
                    for k in range(3)
                ]
                ys = [har[b, m, pl.ds(first + s, 1), :] for m in range(8)]
                t0 = w0 * xs[0]
                vec = xs[1] * ys[0] + xs[2] * ys[1] + xs[3] * ys[2]
                total[0] = total[0] + (t0 + w1 * xs[0]) + w2 * vec
                for m in range(1, 9):
                    total[m] = total[m] + (t0 * ys[m - 1] + w1 * xs[m])
            for m in range(9):
                acc[b, m, at : at + group, :] = total[m]

    def advance(new, old, step):
        gather(new, step)
        network(new, step)
        collect(old, step - 1)
        if stream:

            @pl.when(step + RING - 1 < steps)
            def _():
                x_copy(step + RING - 1).start()

    def forward(i, _):
        advance(even, odd, 2 * i)
        advance(odd, even, 2 * i + 1)
        return 0

    gather(even, 0)
    network(even, 0)
    advance(odd, even, 1)
    lax.fori_loop(1, steps // 2, forward, 0)
    collect(odd, steps - 1)

    for b in range(blocks):
        ln = slice(b * LANES, (b + 1) * LANES)
        a = [acc[b, m] for m in range(9)]
        inv[0:channels, ln] = a[0] * a[0]
        inv[channels : 2 * channels, ln] = a[1] * a[1] + a[2] * a[2] + a[3] * a[3]
        inv[2 * channels :, ln] = (
            a[4] * a[4] + a[5] * a[5] + a[6] * a[6] + a[7] * a[7] + a[8] * a[8]
        )
    z = dot(wrs[...], value_rows(inv[...]))
    gate = 1.0 / (1.0 + jnp.exp(-z))
    out = z * gate
    wo = woc[...]
    energy = jnp.sum(out * wo, axis=0, keepdims=True)
    dinv = dot(wrt[...], value_rows(wo * (gate + out * (1.0 - gate))))
    for b in range(blocks):
        ln = slice(b * LANES, (b + 1) * LANES)
        en_ref[b // cols, b % cols] = energy[:, ln]
        for m in range(9):
            part = 0 if m == 0 else (1 if m < 4 else 2)
            d = dinv[part * channels : (part + 1) * channels, ln]
            acc[b, m] = 2.0 * acc[b, m] * d

    def edge_terms(buffers, step):
        xg, wsc, dsc = buffers
        b, first = step // quads, (step % quads) * QUAD
        for s in range(QUAD):
            ln = slice(s * LANES, (s + 1) * LANES)
            ys = [har[b, m, pl.ds(first + s, 1), :] for m in range(8)]
            dy = [jnp.zeros((group, LANES), F32) for _ in range(9)]
            for g in range(channels // group):
                at = g * group
                xs = [
                    xg[step // 2, m * channels + at : m * channels + at + group, ln]
                    for m in range(9)
                ]
                gs = [acc[b, m, at : at + group, :] for m in range(9)]
                w0 = wsc[step // 2, at : at + group, ln]
                w2 = wsc[step // 2, 2 * channels + at : 2 * channels + at + group, ln]
                d0, d1, d2 = [
                    dsc[step // 2, k * channels + at : k * channels + at + group, ln]
                    for k in range(3)
                ]
                t0 = w0 * xs[0]
                t2 = w2 * gs[0]
                vec = xs[1] * ys[0] + xs[2] * ys[1] + xs[3] * ys[2]
                along = gs[0]
                direct = gs[0] * xs[0]
                for m in range(1, 9):
                    along = along + gs[m] * ys[m - 1]
                    direct = direct + gs[m] * xs[m]
                    dy[m - 1] = dy[m - 1] + t0 * gs[m]
                    if m < 4:
                        dy[m - 1] = dy[m - 1] + t2 * xs[m]
                dy[8] = dy[8] + (d0 * xs[0] * along + d1 * direct + d2 * gs[0] * vec)
            for m in range(9):
                dys[b, m, pl.ds(first + s, 1), :] = jnp.sum(dy[m], axis=0, keepdims=True)

    def backward(i, _):
        edge_terms(even, 2 * i)
        edge_terms(odd, 2 * i + 1)
        return 0

    lax.fori_loop(0, steps // 2, backward, 0)
    force_ref[...] = jnp.zeros(force_ref.shape, F32)

    def pull(b, _):
        r, c = b // cols, b % cols
        ux, uy, uz, recip = geo[b, 4], geo[b, 5], geo[b, 6], geo[b, 1]
        d1, d2, d3, d4, d5, d6, d7, d8 = [dys[b, m] for m in range(8)]
        gx = root3 * d1 + root15 * (uy * d4 + uz * d7 + ux * d8)
        gy = root3 * d2 + root15 * (ux * d4 + uz * d5 - uy * d8)
        gz = root3 * d3 + root15 * (uy * d5 + ux * d7) + (3.0 * root5) * uz * d6
        radial = dys[b, 8] - (ux * gx + uy * gy + uz * gz) * recip
        grads = [gx * recip + ux * radial, gy * recip + uy * radial, gz * recip + uz * radial]
        for i in range(3):
            here = jnp.sum(grads[i], axis=0, keepdims=True)
            force_ref[r + 1, c + 1, i : i + 1, :] += here
        split = [halves(g) for g in grads]
        which = lax.broadcasted_iota(jnp.int32, (16, LANES), 0).astype(F32)
        place = geo[b, 7]
        for n in range(slots):
            ln = slice(n * LANES, (n + 1) * LANES)
            hit = which == place[n : n + 1]
            for i in range(3):
                for v in range(2):
                    line = split[i][v][n : n + 1].astype(F32)
                    at = (3 * v + i) * 16
                    lhs[at : at + 16, ln] = jnp.where(hit, line, 0.0).astype(BF16)
        total = jnp.zeros((96, LANES), F32)
        for p in range(quads):
            total = total + lax.dot_general(
                lhs[:, p * wide : (p + 1) * wide],
                near[b * quads + p],
                (((1,), (1,)), ((), ())),
                preferred_element_type=F32,
            )
        for i in range(3):
            for k in range(9):
                at = i * 16 + k
                value = total[at : at + 1] + total[48 + at : 49 + at]
                force_ref[r + k // 3, c + k % 3, i : i + 1, :] -= value
        return 0

    lax.fori_loop(0, blocks, pull, 0)
    for r in range(rows + 2):
        for i in range(3):
            fleft_ref[r, i] = force_ref[r, 0:1, i, :]
            fright_ref[r, i] = force_ref[r, cols + 1 :, i, :]
            fown_ref[r, i] = force_ref[r, 1 : cols + 1, i, :]


def vmem_call(body, name, ins, out_shape, scratch, limit, flops):
    vmem = pl.BlockSpec(memory_space=pltpu.VMEM)
    return pl.pallas_call(
        body,
        out_shape=out_shape,
        in_specs=ins,
        out_specs=[vmem] * len(out_shape),
        scratch_shapes=scratch,
        compiler_params=pltpu.CompilerParams(vmem_limit_bytes=limit * 1024 * 1024),
        cost_estimate=pl.CostEstimate(flops=flops, bytes_accessed=1024 * 1024, transcendentals=0),
        name=name,
    )


def pinned(*args):
    return [pltpu.with_memory_space_constraint(x, pltpu.HBM) for x in args]


def prepare_part(own, feats, neighbours, w_first, w_second, w_read, w_out):
    rows, cols, slots = neighbours.shape[0], neighbours.shape[1], neighbours.shape[2]
    hidden, basis = w_first.shape
    units, reads = w_read.shape
    weights = w_second.shape[0]
    blocks, steps, wide = rows * cols, rows * cols * slots // QUAD, QUAD * LANES
    spans = min(rows, 3)
    vmem = pl.BlockSpec(memory_space=pltpu.VMEM)
    hbm = pl.BlockSpec(memory_space=pltpu.HBM)
    sds = jax.ShapeDtypeStruct
    call = vmem_call(
        functools.partial(prepare_kernel, rows, cols, slots),
        "prepare",
        [vmem] + [hbm] * 5,
        [
            sds((steps, LANES, wide), BF16),
            sds((blocks, slots, LANES), F32),
            sds((2 * hidden, 8 * basis), BF16),
            sds((weights, 3 * hidden), BF16),
            sds((units, 3 * reads), BF16),
            sds((reads, 3 * units), BF16),
            sds((units, 1), F32),
            sds((steps, feats, wide), BF16),
        ],
        [
            pltpu.VMEM(neighbours.shape, jnp.int32),
            pltpu.VMEM((basis, hidden), F32),
            pltpu.VMEM((hidden, weights), F32),
            pltpu.VMEM((reads, units), F32),
            pltpu.VMEM((1, units), F32),
            pltpu.VMEM((blocks, slots, LANES), F32),
            pltpu.VMEM((blocks, feats, spans * LANES), BF16),
            pltpu.VMEM((spans * LANES, wide), BF16),
            pltpu.VMEM((spans * LANES, wide), BF16),
            pltpu.SemaphoreType.DMA((5,)),
        ],
        16,
        2 * feats * spans * LANES * steps * wide,
    )
    return call(
        own, *pinned(neighbours, w_first.T, w_second.T, w_read.T, w_out.reshape(1, units))
    )


def pack_part(features, pos):
    rows, cols, feats, _ = features.shape
    vmem = pl.BlockSpec(memory_space=pltpu.VMEM)
    hbm = pl.BlockSpec(memory_space=pltpu.HBM)
    call = vmem_call(
        functools.partial(pack_kernel, rows, cols),
        "pack",
        [hbm] * 2,
        [jax.ShapeDtypeStruct((rows, cols, feats + 16, LANES), BF16)],
        [pltpu.VMEM(pos.shape, F32), pltpu.SemaphoreType.DMA((1 + rows * cols,))],
        2,
        1000000,
    )
    return call(*pinned(features, pos))[0]


def ends_part(left, right):
    vmem = pl.BlockSpec(memory_space=pltpu.VMEM)
    message = jax.ShapeDtypeStruct((left.shape[2], 2 * LANES), BF16)
    call = vmem_call(
        functools.partial(ends_kernel, left.shape[0]),
        "ends",
        [vmem] * 2,
        [message] * 2,
        [],
        2,
        1000000,
    )
    return call(left, right)


def local_part(before, after, left, right, own, near, place, xa):
    rows, cols, feats = own.shape[0], own.shape[1], xa.shape[1]
    steps, _, wide = near.shape
    most = 5 if rows == 2 else 6
    vmem = pl.BlockSpec(memory_space=pltpu.VMEM)
    call = vmem_call(
        functools.partial(local_kernel, rows, cols),
        "local",
        [vmem] * 8,
        [jax.ShapeDtypeStruct((steps, feats, wide), BF16)],
        [
            pltpu.VMEM((rows * cols, feats, most * LANES), BF16),
            pltpu.VMEM((most * LANES, wide), BF16),
            pltpu.VMEM((most * LANES, wide), BF16),
        ],
        16,
        2 * feats * most * LANES * steps * wide,
    )
    return call(before, after, left, right, own, near, place, xa)[0]


def energy_part(ghosts, own, left, right, neighbours, counts, prepared, gathered):
    near, place, w1s, w2s, wrs, wrt, woc = prepared[:7]
    rows, cols, slots = neighbours.shape[0], neighbours.shape[1], neighbours.shape[2]
    steps, _, wide = near.shape
    weights = w2s.shape[0]
    channels, blocks, feats = weights // 3, rows * cols, gathered.shape[1]
    vmem = pl.BlockSpec(memory_space=pltpu.VMEM)
    hbm = pl.BlockSpec(memory_space=pltpu.HBM)
    sds = jax.ShapeDtypeStruct
    side = sds((rows + 2, 3, 1, LANES), F32)
    stream = blocks > 2
    half = steps // 2
    call = vmem_call(
        functools.partial(energy_kernel, rows, cols, channels, slots, stream=stream),
        "energy",
        [vmem] * 7 + [hbm] * 2 + [vmem] * 6 + [hbm if stream else vmem],
        [sds((rows, cols, 1, LANES), F32), side, sds((rows + 2, 3, cols, LANES), F32), side],
        [
            pltpu.VMEM((rows + 2, cols + 2, 3, LANES), F32),
            pltpu.VMEM((rows + 2, cols + 2, 3, LANES), F32),
            pltpu.VMEM((rows, cols, slots, LANES), jnp.int32),
            pltpu.VMEM((rows, cols, 1, LANES), jnp.int32),
            pltpu.VMEM((blocks, 8, slots, LANES), F32),
            pltpu.VMEM((blocks, 8, slots, LANES), F32),
            pltpu.VMEM((blocks, feats, 2 * LANES), BF16),
            pltpu.VMEM((RING, feats, wide) if stream else (1, 16, LANES), BF16),
            pltpu.VMEM((half, feats, wide), F32),
            pltpu.VMEM((half, feats, wide), F32),
            pltpu.VMEM((half, weights, wide), F32),
            pltpu.VMEM((half, weights, wide), F32),
            pltpu.VMEM((half, weights, wide), F32),
            pltpu.VMEM((half, weights, wide), F32),
            pltpu.VMEM((blocks, 9, channels, LANES), F32),
            pltpu.VMEM((weights, blocks * LANES), F32),
            pltpu.VMEM((blocks, 9, slots, LANES), F32),
            pltpu.VMEM((96, slots * LANES), BF16),
            pltpu.SemaphoreType.DMA((2,)),
            pltpu.SemaphoreType.DMA((RING,)),
        ],
        56 if stream else 32,
        2 * feats * 9 * LANES * steps * wide,
    )
    energies, f_left, f_own, f_right = call(
        *ghosts,
        own,
        left,
        right,
        *pinned(neighbours, counts.reshape(rows, cols, 1, LANES)),
        near,
        w1s,
        w2s,
        wrs,
        wrt,
        woc,
        gathered,
    )
    return f_left, f_own, f_right, energies.reshape(rows, cols, LANES)


def local(
    positions,
    velocities,
    features,
    neighbours,
    counts,
    w_first,
    w_second,
    w_read,
    w_out,
    fresh_positions,
    fresh_velocities,
):
    nrows, ncols = (positions.shape[0], positions.shape[1])
    shock_place = lax.axis_index("shock")
    front = lax.axis_size("shock") - 1
    assert nrows >= 2 and neighbours.shape[2] % (2 * QUAD) == 0

    def sides(x, axis):
        last = lax.slice_in_dim(x, ncols - 1, ncols, axis=axis)
        first = lax.slice_in_dim(x, 0, 1, axis=axis)
        return shifted(last, "trans", 1), shifted(first, "trans", -1)

    pos = positions.transpose(0, 2, 1, 3)
    vel = velocities.transpose(0, 2, 1, 3)
    own = pack_part(features, pos)
    left, right = sides(own, 1)
    before = passed_along(own[nrows - 1 :], "shock", 1)
    after = passed_along(own[:1], "shock", -1)
    feats = features.shape[2]
    prepared = prepare_part(own, feats, neighbours, w_first, w_second, w_read, w_out)
    near, place, xa = prepared[0], prepared[1], prepared[7]
    left, right, near = lax.optimization_barrier((left, right, near))
    last, first = ends_part(left, right)
    ghosts = (
        passed_along(last, "shock", 1),
        passed_along(first, "shock", -1),
        before,
        after,
    )
    gathered = local_part(before, after, left, right, own, near, place, xa)
    f_left, f_own, f_right, energies = energy_part(
        ghosts, own, left, right, neighbours, counts, prepared, gathered
    )
    from_right = shifted(f_left, "trans", -1)
    from_left = shifted(f_right, "trans", 1)
    folded = f_own.at[:, :, ncols - 1].add(from_right[:, :, 0])
    folded = folded.at[:, :, 0].add(from_left[:, :, 0])
    packed = jnp.concatenate([folded[:2], vel[:1], pos[:1]], axis=0)
    ahead = passed_along(packed, "shock", -1)
    force = folded[2 : nrows + 2]
    force = jnp.concatenate([force[: nrows - 2], force[nrows - 2 :] + ahead[:2]], axis=0)
    old_vel = jnp.concatenate([vel[1:], ahead[2:3]], axis=0)
    old_pos = jnp.concatenate([pos[1:], ahead[3:4]], axis=0)
    new_vel = old_vel + KICK_FACTOR * force
    moved = old_pos + MOVE_FACTOR * new_vel
    at_front = shock_place == front
    last_pos = jnp.where(at_front, fresh_positions.transpose(1, 0, 2), moved[nrows - 1])
    last_vel = jnp.where(at_front, fresh_velocities.transpose(1, 0, 2), new_vel[nrows - 1])
    new_positions = jnp.concatenate([moved[: nrows - 1], last_pos[None]], axis=0)
    new_velocities = jnp.concatenate([new_vel[: nrows - 1], last_vel[None]], axis=0)
    return (energies, new_positions.transpose(0, 2, 1, 3), new_velocities.transpose(0, 2, 1, 3))


def solution(mesh):
    return jax.shard_map(
        local,
        mesh=mesh,
        in_specs=(
            P("shock", "trans", None, None),
            P("shock", "trans", None, None),
            P("shock", "trans", None, None),
            P("shock", "trans", None, None),
            P("shock", "trans", None),
            P(),
            P(),
            P(),
            P(),
            P("trans", None, None),
            P("trans", None, None),
        ),
        out_specs=(
            P("shock", "trans", None),
            P("shock", "trans", None, None),
            P("shock", "trans", None, None),
        ),
        check_vma=False,
    )
```

time: 74.4 us -> 63 us (0.85)
  local copies, waits for them, and re-layouts: 6.95 us -> 0.74 us
  starting transfers between devices: 23.2 us -> 21.4 us
  Pallas kernels: 30.4 us -> 28.8 us
  waiting for transfers between devices: 10.8 us -> 9.65 us
    unnamed x22 -> x6, local copies, waits for them, and re-layouts: 5.19 us -> 0.01 us
    ppermute x5, waiting for transfers between devices: 6.82 us -> 3.5 us  [passed_along(): return lax.ppermute(block, axis, route)]
    ppermute x6 -> x4, starting transfers between devices: 8.22 us -> 5.53 us  [shifted(): return lax.ppermute(x, axis, [(i, (i + by) % count) for i in range(count)])]
    ppermute x6 -> x4, waiting for transfers between devices: 3.96 us -> 6.15 us  [shifted(): return lax.ppermute(x, axis, [(i, (i + by) % count) for i in range(count)])]
    pallas_call x3 -> x5, Pallas kernels: 30.4 us -> 28.8 us  [the longest x1 16.7 us: energy_part(): call(*ghosts, own, left, right, *pinned(neighbours, counts.reshape(rows,...]
    slice x5 -> x2, local copies, waits for them, and re-layouts: 1.75 us -> 0.72 us  [the longest x1 0.7 us: local(): old_pos = jnp.concatenate([pos[1:], ahead[3:4]], axis=0)]
    ppermute x5, starting transfers between devices: 15 us -> 15.9 us  [passed_along(): return lax.ppermute(block, axis, route)]
  transfers between devices with their start and end apart: 11 -> 9, of which waited for: 4 -> 5; matrix products, arithmetic and copies ran while one was open for 2% -> 1% of each run, Pallas kernels for 20% -> 18%
where the time goes in v4:
time: 63 us; the launch traced here: 62.6 us
  Pallas kernels  28.8 us (46%)
  starting transfers between devices  21.4 us (34%)
  waiting for transfers between devices  9.65 us (15%)
  other arithmetic  1.21 us (2%)
  between operations  0.8 us (1%)
  local copies, waits for them, and re-layouts  0.74 us (1%)
    pallas_call x1, Pallas kernels, energy_part(): call(*ghosts, own, left, right, *pinned(neighbours, counts.reshape(rows,...  16.7 us
    ppermute x5, starting transfers between devices, passed_along(): return lax.ppermute(block, axis, route)  15.9 us
    pallas_call x1, Pallas kernels, local_part(): return call(before, after, left, right, own, near, place, xa)[0]  6.85 us
    ppermute x4, waiting for transfers between devices, shifted(): return lax.ppermute(x, axis, [(i, (i + by) % count) for i in range(count)])  6.15 us
    ppermute x4, starting transfers between devices, shifted(): return lax.ppermute(x, axis, [(i, (i + by) % count) for i in range(count)])  5.53 us
    pallas_call x1, Pallas kernels, prepare_part(): call(own, *pinned(neighbours, w_first.T, w_second.T, w_read.T, w_out.resh...  4.21 us
    ppermute x5, waiting for transfers between devices, passed_along(): return lax.ppermute(block, axis, route)  3.5 us
  transfers between devices with their start and end apart: 9, of which 5 were waited for; matrix products, arithmetic and copies ran while one was open for 1% of the time, Pallas kernels for 18%

profile of v4, /device:TPU:3, one launch (start us, length us, event | category | flops | bytes accessed | tf_op | source)
XLA Modules:
  0.0 62.6 jit_solution(17513844227566331502)
XLA Ops:
  0.6 1.0 %pack.1.own_ref = bf16[2,1,592,128]{3,2,1,0:T(8,128)(2,1)S(1)} custom-call(bf16[2,1,576,128]{3,2,1,0:T(8,128)(2,1)} %feat_hbm.1, f32[2,3,1,128]{3,2,1,0:T(1,128)} %bitcast.33), custom_call_target="tpu_custom_call" | custom-call | flops 1000000 | bytes 1048576 | tf_op jit(solution)/shard_map/pack/pallas_call | solution.py:712
  1.7 1.3 %collective-permute-start = (bf16[2,1,592,128]{3,2,1,0:T(8,128)(2,1)S(1)}, bf16[2,1,592,128]{3,2,1,0:T(8,128)(2,1)S(1)}, u32[]{:S(2)}, u32[]{:S(2)}) collective-permute-start(bf16[2,1,592,128]{3,2,1,0:T(8,128)(2,1)S(1)} %pack.1.own_ref), channel_id=1, source_target_pairs={{0,1},{1,2},{2,3},{3,0},{4,5},{5,6},{6,7},{7,4},{8,9},{9,10},{10,1... | collective-permute-start | bytes 909320 | tf_op jit(solution)/shard_map/ppermute | solution.py:23
  3.0 2.1 %collective-permute-start.1 = (bf16[2,1,592,128]{3,2,1,0:T(8,128)(2,1)S(1)}, bf16[2,1,592,128]{3,2,1,0:T(8,128)(2,1)S(1)}, u32[]{:S(2)}, u32[]{:S(2)}) collective-permute-start(bf16[2,1,592,128]{3,2,1,0:T(8,128)(2,1)S(1)} %pack.1.own_ref), channel_id=1, source_target_pairs={{0,3},{1,0},{2,1},{3,2},{4,7},{5,4},{6,5},{7,6},{8,11},{9,8},{10,9... | collective-permute-start | bytes 909320 | tf_op jit(solution)/shard_map/ppermute | solution.py:23
  5.1 4.1 %collective-permute-start.4 = (bf16[1,1,592,128]{3,2,1,0:T(8,128)(2,1)S(1)}, bf16[1,1,592,128]{3,2,1,0:T(8,128)(2,1)S(1)}, u32[]{:S(2)}, u32[]{:S(2)}) collective-permute-start(bf16[1,1,592,128]{3,2,1,0:T(8,128)(2,1)S(1)} %get-tuple-element.67), channel_id=1, source_target_pairs={{0,4},{4,8},{8,12},{12,16},{16,20},{20,24},{24,28},{1,5},{5,9},{9,... | collective-permute-start | bytes 454664 | tf_op jit(solution)/shard_map/ppermute | solution.py:29
  9.3 1.9 %collective-permute-start.5 = (bf16[1,1,592,128]{3,2,1,0:T(8,128)(2,1)S(1)}, bf16[1,1,592,128]{3,2,1,0:T(8,128)(2,1)S(1)}, u32[]{:S(2)}, u32[]{:S(2)}) collective-permute-start(bf16[1,1,592,128]{3,2,1,0:T(8,128)(2,1)S(1)} %get-tuple-element.66), channel_id=1, source_target_pairs={{4,0},{8,4},{12,8},{16,12},{20,16},{24,20},{28,24},{5,1},{9,5},{13... | collective-permute-start | bytes 454664 | tf_op jit(solution)/shard_map/ppermute | solution.py:29
  11.2 0.7 %slice_bitcast_fusion.3 = (f32[1,3,1,128]{3,2,1,0:T(1,128)S(1)}, f32[1,3,1,128]{3,2,1,0:T(1,128)S(1)}) fusion(f32[2,1,3,128]{3,1,2,0:T(1,128)} %param.15), kind=kLoop, calls=%fused_computation.13 | loop fusion | bytes 6144 | tf_op jit(solution)/shard_map/slice | solution.py:863
  11.9 4.2 %prepare.1 = (bf16[12,128,512]{2,1,0:T(8,128)(2,1)S(1)}, f32[2,24,128]{2,1,0:T(8,128)S(1)}, bf16[128,64]{1,0:T(8,128)(2,1)S(1)}, bf16[192,192]{1,0:T(8,128)(2,1)...) custom-call(bf16[2,1,592,128]{3,2,1,0:T(8,128)(2,1)S(1)} %pack.1.own, ...), custom_call_target="tpu_custom_call" | custom-call | flops 1811939328 | bytes 1048576 | tf_op jit(solution)/shard_map/prepare/pallas_call | solution.py:694
  16.1 0.0 collective-permute-done.left_ref
  16.1 1.9 %collective-permute-done.1.right_ref = bf16[2,1,592,128]{3,2,1,0:T(8,128)(2,1)S(1)} collective-permute-done((bf16[2,1,592,128]{3,2,1,0:T(8,128)(2,1)S(1)}, bf16[2,1,592,128]{3,2,1,0:T(8,128)(2,1)S(1)}, u32[]{:S(2)}, u32[]{:S(2)}) %collective-permute-start.1) | collective-permute-done | bytes 303136 | tf_op jit(solution)/shard_map/ppermute | solution.py:23
  18.0 0.1 ends.1
  18.1 4.1 %collective-permute-start.2 = (bf16[592,256]{1,0:T(8,128)(2,1)S(1)}, bf16[592,256]{1,0:T(8,128)(2,1)S(1)}, u32[]{:S(2)}, u32[]{:S(2)}) collective-permute-start(bf16[592,256]{1,0:T(8,128)(2,1)S(1)} %get-tuple-element.47), channel_id=1, source_target_pairs={{0,4},{4,8},{8,12},{12,16},{16,20},{20,24},{24,28},{1,5},{5,9},{9,... | collective-permute-start | bytes 909320 | tf_op jit(solution)/shard_map/ppermute | solution.py:29
  22.2 1.9 %collective-permute-start.3 = (bf16[592,256]{1,0:T(8,128)(2,1)S(1)}, bf16[592,256]{1,0:T(8,128)(2,1)S(1)}, u32[]{:S(2)}, u32[]{:S(2)}) collective-permute-start(bf16[592,256]{1,0:T(8,128)(2,1)S(1)} %get-tuple-element.48), channel_id=1, source_target_pairs={{4,0},{8,4},{12,8},{16,12},{20,16},{24,20},{28,24},{5,1},{9,5},{13... | collective-permute-start | bytes 909320 | tf_op jit(solution)/shard_map/ppermute | solution.py:29
  24.2 0.0 collective-permute-done.4.prev_ref.prev_own_ref
  24.2 0.0 collective-permute-done.5.next_ref.next_own_ref
  24.2 6.9 %local.1.xl_hbm = bf16[12,576,512]{2,1,0:T(8,128)(2,1)S(1)} custom-call(bf16[1,1,592,128]{3,2,1,0:T(8,128)(2,1)S(1)} %collective-permute-done.4.prev_ref.prev_own_ref, bf16[1,1,592,128]{3,2,1,0:T(8,128)(2,1)S(1)} %collective-permute-done.5.next_ref.next_own_ref, bf16[2,1,592,128]{3,2,1,0:T(8,128)(2,1)S(1)} %collective-permute-done.left_ref, ...), custom_call_target="tpu_custom_call" | custom-call | flops 4529848320 | bytes 1048576 | tf_op jit(solution)/shard_map/local/pallas_call | solution.py:748
  31.0 0.0 collective-permute-done.2.prev_ref
  31.0 0.2 collective-permute-done.3.next_ref
  31.3 0.0 copy-start
  31.3 0.0 copy-start.1
  31.3 0.0 copy-start.2
  31.3 16.7 %energy.1 = (f32[2,1,1,128]{3,2,1,0:T(1,128)}, f32[4,3,1,128]{3,2,1,0:T(1,128)S(1)}, f32[4,3,1,128]{3,2,1,0:T(1,128)S(1)}, f32[4,3,1,128]{3,2,1,0:T(1,128)S(1)}) custom-call(bf16[592,256]{1,0:T(8,128)(2,1)S(1)} %collective-permute-done.2.prev_ref, bf16[592,256]{1,0:T(8,128)(2,1)S(1)} %collective-permute-done.3.next_ref, ...), custom_call_target="tpu_custom_call" | custom-call | flops 8153726976 | bytes 1048576 | tf_op jit(solution)/shard_map/energy/pallas_call | solution.py:793
  47.9 2.1 %collective-permute-start.6 = (f32[4,3,1,128]{3,2,1,0:T(1,128)S(1)}, f32[4,3,1,128]{3,2,1,0:T(1,128)S(1)}, u32[]{:S(2)}, u32[]{:S(2)}) collective-permute-start(f32[4,3,1,128]{3,2,1,0:T(1,128)S(1)} %get-tuple-element.59), channel_id=1, source_target_pairs={{0,3},{1,0},{2,1},{3,2},{4,7},{5,4},{6,5},{7,6},{8,11},{9,8},{10,9... | collective-permute-start | bytes 18440 | tf_op jit(solution)/shard_map/ppermute | solution.py:23
  50.0 0.0 collective-permute-start.7
  50.0 0.0 copy-done
  50.0 0.8 %collective-permute-done.6 = f32[4,3,1,128]{3,2,1,0:T(1,128)S(1)} collective-permute-done((f32[4,3,1,128]{3,2,1,0:T(1,128)S(1)}, f32[4,3,1,128]{3,2,1,0:T(1,128)S(1)}, u32[]{:S(2)}, u32[]{:S(2)}) %collective-permute-start.6) | collective-permute-done | bytes 6176 | tf_op jit(solution)/shard_map/ppermute | solution.py:23
  50.8 3.5 %collective-permute-done.7 = f32[4,3,1,128]{3,2,1,0:T(1,128)S(1)} collective-permute-done((f32[4,3,1,128]{3,2,1,0:T(1,128)S(1)}, f32[4,3,1,128]{3,2,1,0:T(1,128)S(1)}, u32[]{:S(2)}, u32[]{:S(2)}) %collective-permute-start.7) | collective-permute-done | bytes 6176 | tf_op jit(solution)/shard_map/ppermute | solution.py:23
  54.3 3.8 %collective-permute-start.8 = (f32[4,3,1,128]{3,2,1,0:T(1,128)S(1)}, f32[4,3,1,128]{3,2,1,0:T(1,128)S(1)}, u32[]{:S(2)}, u32[]{:S(2)}) collective-permute-start(f32[4,3,1,128]{3,2,1,0:T(1,128)S(1)} %pad_maximum_fusion), channel_id=1, source_target_pairs={{4,0},{8,4},{12,8},{16,12},{20,16},{24,20},{28,24},{5,1},{9,5},{13... | collective-permute-start | bytes 18440 | tf_op jit(solution)/shard_map/ppermute | solution.py:29
  58.1 3.3 %collective-permute-done.8 = f32[4,3,1,128]{3,2,1,0:T(1,128)S(1)} collective-permute-done((f32[4,3,1,128]{3,2,1,0:T(1,128)S(1)}, f32[4,3,1,128]{3,2,1,0:T(1,128)S(1)}, u32[]{:S(2)}, u32[]{:S(2)}) %collective-permute-start.8) | collective-permute-done | bytes 6176 | tf_op jit(solution)/shard_map/ppermute | solution.py:29
  61.4 0.0 copy-done.1
  61.4 0.0 copy-done.2
  61.5 0.6 maximum_bitcast_fusion.1
  62.1 0.6 maximum_bitcast_fusion
  (8 shorter events, 0.1 us)
Async XLA Ops:
  1.7 14.4 %collective-permute-start = (bf16[2,1,592,128]{3,2,1,0:T(8,128)(2,1)S(1)}, bf16[2,1,592,128]{3,2,1,0:T(8,128)(2,1)S(1)}, u32[]{:S(2)}, u32[]{:S(2)}) collective-permute-start(bf16[2,1,592,128]{3,2,1,0:T(8,128)(2,1)S(1)} %pack.1.own_ref), channel_id=1, source_target_pairs={{0,1},{1,2},{2,3},{3,0},{4,5},{5,6},{6,7},{7,4},{8,9},{9,10},{10,1... | collective-permute-start | bytes 909320 | tf_op jit(solution)/shard_map/ppermute | solution.py:23
  3.0 15.0 %collective-permute-start.1 = (bf16[2,1,592,128]{3,2,1,0:T(8,128)(2,1)S(1)}, bf16[2,1,592,128]{3,2,1,0:T(8,128)(2,1)S(1)}, u32[]{:S(2)}, u32[]{:S(2)}) collective-permute-start(bf16[2,1,592,128]{3,2,1,0:T(8,128)(2,1)S(1)} %pack.1.own_ref), channel_id=1, source_target_pairs={{0,3},{1,0},{2,1},{3,2},{4,7},{5,4},{6,5},{7,6},{8,11},{9,8},{10,9... | collective-permute-start | bytes 909320 | tf_op jit(solution)/shard_map/ppermute | solution.py:23
  5.1 19.0 %collective-permute-start.4 = (bf16[1,1,592,128]{3,2,1,0:T(8,128)(2,1)S(1)}, bf16[1,1,592,128]{3,2,1,0:T(8,128)(2,1)S(1)}, u32[]{:S(2)}, u32[]{:S(2)}) collective-permute-start(bf16[1,1,592,128]{3,2,1,0:T(8,128)(2,1)S(1)} %get-tuple-element.67), channel_id=1, source_target_pairs={{0,4},{4,8},{8,12},{12,16},{16,20},{20,24},{24,28},{1,5},{5,9},{9,... | collective-permute-start | bytes 454664 | tf_op jit(solution)/shard_map/ppermute | solution.py:29
  9.3 14.9 %collective-permute-start.5 = (bf16[1,1,592,128]{3,2,1,0:T(8,128)(2,1)S(1)}, bf16[1,1,592,128]{3,2,1,0:T(8,128)(2,1)S(1)}, u32[]{:S(2)}, u32[]{:S(2)}) collective-permute-start(bf16[1,1,592,128]{3,2,1,0:T(8,128)(2,1)S(1)} %get-tuple-element.66), channel_id=1, source_target_pairs={{4,0},{8,4},{12,8},{16,12},{20,16},{24,20},{28,24},{5,1},{9,5},{13... | collective-permute-start | bytes 454664 | tf_op jit(solution)/shard_map/ppermute | solution.py:29
  18.1 12.9 %collective-permute-start.2 = (bf16[592,256]{1,0:T(8,128)(2,1)S(1)}, bf16[592,256]{1,0:T(8,128)(2,1)S(1)}, u32[]{:S(2)}, u32[]{:S(2)}) collective-permute-start(bf16[592,256]{1,0:T(8,128)(2,1)S(1)} %get-tuple-element.47), channel_id=1, source_target_pairs={{0,4},{4,8},{8,12},{12,16},{16,20},{20,24},{24,28},{1,5},{5,9},{9,... | collective-permute-start | bytes 909320 | tf_op jit(solution)/shard_map/ppermute | solution.py:29
  22.2 9.0 %collective-permute-start.3 = (bf16[592,256]{1,0:T(8,128)(2,1)S(1)}, bf16[592,256]{1,0:T(8,128)(2,1)S(1)}, u32[]{:S(2)}, u32[]{:S(2)}) collective-permute-start(bf16[592,256]{1,0:T(8,128)(2,1)S(1)} %get-tuple-element.48), channel_id=1, source_target_pairs={{4,0},{8,4},{12,8},{16,12},{20,16},{24,20},{28,24},{5,1},{9,5},{13... | collective-permute-start | bytes 909320 | tf_op jit(solution)/shard_map/ppermute | solution.py:29
  31.3 18.8 %copy-start = (f32[2,1,3,128]{3,1,2,0:T(1,128)S(1)}, f32[2,1,3,128]{3,1,2,0:T(1,128)}, u32[]{:S(2)}) copy-start(f32[2,1,3,128]{3,1,2,0:T(1,128)} %param.16) | copy-start | bytes 9220
  31.3 30.2 %copy-start.1 = (f32[1,3,128]{2,0,1:T(1,128)S(1)}, f32[1,3,128]{2,0,1:T(1,128)}, u32[]{:S(2)}) copy-start(f32[1,3,128]{2,0,1:T(1,128)} %param.25) | copy-start | bytes 4612
  31.3 30.2 %copy-start.2 = (f32[1,3,128]{2,0,1:T(1,128)S(1)}, f32[1,3,128]{2,0,1:T(1,128)}, u32[]{:S(2)}) copy-start(f32[1,3,128]{2,0,1:T(1,128)} %param.24) | copy-start | bytes 4612
  47.9 2.9 %collective-permute-start.6 = (f32[4,3,1,128]{3,2,1,0:T(1,128)S(1)}, f32[4,3,1,128]{3,2,1,0:T(1,128)S(1)}, u32[]{:S(2)}, u32[]{:S(2)}) collective-permute-start(f32[4,3,1,128]{3,2,1,0:T(1,128)S(1)} %get-tuple-element.59), channel_id=1, source_target_pairs={{0,3},{1,0},{2,1},{3,2},{4,7},{5,4},{6,5},{7,6},{8,11},{9,8},{10,9... | collective-permute-start | bytes 18440 | tf_op jit(solution)/shard_map/ppermute | solution.py:23
  50.0 4.3 %collective-permute-start.7 = (f32[4,3,1,128]{3,2,1,0:T(1,128)S(1)}, f32[4,3,1,128]{3,2,1,0:T(1,128)S(1)}, u32[]{:S(2)}, u32[]{:S(2)}) collective-permute-start(f32[4,3,1,128]{3,2,1,0:T(1,128)S(1)} %get-tuple-element.60), channel_id=1, source_target_pairs={{0,1},{1,2},{2,3},{3,0},{4,5},{5,6},{6,7},{7,4},{8,9},{9,10},{10,1... | collective-permute-start | bytes 18440 | tf_op jit(solution)/shard_map/ppermute | solution.py:23
  54.3 7.1 %collective-permute-start.8 = (f32[4,3,1,128]{3,2,1,0:T(1,128)S(1)}, f32[4,3,1,128]{3,2,1,0:T(1,128)S(1)}, u32[]{:S(2)}, u32[]{:S(2)}) collective-permute-start(f32[4,3,1,128]{3,2,1,0:T(1,128)S(1)} %pad_maximum_fusion), channel_id=1, source_target_pairs={{4,0},{8,4},{12,8},{16,12},{20,16},{24,20},{28,24},{5,1},{9,5},{13... | collective-permute-start | bytes 18440 | tf_op jit(solution)/shard_map/ppermute | solution.py:29

commit v5 on v4

--- a/solution.py
+++ b/solution.py
@@ -245,11 +245,52 @@
         out[:, LANES:] = right_ref[r, 0]
 
 
+def ghost_kernel(rows, cols, prev_ref, next_ref, near, place, xa, out):
+    steps = near.shape[0]
+    quads = steps // (rows * cols)
+    feats = out.shape[1]
+    for b in range(rows * cols):
+        r, c = b // cols, b % cols
+
+        def pick(step):
+            first = (step % quads) * QUAD
+            if r == 0 or r == rows - 1:
+                ref, slot = (prev_ref, 1) if r == 0 else (next_ref, 7)
+                hot = window_hot(near[step], lines(place, b, first, QUAD), [slot])[0]
+                out[step] = xa[step] + dot(ref[0, c, :feats], hot).astype(BF16)
+            else:
+                out[step] = xa[step]
+
+        def body(i, _):
+            pick(b * quads + 2 * i)
+            pick(b * quads + 2 * i + 1)
+            return 0
+
+        lax.fori_loop(0, quads // 2, body, 0)
+
+
+def finish_kernel(
+    rows, front_ref, force, ahead, vel, pos, fresh_pos, fresh_vel, new_pos, new_vel
+):
+    front = front_ref[0] == 1
+    for r in range(rows):
+        total = force[r + 2]
+        if r >= rows - 2:
+            total = total + ahead[r - rows + 2]
+        old_vel = vel[r + 1] if r < rows - 1 else ahead[2]
+        old_pos = pos[r + 1] if r < rows - 1 else ahead[3]
+        v = old_vel + KICK_FACTOR * total
+        p = old_pos + MOVE_FACTOR * v
+        if r == rows - 1:
+            v = jnp.where(front, fresh_vel[...], v)
+            p = jnp.where(front, fresh_pos[...], p)
+        new_vel[r] = v
+        new_pos[r] = p
+
+
 def local_kernel(
     rows,
     cols,
-    prev_ref,
-    next_ref,
     left_ref,
     right_ref,
     own_ref,
@@ -279,9 +320,6 @@
                         found.append((slot, right_ref[row, 0, :feats]))
                     else:
                         found.append((slot, own_ref[row, col, :feats]))
-                elif not 0 <= row < rows and 0 <= col < cols:
-                    ref = prev_ref if row < 0 else next_ref
-                    found.append((slot, ref[0, col, :feats]))
         return found
 
     for b in range(blocks):
@@ -348,6 +386,8 @@
     w_odd,
     d_even,
     d_odd,
+    held_even,
+    held_odd,
     acc,
     inv,
     dys,
@@ -364,7 +404,7 @@
     group = 8
     feats = 9 * channels
     root3, root5, root15 = math.sqrt(3.0), math.sqrt(5.0), math.sqrt(15.0)
-    even, odd = (xg_even, w_even, d_even), (xg_odd, w_odd, d_odd)
+    even, odd = (xg_even, w_even, d_even, held_even), (xg_odd, w_odd, d_odd, held_odd)
 
     def x_copy(step):
         at = step % RING
@@ -444,8 +484,8 @@
 
     lax.fori_loop(0, blocks, geometry, 0)
 
-    def network(buffers, step):
-        _, wsc, dsc = buffers
+    def hidden_rows(buffers, step):
+        held = buffers[3]
         b, first = step // quads, (step % quads) * QUAD
         dist, recip, env, denv = [joined(geo, b, k, first, QUAD) for k in range(4)]
         order = (lax.broadcasted_iota(jnp.int32, (8, wide), 0) + 1).astype(F32)
@@ -462,8 +502,13 @@
         gate = 1.0 / (1.0 + jnp.exp(-pre))
         h = pre * gate
         dh = gate + h * (1.0 - gate)
-        wsc[step // 2] = dot(w2s[...], value_rows(h * env))
-        dsc[step // 2] = dot(w2s[...], value_rows(dh * dpre * env + h * denv))
+        held[0] = value_rows(h * env)
+        held[1] = value_rows(dh * dpre * env + h * denv)
+
+    def radial_rows(buffers, step):
+        _, wsc, dsc, held = buffers
+        wsc[step // 2] = dot(w2s[...], held[0])
+        dsc[step // 2] = dot(w2s[...], held[1])
 
     def gather(buffers, step):
         b, first = step // quads, (step % quads) * QUAD
@@ -478,7 +523,7 @@
         buffers[0][step // 2] = held.astype(F32) + dot(win[b], jnp.concatenate(parts, axis=0))
 
     def collect(buffers, step):
-        xg, wsc, _ = buffers
+        xg, wsc = buffers[:2]
         b, first = step // quads, (step % quads) * QUAD
         for g in range(channels // group):
             at = g * group
@@ -502,10 +547,12 @@
             for m in range(9):
                 acc[b, m, at : at + group, :] = total[m]
 
-    def advance(new, old, step):
+    def advance(new, old, step, last=False):
+        radial_rows(new, step)
         gather(new, step)
-        network(new, step)
         collect(old, step - 1)
+        if not last:
+            hidden_rows(old, step + 1)
         if stream:
 
             @pl.when(step + RING - 1 < steps)
@@ -517,10 +564,14 @@
         advance(odd, even, 2 * i + 1)
         return 0
 
+    hidden_rows(even, 0)
+    hidden_rows(odd, 1)
+    radial_rows(even, 0)
     gather(even, 0)
-    network(even, 0)
     advance(odd, even, 1)
-    lax.fori_loop(1, steps // 2, forward, 0)
+    lax.fori_loop(1, steps // 2 - 1, forward, 0)
+    advance(even, odd, steps - 2)
+    advance(odd, even, steps - 1, last=True)
     collect(odd, steps - 1)
 
     for b in range(blocks):
@@ -546,7 +597,7 @@
             acc[b, m] = 2.0 * acc[b, m] * d
 
     def edge_terms(buffers, step):
-        xg, wsc, dsc = buffers
+        xg, wsc, dsc = buffers[:3]
         b, first = step // quads, (step % quads) * QUAD
         for s in range(QUAD):
             ln = slice(s * LANES, (s + 1) * LANES)
@@ -727,15 +778,45 @@
     return call(left, right)
 
 
-def local_part(before, after, left, right, own, near, place, xa):
+def ghost_part(before, after, near, place, xa, rows, cols):
+    vmem = pl.BlockSpec(memory_space=pltpu.VMEM)
+    steps, feats, wide = xa.shape
+    call = vmem_call(
+        functools.partial(ghost_kernel, rows, cols),
+        "ghost",
+        [vmem] * 5,
+        [jax.ShapeDtypeStruct(xa.shape, BF16)],
+        [],
+        8,
+        2 * feats * LANES * steps * wide,
+    )
+    return call(before, after, near, place, xa)[0]
+
+
+def finish_part(front, force, ahead, vel, pos, fresh_pos, fresh_vel):
+    vmem = pl.BlockSpec(memory_space=pltpu.VMEM)
+    smem = pl.BlockSpec(memory_space=pltpu.SMEM)
+    call = vmem_call(
+        functools.partial(finish_kernel, vel.shape[0]),
+        "finish",
+        [smem] + [vmem] * 6,
+        [jax.ShapeDtypeStruct(vel.shape, F32)] * 2,
+        [],
+        2,
+        100000,
+    )
+    return call(front, force, ahead, vel, pos, fresh_pos, fresh_vel)
+
+
+def local_part(left, right, own, near, place, xa):
     rows, cols, feats = own.shape[0], own.shape[1], xa.shape[1]
     steps, _, wide = near.shape
-    most = 5 if rows == 2 else 6
+    most = 2 * min(rows, 3)
     vmem = pl.BlockSpec(memory_space=pltpu.VMEM)
     call = vmem_call(
         functools.partial(local_kernel, rows, cols),
         "local",
-        [vmem] * 8,
+        [vmem] * 6,
         [jax.ShapeDtypeStruct((steps, feats, wide), BF16)],
         [
             pltpu.VMEM((rows * cols, feats, most * LANES), BF16),
@@ -745,7 +826,7 @@
         16,
         2 * feats * most * LANES * steps * wide,
     )
-    return call(before, after, left, right, own, near, place, xa)[0]
+    return call(left, right, own, near, place, xa)[0]
 
 
 def energy_part(ghosts, own, left, right, neighbours, counts, prepared, gathered):
@@ -780,6 +861,8 @@
             pltpu.VMEM((half, weights, wide), F32),
             pltpu.VMEM((half, weights, wide), F32),
             pltpu.VMEM((half, weights, wide), F32),
+            pltpu.VMEM((2, 3 * (w1s.shape[0] // 2), wide), BF16),
+            pltpu.VMEM((2, 3 * (w1s.shape[0] // 2), wide), BF16),
             pltpu.VMEM((blocks, 9, channels, LANES), F32),
             pltpu.VMEM((weights, blocks * LANES), F32),
             pltpu.VMEM((blocks, 9, slots, LANES), F32),
@@ -839,7 +922,8 @@
     feats = features.shape[2]
     prepared = prepare_part(own, feats, neighbours, w_first, w_second, w_read, w_out)
     near, place, xa = prepared[0], prepared[1], prepared[7]
-    left, right, near = lax.optimization_barrier((left, right, near))
+    xa = ghost_part(before, after, near, place, xa, nrows, ncols)
+    left, right, xa = lax.optimization_barrier((left, right, xa))
     last, first = ends_part(left, right)
     ghosts = (
         passed_along(last, "shock", 1),
@@ -847,7 +931,7 @@
         before,
         after,
     )
-    gathered = local_part(before, after, left, right, own, near, place, xa)
+    gathered = local_part(left, right, own, near, place, xa)
     f_left, f_own, f_right, energies = energy_part(
         ghosts, own, left, right, neighbours, counts, prepared, gathered
     )
@@ -857,17 +941,16 @@
     folded = folded.at[:, :, 0].add(from_left[:, :, 0])
     packed = jnp.concatenate([folded[:2], vel[:1], pos[:1]], axis=0)
     ahead = passed_along(packed, "shock", -1)
-    force = folded[2 : nrows + 2]
-    force = jnp.concatenate([force[: nrows - 2], force[nrows - 2 :] + ahead[:2]], axis=0)
-    old_vel = jnp.concatenate([vel[1:], ahead[2:3]], axis=0)
-    old_pos = jnp.concatenate([pos[1:], ahead[3:4]], axis=0)
-    new_vel = old_vel + KICK_FACTOR * force
-    moved = old_pos + MOVE_FACTOR * new_vel
-    at_front = shock_place == front
-    last_pos = jnp.where(at_front, fresh_positions.transpose(1, 0, 2), moved[nrows - 1])
-    last_vel = jnp.where(at_front, fresh_velocities.transpose(1, 0, 2), new_vel[nrows - 1])
-    new_positions = jnp.concatenate([moved[: nrows - 1], last_pos[None]], axis=0)
-    new_velocities = jnp.concatenate([new_vel[: nrows - 1], last_vel[None]], axis=0)
+    at_front = (shock_place == front).astype(jnp.int32).reshape(1)
+    new_positions, new_velocities = finish_part(
+        at_front,
+        folded,
+        ahead,
+        vel,
+        pos,
+        fresh_positions.transpose(1, 0, 2),
+        fresh_velocities.transpose(1, 0, 2),
+    )
     return (energies, new_positions.transpose(0, 2, 1, 3), new_velocities.transpose(0, 2, 1, 3))
 
 

time: 63 us -> 61.6 us (0.978)
  starting transfers between devices: 21.4 us -> 18.9 us
  waiting for transfers between devices: 9.65 us -> 10.9 us
  other arithmetic: 1.21 us -> 0.02 us
  Pallas kernels: 28.8 us -> 29.9 us
    ppermute x5, waiting for transfers between devices: 3.5 us -> 6.6 us  [passed_along(): return lax.ppermute(block, axis, route)]
    ppermute x5, starting transfers between devices: 15.9 us -> 13.9 us  [passed_along(): return lax.ppermute(block, axis, route)]
    ppermute x4, waiting for transfers between devices: 6.15 us -> 4.27 us  [shifted(): return lax.ppermute(x, axis, [(i, (i + by) % count) for i in range(count)])]
    pallas_call x1 -> x3, Pallas kernels: 6.85 us -> 8.38 us  [the longest x1 4.96 us: local_part(): return call(left, right, own, near, place, xa)[0]]
    transpose x2 -> x0, other arithmetic: 1.16 us -> none  [the longest x1 0.58 us: local(): new_velocities.transpose(0, 2, 1, 3)]
    slice x3 -> x0, local copies, waits for them, and re-layouts: 0.71 us -> none  [the longest x1 0.7 us: local(): old_pos = jnp.concatenate([pos[1:], ahead[3:4]], axis=0)]
    slice x1 -> x3, local copies, waits for them, and re-layouts: 0.01 us -> 0.69 us  [local(): packed = jnp.concatenate([folded[:2], vel[:1], pos[:1]], axis=0)]
  transfers between devices with their start and end apart: 9 -> 9, of which waited for: 5 -> 5; matrix products, arithmetic and copies ran while one was open for 1% -> 1% of each run, Pallas kernels for 18% -> 20%
where the time goes in v5:
time: 61.6 us; the launch traced here: 61.2 us
  Pallas kernels  29.9 us (49%)
  starting transfers between devices  18.9 us (31%)
  waiting for transfers between devices  10.9 us (18%)
  between operations  0.79 us (1%)
  local copies, waits for them, and re-layouts  0.72 us (1%)
    pallas_call x1, Pallas kernels, energy_part(): call(*ghosts, own, left, right, *pinned(neighbours, counts.reshape(rows,...  16.2 us
    ppermute x5, starting transfers between devices, passed_along(): return lax.ppermute(block, axis, route)  13.9 us
    ppermute x5, waiting for transfers between devices, passed_along(): return lax.ppermute(block, axis, route)  6.6 us
    ppermute x4, starting transfers between devices, shifted(): return lax.ppermute(x, axis, [(i, (i + by) % count) for i in range(count)])  5.02 us
    pallas_call x1, Pallas kernels, local_part(): return call(left, right, own, near, place, xa)[0]  4.96 us
    ppermute x4, waiting for transfers between devices, shifted(): return lax.ppermute(x, axis, [(i, (i + by) % count) for i in range(count)])  4.27 us
    pallas_call x1, Pallas kernels, prepare_part(): call(own, *pinned(neighbours, w_first.T, w_second.T, w_read.T, w_out.resh...  4.21 us
    pallas_call x1, Pallas kernels, ghost_part(): return call(before, after, near, place, xa)[0]  2.82 us
  transfers between devices with their start and end apart: 9, of which 5 were waited for; matrix products, arithmetic and copies ran while one was open for 1% of the time, Pallas kernels for 20%

profile of v5, /device:TPU:3, one launch (start us, length us, event | category | flops | bytes accessed | tf_op | source)
XLA Modules:
  0.0 61.2 jit_solution(12191358592814346752)
XLA Ops:
  0.6 1.0 %pack.1.own_ref = bf16[2,1,592,128]{3,2,1,0:T(8,128)(2,1)S(1)} custom-call(bf16[2,1,576,128]{3,2,1,0:T(8,128)(2,1)} %feat_hbm.1, f32[2,3,1,128]{3,2,1,0:T(1,128)} %bitcast.23), custom_call_target="tpu_custom_call" | custom-call | flops 1000000 | bytes 1048576 | tf_op jit(solution)/shard_map/pack/pallas_call | solution.py:763
  1.7 1.3 %collective-permute-start = (bf16[2,1,592,128]{3,2,1,0:T(8,128)(2,1)S(1)}, bf16[2,1,592,128]{3,2,1,0:T(8,128)(2,1)S(1)}, u32[]{:S(2)}, u32[]{:S(2)}) collective-permute-start(bf16[2,1,592,128]{3,2,1,0:T(8,128)(2,1)S(1)} %pack.1.own_ref), channel_id=1, source_target_pairs={{0,1},{1,2},{2,3},{3,0},{4,5},{5,6},{6,7},{7,4},{8,9},{9,10},{10,1... | collective-permute-start | bytes 909320 | tf_op jit(solution)/shard_map/ppermute | solution.py:23
  3.0 2.1 %collective-permute-start.1 = (bf16[2,1,592,128]{3,2,1,0:T(8,128)(2,1)S(1)}, bf16[2,1,592,128]{3,2,1,0:T(8,128)(2,1)S(1)}, u32[]{:S(2)}, u32[]{:S(2)}) collective-permute-start(bf16[2,1,592,128]{3,2,1,0:T(8,128)(2,1)S(1)} %pack.1.own_ref), channel_id=1, source_target_pairs={{0,3},{1,0},{2,1},{3,2},{4,7},{5,4},{6,5},{7,6},{8,11},{9,8},{10,9... | collective-permute-start | bytes 909320 | tf_op jit(solution)/shard_map/ppermute | solution.py:23
  5.1 4.1 %collective-permute-start.2 = (bf16[1,1,592,128]{3,2,1,0:T(8,128)(2,1)S(1)}, bf16[1,1,592,128]{3,2,1,0:T(8,128)(2,1)S(1)}, u32[]{:S(2)}, u32[]{:S(2)}) collective-permute-start(bf16[1,1,592,128]{3,2,1,0:T(8,128)(2,1)S(1)} %get-tuple-element.69), channel_id=1, source_target_pairs={{0,4},{4,8},{8,12},{12,16},{16,20},{20,24},{24,28},{1,5},{5,9},{9,... | collective-permute-start | bytes 454664 | tf_op jit(solution)/shard_map/ppermute | solution.py:29
  9.3 1.9 %collective-permute-start.3 = (bf16[1,1,592,128]{3,2,1,0:T(8,128)(2,1)S(1)}, bf16[1,1,592,128]{3,2,1,0:T(8,128)(2,1)S(1)}, u32[]{:S(2)}, u32[]{:S(2)}) collective-permute-start(bf16[1,1,592,128]{3,2,1,0:T(8,128)(2,1)S(1)} %get-tuple-element.68), channel_id=1, source_target_pairs={{4,0},{8,4},{12,8},{16,12},{20,16},{24,20},{28,24},{5,1},{9,5},{13... | collective-permute-start | bytes 454664 | tf_op jit(solution)/shard_map/ppermute | solution.py:29
  11.2 0.7 %slice_bitcast_fusion = f32[1,3,1,128]{3,2,1,0:T(1,128)S(1)} fusion(f32[2,1,3,128]{3,1,2,0:T(1,128)} %param.15), kind=kLoop, calls=%fused_computation.2 | loop fusion | bytes 3072 | tf_op jit(solution)/shard_map/slice | solution.py:942
  11.9 4.2 %prepare.1 = (bf16[12,128,512]{2,1,0:T(8,128)(2,1)S(1)}, f32[2,24,128]{2,1,0:T(8,128)S(1)}, bf16[128,64]{1,0:T(8,128)(2,1)S(1)}, bf16[192,192]{1,0:T(8,128)(2,1)...) custom-call(bf16[2,1,592,128]{3,2,1,0:T(8,128)(2,1)S(1)} %pack.1.own, ...), custom_call_target="tpu_custom_call" | custom-call | flops 1811939328 | bytes 1048576 | tf_op jit(solution)/shard_map/prepare/pallas_call | solution.py:745
  16.1 0.0 collective-permute-done.2.prev_ref.prev_own_ref
  16.1 0.6 collective-permute-done.3.next_ref.next_own_ref
  16.7 2.8 %ghost.1.xa = bf16[12,576,512]{2,1,0:T(8,128)(2,1)S(1)} custom-call(bf16[1,1,592,128]{3,2,1,0:T(8,128)(2,1)S(1)} %collective-permute-done.2.prev_ref.prev_own_ref, bf16[1,1,592,128]{3,2,1,0:T(8,128)(2,1)S(1)} %collective-permute-done.3.next_ref.next_own_ref, bf16[12,128,512]{2,1,0:T(8,128)(2,1)S(1)} %get-tuple-element.46.near, ...), custom_call_target="tpu_custom_call" | custom-call | flops 905969664 | bytes 1048576 | tf_op jit(solution)/shard_map/ghost/pallas_call | solution.py:793
  19.5 0.0 collective-permute-done.left_ref
  19.5 0.0 collective-permute-done.1.right_ref
  19.5 0.1 ends.1
  19.6 4.0 %collective-permute-start.4 = (bf16[592,256]{1,0:T(8,128)(2,1)S(1)}, bf16[592,256]{1,0:T(8,128)(2,1)S(1)}, u32[]{:S(2)}, u32[]{:S(2)}) collective-permute-start(bf16[592,256]{1,0:T(8,128)(2,1)S(1)} %get-tuple-element.51), channel_id=1, source_target_pairs={{0,4},{4,8},{8,12},{12,16},{16,20},{20,24},{24,28},{1,5},{5,9},{9,... | collective-permute-start | bytes 909320 | tf_op jit(solution)/shard_map/ppermute | solution.py:29
  23.6 1.9 %collective-permute-start.5 = (bf16[592,256]{1,0:T(8,128)(2,1)S(1)}, bf16[592,256]{1,0:T(8,128)(2,1)S(1)}, u32[]{:S(2)}, u32[]{:S(2)}) collective-permute-start(bf16[592,256]{1,0:T(8,128)(2,1)S(1)} %get-tuple-element.52), channel_id=1, source_target_pairs={{4,0},{8,4},{12,8},{16,12},{20,16},{24,20},{28,24},{5,1},{9,5},{13... | collective-permute-start | bytes 909320 | tf_op jit(solution)/shard_map/ppermute | solution.py:29
  25.6 5.0 %local.1.xl_hbm = bf16[12,576,512]{2,1,0:T(8,128)(2,1)S(1)} custom-call(bf16[2,1,592,128]{3,2,1,0:T(8,128)(2,1)S(1)} %collective-permute-done.left_ref, bf16[2,1,592,128]{3,2,1,0:T(8,128)(2,1)S(1)} %collective-permute-done.1.right_ref, bf16[2,1,592,128]{3,2,1,0:T(8,128)(2,1)S(1)} %pack.1.own_ref, bf16[12,128,512]{2,1,0:T(8,128)(2,1)S(1)} %get-tuple-element.46.near, ...), custom_call_target="tpu_custom_call" | custom-call | flops 3623878656 | bytes 1048576 | tf_op jit(solution)/shard_map/local/pallas_call | solution.py:829
  30.5 0.0 collective-permute-done.4.prev_ref
  30.5 2.1 %collective-permute-done.5.next_ref = bf16[592,256]{1,0:T(8,128)(2,1)S(1)} collective-permute-done((bf16[592,256]{1,0:T(8,128)(2,1)S(1)}, bf16[592,256]{1,0:T(8,128)(2,1)S(1)}, u32[]{:S(2)}, u32[]{:S(2)}) %collective-permute-start.5) | collective-permute-done | bytes 303136 | tf_op jit(solution)/shard_map/ppermute | solution.py:29
  32.7 0.0 copy-start.1
  32.7 0.0 copy-start
  32.7 16.2 %energy.1 = (f32[2,1,1,128]{3,2,1,0:T(1,128)}, f32[4,3,1,128]{3,2,1,0:T(1,128)S(1)}, f32[4,3,1,128]{3,2,1,0:T(1,128)S(1)}, f32[4,3,1,128]{3,2,1,0:T(1,128)S(1)}) custom-call(bf16[592,256]{1,0:T(8,128)(2,1)S(1)} %collective-permute-done.4.prev_ref, bf16[592,256]{1,0:T(8,128)(2,1)S(1)} %collective-permute-done.5.next_ref, ...), custom_call_target="tpu_custom_call" | custom-call | flops 8153726976 | bytes 1048576 | tf_op jit(solution)/shard_map/energy/pallas_call | solution.py:876
  48.9 1.6 %collective-permute-start.6 = (f32[4,3,1,128]{3,2,1,0:T(1,128)S(1)}, f32[4,3,1,128]{3,2,1,0:T(1,128)S(1)}, u32[]{:S(2)}, u32[]{:S(2)}) collective-permute-start(f32[4,3,1,128]{3,2,1,0:T(1,128)S(1)} %get-tuple-element.61), channel_id=1, source_target_pairs={{0,3},{1,0},{2,1},{3,2},{4,7},{5,4},{6,5},{7,6},{8,11},{9,8},{10,9... | collective-permute-start | bytes 18440 | tf_op jit(solution)/shard_map/ppermute | solution.py:23
  50.5 0.0 collective-permute-start.7
  50.5 0.0 copy-done.1
  50.5 0.9 %collective-permute-done.6 = f32[4,3,1,128]{3,2,1,0:T(1,128)S(1)} collective-permute-done((f32[4,3,1,128]{3,2,1,0:T(1,128)S(1)}, f32[4,3,1,128]{3,2,1,0:T(1,128)S(1)}, u32[]{:S(2)}, u32[]{:S(2)}) %collective-permute-start.6) | collective-permute-done | bytes 6176 | tf_op jit(solution)/shard_map/ppermute | solution.py:23
  51.4 3.3 %collective-permute-done.7 = f32[4,3,1,128]{3,2,1,0:T(1,128)S(1)} collective-permute-done((f32[4,3,1,128]{3,2,1,0:T(1,128)S(1)}, f32[4,3,1,128]{3,2,1,0:T(1,128)S(1)}, u32[]{:S(2)}, u32[]{:S(2)}) %collective-permute-start.7) | collective-permute-done | bytes 6176 | tf_op jit(solution)/shard_map/ppermute | solution.py:23
  54.8 1.9 %collective-permute-start.8 = (f32[4,3,1,128]{3,2,1,0:T(1,128)S(1)}, f32[4,3,1,128]{3,2,1,0:T(1,128)S(1)}, u32[]{:S(2)}, u32[]{:S(2)}) collective-permute-start(f32[4,3,1,128]{3,2,1,0:T(1,128)S(1)} %pad_maximum_fusion), channel_id=1, source_target_pairs={{4,0},{8,4},{12,8},{16,12},{20,16},{24,20},{28,24},{5,1},{9,5},{13... | collective-permute-start | bytes 18440 | tf_op jit(solution)/shard_map/ppermute | solution.py:29
  56.7 3.9 %collective-permute-done.8.ahead = f32[4,3,1,128]{3,2,1,0:T(1,128)S(1)} collective-permute-done((f32[4,3,1,128]{3,2,1,0:T(1,128)S(1)}, f32[4,3,1,128]{3,2,1,0:T(1,128)S(1)}, u32[]{:S(2)}, u32[]{:S(2)}) %collective-permute-start.8) | collective-permute-done | bytes 6176 | tf_op jit(solution)/shard_map/ppermute | solution.py:29
  60.6 0.0 copy-done
  60.6 0.0 copy-done.2
  60.6 0.0 copy-done.3
  60.6 0.6 finish.1
  (7 shorter events, 0.0 us)
Async XLA Ops:
  1.7 17.8 %collective-permute-start = (bf16[2,1,592,128]{3,2,1,0:T(8,128)(2,1)S(1)}, bf16[2,1,592,128]{3,2,1,0:T(8,128)(2,1)S(1)}, u32[]{:S(2)}, u32[]{:S(2)}) collective-permute-start(bf16[2,1,592,128]{3,2,1,0:T(8,128)(2,1)S(1)} %pack.1.own_ref), channel_id=1, source_target_pairs={{0,1},{1,2},{2,3},{3,0},{4,5},{5,6},{6,7},{7,4},{8,9},{9,10},{10,1... | collective-permute-start | bytes 909320 | tf_op jit(solution)/shard_map/ppermute | solution.py:23
  3.0 16.5 %collective-permute-start.1 = (bf16[2,1,592,128]{3,2,1,0:T(8,128)(2,1)S(1)}, bf16[2,1,592,128]{3,2,1,0:T(8,128)(2,1)S(1)}, u32[]{:S(2)}, u32[]{:S(2)}) collective-permute-start(bf16[2,1,592,128]{3,2,1,0:T(8,128)(2,1)S(1)} %pack.1.own_ref), channel_id=1, source_target_pairs={{0,3},{1,0},{2,1},{3,2},{4,7},{5,4},{6,5},{7,6},{8,11},{9,8},{10,9... | collective-permute-start | bytes 909320 | tf_op jit(solution)/shard_map/ppermute | solution.py:23
  5.1 11.0 %collective-permute-start.2 = (bf16[1,1,592,128]{3,2,1,0:T(8,128)(2,1)S(1)}, bf16[1,1,592,128]{3,2,1,0:T(8,128)(2,1)S(1)}, u32[]{:S(2)}, u32[]{:S(2)}) collective-permute-start(bf16[1,1,592,128]{3,2,1,0:T(8,128)(2,1)S(1)} %get-tuple-element.69), channel_id=1, source_target_pairs={{0,4},{4,8},{8,12},{12,16},{16,20},{20,24},{24,28},{1,5},{5,9},{9,... | collective-permute-start | bytes 454664 | tf_op jit(solution)/shard_map/ppermute | solution.py:29
  9.3 7.4 %collective-permute-start.3 = (bf16[1,1,592,128]{3,2,1,0:T(8,128)(2,1)S(1)}, bf16[1,1,592,128]{3,2,1,0:T(8,128)(2,1)S(1)}, u32[]{:S(2)}, u32[]{:S(2)}) collective-permute-start(bf16[1,1,592,128]{3,2,1,0:T(8,128)(2,1)S(1)} %get-tuple-element.68), channel_id=1, source_target_pairs={{4,0},{8,4},{12,8},{16,12},{20,16},{24,20},{28,24},{5,1},{9,5},{13... | collective-permute-start | bytes 454664 | tf_op jit(solution)/shard_map/ppermute | solution.py:29
  19.6 10.9 %collective-permute-start.4 = (bf16[592,256]{1,0:T(8,128)(2,1)S(1)}, bf16[592,256]{1,0:T(8,128)(2,1)S(1)}, u32[]{:S(2)}, u32[]{:S(2)}) collective-permute-start(bf16[592,256]{1,0:T(8,128)(2,1)S(1)} %get-tuple-element.51), channel_id=1, source_target_pairs={{0,4},{4,8},{8,12},{12,16},{16,20},{20,24},{24,28},{1,5},{5,9},{9,... | collective-permute-start | bytes 909320 | tf_op jit(solution)/shard_map/ppermute | solution.py:29
  23.6 9.0 %collective-permute-start.5 = (bf16[592,256]{1,0:T(8,128)(2,1)S(1)}, bf16[592,256]{1,0:T(8,128)(2,1)S(1)}, u32[]{:S(2)}, u32[]{:S(2)}) collective-permute-start(bf16[592,256]{1,0:T(8,128)(2,1)S(1)} %get-tuple-element.52), channel_id=1, source_target_pairs={{4,0},{8,4},{12,8},{16,12},{20,16},{24,20},{28,24},{5,1},{9,5},{13... | collective-permute-start | bytes 909320 | tf_op jit(solution)/shard_map/ppermute | solution.py:29
  32.7 17.8 %copy-start.1 = (f32[2,1,3,128]{3,1,2,0:T(1,128)S(1)}, f32[2,1,3,128]{3,1,2,0:T(1,128)}, u32[]{:S(2)}) copy-start(f32[2,1,3,128]{3,1,2,0:T(1,128)} %param.16) | copy-start | bytes 9220
  32.7 28.0 %copy-start = (f32[2,1,3,128]{3,1,2,0:T(1,128)S(1)}, f32[2,1,3,128]{3,1,2,0:T(1,128)}, u32[]{:S(2)}) copy-start(f32[2,1,3,128]{3,1,2,0:T(1,128)} %param.15) | copy-start | bytes 9220
  32.7 28.0 %copy-start.2 = (f32[1,3,128]{2,0,1:T(1,128)S(1)}, f32[1,3,128]{2,0,1:T(1,128)}, u32[]{:S(2)}) copy-start(f32[1,3,128]{2,0,1:T(1,128)} %param.24) | copy-start | bytes 4612
  32.7 28.0 %copy-start.3 = (f32[1,3,128]{2,0,1:T(1,128)S(1)}, f32[1,3,128]{2,0,1:T(1,128)}, u32[]{:S(2)}) copy-start(f32[1,3,128]{2,0,1:T(1,128)} %param.25) | copy-start | bytes 4612
  48.9 2.5 %collective-permute-start.6 = (f32[4,3,1,128]{3,2,1,0:T(1,128)S(1)}, f32[4,3,1,128]{3,2,1,0:T(1,128)S(1)}, u32[]{:S(2)}, u32[]{:S(2)}) collective-permute-start(f32[4,3,1,128]{3,2,1,0:T(1,128)S(1)} %get-tuple-element.61), channel_id=1, source_target_pairs={{0,3},{1,0},{2,1},{3,2},{4,7},{5,4},{6,5},{7,6},{8,11},{9,8},{10,9... | collective-permute-start | bytes 18440 | tf_op jit(solution)/shard_map/ppermute | solution.py:23
  50.5 4.3 %collective-permute-start.7 = (f32[4,3,1,128]{3,2,1,0:T(1,128)S(1)}, f32[4,3,1,128]{3,2,1,0:T(1,128)S(1)}, u32[]{:S(2)}, u32[]{:S(2)}) collective-permute-start(f32[4,3,1,128]{3,2,1,0:T(1,128)S(1)} %get-tuple-element.62), channel_id=1, source_target_pairs={{0,1},{1,2},{2,3},{3,0},{4,5},{5,6},{6,7},{7,4},{8,9},{9,10},{10,1... | collective-permute-start | bytes 18440 | tf_op jit(solution)/shard_map/ppermute | solution.py:23
  54.8 5.8 %collective-permute-start.8 = (f32[4,3,1,128]{3,2,1,0:T(1,128)S(1)}, f32[4,3,1,128]{3,2,1,0:T(1,128)S(1)}, u32[]{:S(2)}, u32[]{:S(2)}) collective-permute-start(f32[4,3,1,128]{3,2,1,0:T(1,128)S(1)} %pad_maximum_fusion), channel_id=1, source_target_pairs={{4,0},{8,4},{12,8},{16,12},{20,16},{24,20},{28,24},{5,1},{9,5},{13... | collective-permute-start | bytes 18440 | tf_op jit(solution)/shard_map/ppermute | solution.py:29

commit v6 on v5

--- a/solution.py
+++ b/solution.py
@@ -548,11 +548,11 @@
                 acc[b, m, at : at + group, :] = total[m]
 
     def advance(new, old, step, last=False):
-        radial_rows(new, step)
-        gather(new, step)
         collect(old, step - 1)
         if not last:
             hidden_rows(old, step + 1)
+        gather(new, step)
+        radial_rows(new, step)
         if stream:
 
             @pl.when(step + RING - 1 < steps)

time: 61.6 us -> 61 us (level)
    pallas_call x1, Pallas kernels: 16.2 us -> 15.6 us  [energy_part(): call(*ghosts, own, left, right, *pinned(neighbours, counts.reshape(rows,...]
where the time goes in v6:
time: 61 us; the launch traced here: 60.6 us
  Pallas kernels  29.3 us (48%)
  starting transfers between devices  18.9 us (31%)
  waiting for transfers between devices  10.9 us (18%)
  between operations  0.79 us (1%)
  local copies, waits for them, and re-layouts  0.72 us (1%)
    pallas_call x1, Pallas kernels, energy_part(): call(*ghosts, own, left, right, *pinned(neighbours, counts.reshape(rows,...  15.6 us
    ppermute x5, starting transfers between devices, passed_along(): return lax.ppermute(block, axis, route)  13.9 us
    ppermute x5, waiting for transfers between devices, passed_along(): return lax.ppermute(block, axis, route)  6.6 us
    ppermute x4, starting transfers between devices, shifted(): return lax.ppermute(x, axis, [(i, (i + by) % count) for i in range(count)])  5.02 us
    pallas_call x1, Pallas kernels, local_part(): return call(left, right, own, near, place, xa)[0]  4.96 us
    ppermute x4, waiting for transfers between devices, shifted(): return lax.ppermute(x, axis, [(i, (i + by) % count) for i in range(count)])  4.27 us
    pallas_call x1, Pallas kernels, prepare_part(): call(own, *pinned(neighbours, w_first.T, w_second.T, w_read.T, w_out.resh...  4.21 us
    pallas_call x1, Pallas kernels, ghost_part(): return call(before, after, near, place, xa)[0]  2.82 us
  transfers between devices with their start and end apart: 9, of which 5 were waited for; matrix products, arithmetic and copies ran while one was open for 1% of the time, Pallas kernels for 20%

profile of v6, /device:TPU:3, one launch (start us, length us, event | category | flops | bytes accessed | tf_op | source)
XLA Modules:
  0.0 60.6 jit_solution(11378347576577680297)
XLA Ops:
  0.6 1.0 %pack.1.own_ref = bf16[2,1,592,128]{3,2,1,0:T(8,128)(2,1)S(1)} custom-call(bf16[2,1,576,128]{3,2,1,0:T(8,128)(2,1)} %feat_hbm.1, f32[2,3,1,128]{3,2,1,0:T(1,128)} %bitcast.23), custom_call_target="tpu_custom_call" | custom-call | flops 1000000 | bytes 1048576 | tf_op jit(solution)/shard_map/pack/pallas_call | solution.py:763
  1.7 1.3 %collective-permute-start = (bf16[2,1,592,128]{3,2,1,0:T(8,128)(2,1)S(1)}, bf16[2,1,592,128]{3,2,1,0:T(8,128)(2,1)S(1)}, u32[]{:S(2)}, u32[]{:S(2)}) collective-permute-start(bf16[2,1,592,128]{3,2,1,0:T(8,128)(2,1)S(1)} %pack.1.own_ref), channel_id=1, source_target_pairs={{0,1},{1,2},{2,3},{3,0},{4,5},{5,6},{6,7},{7,4},{8,9},{9,10},{10,1... | collective-permute-start | bytes 909320 | tf_op jit(solution)/shard_map/ppermute | solution.py:23
  3.0 2.1 %collective-permute-start.1 = (bf16[2,1,592,128]{3,2,1,0:T(8,128)(2,1)S(1)}, bf16[2,1,592,128]{3,2,1,0:T(8,128)(2,1)S(1)}, u32[]{:S(2)}, u32[]{:S(2)}) collective-permute-start(bf16[2,1,592,128]{3,2,1,0:T(8,128)(2,1)S(1)} %pack.1.own_ref), channel_id=1, source_target_pairs={{0,3},{1,0},{2,1},{3,2},{4,7},{5,4},{6,5},{7,6},{8,11},{9,8},{10,9... | collective-permute-start | bytes 909320 | tf_op jit(solution)/shard_map/ppermute | solution.py:23
  5.1 4.1 %collective-permute-start.2 = (bf16[1,1,592,128]{3,2,1,0:T(8,128)(2,1)S(1)}, bf16[1,1,592,128]{3,2,1,0:T(8,128)(2,1)S(1)}, u32[]{:S(2)}, u32[]{:S(2)}) collective-permute-start(bf16[1,1,592,128]{3,2,1,0:T(8,128)(2,1)S(1)} %get-tuple-element.69), channel_id=1, source_target_pairs={{0,4},{4,8},{8,12},{12,16},{16,20},{20,24},{24,28},{1,5},{5,9},{9,... | collective-permute-start | bytes 454664 | tf_op jit(solution)/shard_map/ppermute | solution.py:29
  9.3 1.9 %collective-permute-start.3 = (bf16[1,1,592,128]{3,2,1,0:T(8,128)(2,1)S(1)}, bf16[1,1,592,128]{3,2,1,0:T(8,128)(2,1)S(1)}, u32[]{:S(2)}, u32[]{:S(2)}) collective-permute-start(bf16[1,1,592,128]{3,2,1,0:T(8,128)(2,1)S(1)} %get-tuple-element.68), channel_id=1, source_target_pairs={{4,0},{8,4},{12,8},{16,12},{20,16},{24,20},{28,24},{5,1},{9,5},{13... | collective-permute-start | bytes 454664 | tf_op jit(solution)/shard_map/ppermute | solution.py:29
  11.2 0.7 %slice_bitcast_fusion = f32[1,3,1,128]{3,2,1,0:T(1,128)S(1)} fusion(f32[2,1,3,128]{3,1,2,0:T(1,128)} %param.15), kind=kLoop, calls=%fused_computation.2 | loop fusion | bytes 3072 | tf_op jit(solution)/shard_map/slice | solution.py:942
  11.9 4.2 %prepare.1 = (bf16[12,128,512]{2,1,0:T(8,128)(2,1)S(1)}, f32[2,24,128]{2,1,0:T(8,128)S(1)}, bf16[128,64]{1,0:T(8,128)(2,1)S(1)}, bf16[192,192]{1,0:T(8,128)(2,1)...) custom-call(bf16[2,1,592,128]{3,2,1,0:T(8,128)(2,1)S(1)} %pack.1.own, ...), custom_call_target="tpu_custom_call" | custom-call | flops 1811939328 | bytes 1048576 | tf_op jit(solution)/shard_map/prepare/pallas_call | solution.py:745
  16.1 0.0 collective-permute-done.2.prev_ref.prev_own_ref
  16.1 0.6 collective-permute-done.3.next_ref.next_own_ref
  16.7 2.8 %ghost.1.xa = bf16[12,576,512]{2,1,0:T(8,128)(2,1)S(1)} custom-call(bf16[1,1,592,128]{3,2,1,0:T(8,128)(2,1)S(1)} %collective-permute-done.2.prev_ref.prev_own_ref, bf16[1,1,592,128]{3,2,1,0:T(8,128)(2,1)S(1)} %collective-permute-done.3.next_ref.next_own_ref, bf16[12,128,512]{2,1,0:T(8,128)(2,1)S(1)} %get-tuple-element.46.near, ...), custom_call_target="tpu_custom_call" | custom-call | flops 905969664 | bytes 1048576 | tf_op jit(solution)/shard_map/ghost/pallas_call | solution.py:793
  19.5 0.0 collective-permute-done.left_ref
  19.5 0.0 collective-permute-done.1.right_ref
  19.5 0.1 ends.1
  19.6 4.0 %collective-permute-start.4 = (bf16[592,256]{1,0:T(8,128)(2,1)S(1)}, bf16[592,256]{1,0:T(8,128)(2,1)S(1)}, u32[]{:S(2)}, u32[]{:S(2)}) collective-permute-start(bf16[592,256]{1,0:T(8,128)(2,1)S(1)} %get-tuple-element.51), channel_id=1, source_target_pairs={{0,4},{4,8},{8,12},{12,16},{16,20},{20,24},{24,28},{1,5},{5,9},{9,... | collective-permute-start | bytes 909320 | tf_op jit(solution)/shard_map/ppermute | solution.py:29
  23.6 1.9 %collective-permute-start.5 = (bf16[592,256]{1,0:T(8,128)(2,1)S(1)}, bf16[592,256]{1,0:T(8,128)(2,1)S(1)}, u32[]{:S(2)}, u32[]{:S(2)}) collective-permute-start(bf16[592,256]{1,0:T(8,128)(2,1)S(1)} %get-tuple-element.52), channel_id=1, source_target_pairs={{4,0},{8,4},{12,8},{16,12},{20,16},{24,20},{28,24},{5,1},{9,5},{13... | collective-permute-start | bytes 909320 | tf_op jit(solution)/shard_map/ppermute | solution.py:29
  25.6 5.0 %local.1.xl_hbm = bf16[12,576,512]{2,1,0:T(8,128)(2,1)S(1)} custom-call(bf16[2,1,592,128]{3,2,1,0:T(8,128)(2,1)S(1)} %collective-permute-done.left_ref, bf16[2,1,592,128]{3,2,1,0:T(8,128)(2,1)S(1)} %collective-permute-done.1.right_ref, bf16[2,1,592,128]{3,2,1,0:T(8,128)(2,1)S(1)} %pack.1.own_ref, bf16[12,128,512]{2,1,0:T(8,128)(2,1)S(1)} %get-tuple-element.46.near, ...), custom_call_target="tpu_custom_call" | custom-call | flops 3623878656 | bytes 1048576 | tf_op jit(solution)/shard_map/local/pallas_call | solution.py:829
  30.5 0.0 collective-permute-done.4.prev_ref
  30.5 2.1 %collective-permute-done.5.next_ref = bf16[592,256]{1,0:T(8,128)(2,1)S(1)} collective-permute-done((bf16[592,256]{1,0:T(8,128)(2,1)S(1)}, bf16[592,256]{1,0:T(8,128)(2,1)S(1)}, u32[]{:S(2)}, u32[]{:S(2)}) %collective-permute-start.5) | collective-permute-done | bytes 303136 | tf_op jit(solution)/shard_map/ppermute | solution.py:29
  32.7 0.0 copy-start.1
  32.7 0.0 copy-start
  32.7 15.6 %energy.1 = (f32[2,1,1,128]{3,2,1,0:T(1,128)}, f32[4,3,1,128]{3,2,1,0:T(1,128)S(1)}, f32[4,3,1,128]{3,2,1,0:T(1,128)S(1)}, f32[4,3,1,128]{3,2,1,0:T(1,128)S(1)}) custom-call(bf16[592,256]{1,0:T(8,128)(2,1)S(1)} %collective-permute-done.4.prev_ref, bf16[592,256]{1,0:T(8,128)(2,1)S(1)} %collective-permute-done.5.next_ref, ...), custom_call_target="tpu_custom_call" | custom-call | flops 8153726976 | bytes 1048576 | tf_op jit(solution)/shard_map/energy/pallas_call | solution.py:876
  48.3 1.6 %collective-permute-start.6 = (f32[4,3,1,128]{3,2,1,0:T(1,128)S(1)}, f32[4,3,1,128]{3,2,1,0:T(1,128)S(1)}, u32[]{:S(2)}, u32[]{:S(2)}) collective-permute-start(f32[4,3,1,128]{3,2,1,0:T(1,128)S(1)} %get-tuple-element.61), channel_id=1, source_target_pairs={{0,3},{1,0},{2,1},{3,2},{4,7},{5,4},{6,5},{7,6},{8,11},{9,8},{10,9... | collective-permute-start | bytes 18440 | tf_op jit(solution)/shard_map/ppermute | solution.py:23
  49.8 0.0 collective-permute-start.7
  49.8 0.0 copy-done.1
  49.9 0.9 %collective-permute-done.6 = f32[4,3,1,128]{3,2,1,0:T(1,128)S(1)} collective-permute-done((f32[4,3,1,128]{3,2,1,0:T(1,128)S(1)}, f32[4,3,1,128]{3,2,1,0:T(1,128)S(1)}, u32[]{:S(2)}, u32[]{:S(2)}) %collective-permute-start.6) | collective-permute-done | bytes 6176 | tf_op jit(solution)/shard_map/ppermute | solution.py:23
  50.8 3.3 %collective-permute-done.7 = f32[4,3,1,128]{3,2,1,0:T(1,128)S(1)} collective-permute-done((f32[4,3,1,128]{3,2,1,0:T(1,128)S(1)}, f32[4,3,1,128]{3,2,1,0:T(1,128)S(1)}, u32[]{:S(2)}, u32[]{:S(2)}) %collective-permute-start.7) | collective-permute-done | bytes 6176 | tf_op jit(solution)/shard_map/ppermute | solution.py:23
  54.2 1.9 %collective-permute-start.8 = (f32[4,3,1,128]{3,2,1,0:T(1,128)S(1)}, f32[4,3,1,128]{3,2,1,0:T(1,128)S(1)}, u32[]{:S(2)}, u32[]{:S(2)}) collective-permute-start(f32[4,3,1,128]{3,2,1,0:T(1,128)S(1)} %pad_maximum_fusion), channel_id=1, source_target_pairs={{4,0},{8,4},{12,8},{16,12},{20,16},{24,20},{28,24},{5,1},{9,5},{13... | collective-permute-start | bytes 18440 | tf_op jit(solution)/shard_map/ppermute | solution.py:29
  56.1 3.9 %collective-permute-done.8.ahead = f32[4,3,1,128]{3,2,1,0:T(1,128)S(1)} collective-permute-done((f32[4,3,1,128]{3,2,1,0:T(1,128)S(1)}, f32[4,3,1,128]{3,2,1,0:T(1,128)S(1)}, u32[]{:S(2)}, u32[]{:S(2)}) %collective-permute-start.8) | collective-permute-done | bytes 6176 | tf_op jit(solution)/shard_map/ppermute | solution.py:29
  60.0 0.0 copy-done
  60.0 0.0 copy-done.2
  60.0 0.0 copy-done.3
  60.0 0.6 finish.1
  (7 shorter events, 0.0 us)
Async XLA Ops:
  1.7 17.8 %collective-permute-start = (bf16[2,1,592,128]{3,2,1,0:T(8,128)(2,1)S(1)}, bf16[2,1,592,128]{3,2,1,0:T(8,128)(2,1)S(1)}, u32[]{:S(2)}, u32[]{:S(2)}) collective-permute-start(bf16[2,1,592,128]{3,2,1,0:T(8,128)(2,1)S(1)} %pack.1.own_ref), channel_id=1, source_target_pairs={{0,1},{1,2},{2,3},{3,0},{4,5},{5,6},{6,7},{7,4},{8,9},{9,10},{10,1... | collective-permute-start | bytes 909320 | tf_op jit(solution)/shard_map/ppermute | solution.py:23
  3.0 16.5 %collective-permute-start.1 = (bf16[2,1,592,128]{3,2,1,0:T(8,128)(2,1)S(1)}, bf16[2,1,592,128]{3,2,1,0:T(8,128)(2,1)S(1)}, u32[]{:S(2)}, u32[]{:S(2)}) collective-permute-start(bf16[2,1,592,128]{3,2,1,0:T(8,128)(2,1)S(1)} %pack.1.own_ref), channel_id=1, source_target_pairs={{0,3},{1,0},{2,1},{3,2},{4,7},{5,4},{6,5},{7,6},{8,11},{9,8},{10,9... | collective-permute-start | bytes 909320 | tf_op jit(solution)/shard_map/ppermute | solution.py:23
  5.1 11.0 %collective-permute-start.2 = (bf16[1,1,592,128]{3,2,1,0:T(8,128)(2,1)S(1)}, bf16[1,1,592,128]{3,2,1,0:T(8,128)(2,1)S(1)}, u32[]{:S(2)}, u32[]{:S(2)}) collective-permute-start(bf16[1,1,592,128]{3,2,1,0:T(8,128)(2,1)S(1)} %get-tuple-element.69), channel_id=1, source_target_pairs={{0,4},{4,8},{8,12},{12,16},{16,20},{20,24},{24,28},{1,5},{5,9},{9,... | collective-permute-start | bytes 454664 | tf_op jit(solution)/shard_map/ppermute | solution.py:29
  9.3 7.4 %collective-permute-start.3 = (bf16[1,1,592,128]{3,2,1,0:T(8,128)(2,1)S(1)}, bf16[1,1,592,128]{3,2,1,0:T(8,128)(2,1)S(1)}, u32[]{:S(2)}, u32[]{:S(2)}) collective-permute-start(bf16[1,1,592,128]{3,2,1,0:T(8,128)(2,1)S(1)} %get-tuple-element.68), channel_id=1, source_target_pairs={{4,0},{8,4},{12,8},{16,12},{20,16},{24,20},{28,24},{5,1},{9,5},{13... | collective-permute-start | bytes 454664 | tf_op jit(solution)/shard_map/ppermute | solution.py:29
  19.6 10.9 %collective-permute-start.4 = (bf16[592,256]{1,0:T(8,128)(2,1)S(1)}, bf16[592,256]{1,0:T(8,128)(2,1)S(1)}, u32[]{:S(2)}, u32[]{:S(2)}) collective-permute-start(bf16[592,256]{1,0:T(8,128)(2,1)S(1)} %get-tuple-element.51), channel_id=1, source_target_pairs={{0,4},{4,8},{8,12},{12,16},{16,20},{20,24},{24,28},{1,5},{5,9},{9,... | collective-permute-start | bytes 909320 | tf_op jit(solution)/shard_map/ppermute | solution.py:29
  23.6 9.0 %collective-permute-start.5 = (bf16[592,256]{1,0:T(8,128)(2,1)S(1)}, bf16[592,256]{1,0:T(8,128)(2,1)S(1)}, u32[]{:S(2)}, u32[]{:S(2)}) collective-permute-start(bf16[592,256]{1,0:T(8,128)(2,1)S(1)} %get-tuple-element.52), channel_id=1, source_target_pairs={{4,0},{8,4},{12,8},{16,12},{20,16},{24,20},{28,24},{5,1},{9,5},{13... | collective-permute-start | bytes 909320 | tf_op jit(solution)/shard_map/ppermute | solution.py:29
  32.7 17.2 %copy-start.1 = (f32[2,1,3,128]{3,1,2,0:T(1,128)S(1)}, f32[2,1,3,128]{3,1,2,0:T(1,128)}, u32[]{:S(2)}) copy-start(f32[2,1,3,128]{3,1,2,0:T(1,128)} %param.16) | copy-start | bytes 9220
  32.7 27.4 %copy-start = (f32[2,1,3,128]{3,1,2,0:T(1,128)S(1)}, f32[2,1,3,128]{3,1,2,0:T(1,128)}, u32[]{:S(2)}) copy-start(f32[2,1,3,128]{3,1,2,0:T(1,128)} %param.15) | copy-start | bytes 9220
  32.7 27.4 %copy-start.2 = (f32[1,3,128]{2,0,1:T(1,128)S(1)}, f32[1,3,128]{2,0,1:T(1,128)}, u32[]{:S(2)}) copy-start(f32[1,3,128]{2,0,1:T(1,128)} %param.24) | copy-start | bytes 4612
  32.7 27.4 %copy-start.3 = (f32[1,3,128]{2,0,1:T(1,128)S(1)}, f32[1,3,128]{2,0,1:T(1,128)}, u32[]{:S(2)}) copy-start(f32[1,3,128]{2,0,1:T(1,128)} %param.25) | copy-start | bytes 4612
  48.3 2.5 %collective-permute-start.6 = (f32[4,3,1,128]{3,2,1,0:T(1,128)S(1)}, f32[4,3,1,128]{3,2,1,0:T(1,128)S(1)}, u32[]{:S(2)}, u32[]{:S(2)}) collective-permute-start(f32[4,3,1,128]{3,2,1,0:T(1,128)S(1)} %get-tuple-element.61), channel_id=1, source_target_pairs={{0,3},{1,0},{2,1},{3,2},{4,7},{5,4},{6,5},{7,6},{8,11},{9,8},{10,9... | collective-permute-start | bytes 18440 | tf_op jit(solution)/shard_map/ppermute | solution.py:23
  49.8 4.3 %collective-permute-start.7 = (f32[4,3,1,128]{3,2,1,0:T(1,128)S(1)}, f32[4,3,1,128]{3,2,1,0:T(1,128)S(1)}, u32[]{:S(2)}, u32[]{:S(2)}) collective-permute-start(f32[4,3,1,128]{3,2,1,0:T(1,128)S(1)} %get-tuple-element.62), channel_id=1, source_target_pairs={{0,1},{1,2},{2,3},{3,0},{4,5},{5,6},{6,7},{7,4},{8,9},{9,10},{10,1... | collective-permute-start | bytes 18440 | tf_op jit(solution)/shard_map/ppermute | solution.py:23
  54.2 5.8 %collective-permute-start.8 = (f32[4,3,1,128]{3,2,1,0:T(1,128)S(1)}, f32[4,3,1,128]{3,2,1,0:T(1,128)S(1)}, u32[]{:S(2)}, u32[]{:S(2)}) collective-permute-start(f32[4,3,1,128]{3,2,1,0:T(1,128)S(1)} %pad_maximum_fusion), channel_id=1, source_target_pairs={{4,0},{8,4},{12,8},{16,12},{20,16},{24,20},{28,24},{5,1},{9,5},{13... | collective-permute-start | bytes 18440 | tf_op jit(solution)/shard_map/ppermute | solution.py:29

commit v7 on v6

--- a/solution.py
+++ b/solution.py
@@ -482,7 +482,7 @@
         har[b, 7] = 0.5 * root15 * (ux * ux - uy * uy)
         return 0
 
-    lax.fori_loop(0, blocks, geometry, 0)
+    lax.fori_loop(0, blocks, geometry, 0, unroll=blocks == 2)
 
     def hidden_rows(buffers, step):
         held = buffers[3]
@@ -677,7 +677,7 @@
                 force_ref[r + k // 3, c + k % 3, i : i + 1, :] -= value
         return 0
 
-    lax.fori_loop(0, blocks, pull, 0)
+    lax.fori_loop(0, blocks, pull, 0, unroll=blocks == 2)
     for r in range(rows + 2):
         for i in range(3):
             fleft_ref[r, i] = force_ref[r, 0:1, i, :]

time: 61 us -> 60.4 us (level)
  no operation moved by 1% of the time
where the time goes in v7:
time: 60.4 us; the launch traced here: 60.1 us
  Pallas kernels  28.8 us (48%)
  starting transfers between devices  18.9 us (31%)
  waiting for transfers between devices  10.9 us (18%)
  between operations  0.79 us (1%)
  local copies, waits for them, and re-layouts  0.72 us (1%)
    pallas_call x1, Pallas kernels, energy_part(): call(*ghosts, own, left, right, *pinned(neighbours, counts.reshape(rows,...  15.1 us
    ppermute x5, starting transfers between devices, passed_along(): return lax.ppermute(block, axis, route)  13.9 us
    ppermute x5, waiting for transfers between devices, passed_along(): return lax.ppermute(block, axis, route)  6.6 us
    ppermute x4, starting transfers between devices, shifted(): return lax.ppermute(x, axis, [(i, (i + by) % count) for i in range(count)])  5.02 us
    pallas_call x1, Pallas kernels, local_part(): return call(left, right, own, near, place, xa)[0]  4.96 us
    ppermute x4, waiting for transfers between devices, shifted(): return lax.ppermute(x, axis, [(i, (i + by) % count) for i in range(count)])  4.27 us
    pallas_call x1, Pallas kernels, prepare_part(): call(own, *pinned(neighbours, w_first.T, w_second.T, w_read.T, w_out.resh...  4.21 us
    pallas_call x1, Pallas kernels, ghost_part(): return call(before, after, near, place, xa)[0]  2.82 us
  transfers between devices with their start and end apart: 9, of which 5 were waited for; matrix products, arithmetic and copies ran while one was open for 1% of the time, Pallas kernels for 20%

profile of v7, /device:TPU:3, one launch (start us, length us, event | category | flops | bytes accessed | tf_op | source)
XLA Modules:
  0.0 60.1 jit_solution(8808713264550581943)
XLA Ops:
  0.6 1.0 %pack.1.own_ref = bf16[2,1,592,128]{3,2,1,0:T(8,128)(2,1)S(1)} custom-call(bf16[2,1,576,128]{3,2,1,0:T(8,128)(2,1)} %feat_hbm.1, f32[2,3,1,128]{3,2,1,0:T(1,128)} %bitcast.23), custom_call_target="tpu_custom_call" | custom-call | flops 1000000 | bytes 1048576 | tf_op jit(solution)/shard_map/pack/pallas_call | solution.py:763
  1.7 1.3 %collective-permute-start = (bf16[2,1,592,128]{3,2,1,0:T(8,128)(2,1)S(1)}, bf16[2,1,592,128]{3,2,1,0:T(8,128)(2,1)S(1)}, u32[]{:S(2)}, u32[]{:S(2)}) collective-permute-start(bf16[2,1,592,128]{3,2,1,0:T(8,128)(2,1)S(1)} %pack.1.own_ref), channel_id=1, source_target_pairs={{0,1},{1,2},{2,3},{3,0},{4,5},{5,6},{6,7},{7,4},{8,9},{9,10},{10,1... | collective-permute-start | bytes 909320 | tf_op jit(solution)/shard_map/ppermute | solution.py:23
  3.0 2.1 %collective-permute-start.1 = (bf16[2,1,592,128]{3,2,1,0:T(8,128)(2,1)S(1)}, bf16[2,1,592,128]{3,2,1,0:T(8,128)(2,1)S(1)}, u32[]{:S(2)}, u32[]{:S(2)}) collective-permute-start(bf16[2,1,592,128]{3,2,1,0:T(8,128)(2,1)S(1)} %pack.1.own_ref), channel_id=1, source_target_pairs={{0,3},{1,0},{2,1},{3,2},{4,7},{5,4},{6,5},{7,6},{8,11},{9,8},{10,9... | collective-permute-start | bytes 909320 | tf_op jit(solution)/shard_map/ppermute | solution.py:23
  5.1 4.1 %collective-permute-start.2 = (bf16[1,1,592,128]{3,2,1,0:T(8,128)(2,1)S(1)}, bf16[1,1,592,128]{3,2,1,0:T(8,128)(2,1)S(1)}, u32[]{:S(2)}, u32[]{:S(2)}) collective-permute-start(bf16[1,1,592,128]{3,2,1,0:T(8,128)(2,1)S(1)} %get-tuple-element.69), channel_id=1, source_target_pairs={{0,4},{4,8},{8,12},{12,16},{16,20},{20,24},{24,28},{1,5},{5,9},{9,... | collective-permute-start | bytes 454664 | tf_op jit(solution)/shard_map/ppermute | solution.py:29
  9.3 1.9 %collective-permute-start.3 = (bf16[1,1,592,128]{3,2,1,0:T(8,128)(2,1)S(1)}, bf16[1,1,592,128]{3,2,1,0:T(8,128)(2,1)S(1)}, u32[]{:S(2)}, u32[]{:S(2)}) collective-permute-start(bf16[1,1,592,128]{3,2,1,0:T(8,128)(2,1)S(1)} %get-tuple-element.68), channel_id=1, source_target_pairs={{4,0},{8,4},{12,8},{16,12},{20,16},{24,20},{28,24},{5,1},{9,5},{13... | collective-permute-start | bytes 454664 | tf_op jit(solution)/shard_map/ppermute | solution.py:29
  11.2 0.7 %slice_bitcast_fusion = f32[1,3,1,128]{3,2,1,0:T(1,128)S(1)} fusion(f32[2,1,3,128]{3,1,2,0:T(1,128)} %param.15), kind=kLoop, calls=%fused_computation.2 | loop fusion | bytes 3072 | tf_op jit(solution)/shard_map/slice | solution.py:942
  11.9 4.2 %prepare.1 = (bf16[12,128,512]{2,1,0:T(8,128)(2,1)S(1)}, f32[2,24,128]{2,1,0:T(8,128)S(1)}, bf16[128,64]{1,0:T(8,128)(2,1)S(1)}, bf16[192,192]{1,0:T(8,128)(2,1)...) custom-call(bf16[2,1,592,128]{3,2,1,0:T(8,128)(2,1)S(1)} %pack.1.own, ...), custom_call_target="tpu_custom_call" | custom-call | flops 1811939328 | bytes 1048576 | tf_op jit(solution)/shard_map/prepare/pallas_call | solution.py:745
  16.1 0.0 collective-permute-done.2.prev_ref.prev_own_ref
  16.1 0.6 collective-permute-done.3.next_ref.next_own_ref
  16.7 2.8 %ghost.1.xa = bf16[12,576,512]{2,1,0:T(8,128)(2,1)S(1)} custom-call(bf16[1,1,592,128]{3,2,1,0:T(8,128)(2,1)S(1)} %collective-permute-done.2.prev_ref.prev_own_ref, bf16[1,1,592,128]{3,2,1,0:T(8,128)(2,1)S(1)} %collective-permute-done.3.next_ref.next_own_ref, bf16[12,128,512]{2,1,0:T(8,128)(2,1)S(1)} %get-tuple-element.46.near, ...), custom_call_target="tpu_custom_call" | custom-call | flops 905969664 | bytes 1048576 | tf_op jit(solution)/shard_map/ghost/pallas_call | solution.py:793
  19.5 0.0 collective-permute-done.left_ref
  19.5 0.0 collective-permute-done.1.right_ref
  19.5 0.1 ends.1
  19.6 4.0 %collective-permute-start.4 = (bf16[592,256]{1,0:T(8,128)(2,1)S(1)}, bf16[592,256]{1,0:T(8,128)(2,1)S(1)}, u32[]{:S(2)}, u32[]{:S(2)}) collective-permute-start(bf16[592,256]{1,0:T(8,128)(2,1)S(1)} %get-tuple-element.51), channel_id=1, source_target_pairs={{0,4},{4,8},{8,12},{12,16},{16,20},{20,24},{24,28},{1,5},{5,9},{9,... | collective-permute-start | bytes 909320 | tf_op jit(solution)/shard_map/ppermute | solution.py:29
  23.6 1.9 %collective-permute-start.5 = (bf16[592,256]{1,0:T(8,128)(2,1)S(1)}, bf16[592,256]{1,0:T(8,128)(2,1)S(1)}, u32[]{:S(2)}, u32[]{:S(2)}) collective-permute-start(bf16[592,256]{1,0:T(8,128)(2,1)S(1)} %get-tuple-element.52), channel_id=1, source_target_pairs={{4,0},{8,4},{12,8},{16,12},{20,16},{24,20},{28,24},{5,1},{9,5},{13... | collective-permute-start | bytes 909320 | tf_op jit(solution)/shard_map/ppermute | solution.py:29
  25.6 5.0 %local.1.xl_hbm = bf16[12,576,512]{2,1,0:T(8,128)(2,1)S(1)} custom-call(bf16[2,1,592,128]{3,2,1,0:T(8,128)(2,1)S(1)} %collective-permute-done.left_ref, bf16[2,1,592,128]{3,2,1,0:T(8,128)(2,1)S(1)} %collective-permute-done.1.right_ref, bf16[2,1,592,128]{3,2,1,0:T(8,128)(2,1)S(1)} %pack.1.own_ref, bf16[12,128,512]{2,1,0:T(8,128)(2,1)S(1)} %get-tuple-element.46.near, ...), custom_call_target="tpu_custom_call" | custom-call | flops 3623878656 | bytes 1048576 | tf_op jit(solution)/shard_map/local/pallas_call | solution.py:829
  30.5 0.0 collective-permute-done.4.prev_ref
  30.5 2.1 %collective-permute-done.5.next_ref = bf16[592,256]{1,0:T(8,128)(2,1)S(1)} collective-permute-done((bf16[592,256]{1,0:T(8,128)(2,1)S(1)}, bf16[592,256]{1,0:T(8,128)(2,1)S(1)}, u32[]{:S(2)}, u32[]{:S(2)}) %collective-permute-start.5) | collective-permute-done | bytes 303136 | tf_op jit(solution)/shard_map/ppermute | solution.py:29
  32.7 0.0 copy-start.1
  32.7 0.0 copy-start
  32.7 15.1 %energy.1 = (f32[2,1,1,128]{3,2,1,0:T(1,128)}, f32[4,3,1,128]{3,2,1,0:T(1,128)S(1)}, f32[4,3,1,128]{3,2,1,0:T(1,128)S(1)}, f32[4,3,1,128]{3,2,1,0:T(1,128)S(1)}) custom-call(bf16[592,256]{1,0:T(8,128)(2,1)S(1)} %collective-permute-done.4.prev_ref, bf16[592,256]{1,0:T(8,128)(2,1)S(1)} %collective-permute-done.5.next_ref, ...), custom_call_target="tpu_custom_call" | custom-call | flops 8153726976 | bytes 1048576 | tf_op jit(solution)/shard_map/energy/pallas_call | solution.py:876
  47.8 1.6 %collective-permute-start.6 = (f32[4,3,1,128]{3,2,1,0:T(1,128)S(1)}, f32[4,3,1,128]{3,2,1,0:T(1,128)S(1)}, u32[]{:S(2)}, u32[]{:S(2)}) collective-permute-start(f32[4,3,1,128]{3,2,1,0:T(1,128)S(1)} %get-tuple-element.61), channel_id=1, source_target_pairs={{0,3},{1,0},{2,1},{3,2},{4,7},{5,4},{6,5},{7,6},{8,11},{9,8},{10,9... | collective-permute-start | bytes 18440 | tf_op jit(solution)/shard_map/ppermute | solution.py:23
  49.3 0.0 collective-permute-start.7
  49.3 0.0 copy-done.1
  49.3 0.9 %collective-permute-done.6 = f32[4,3,1,128]{3,2,1,0:T(1,128)S(1)} collective-permute-done((f32[4,3,1,128]{3,2,1,0:T(1,128)S(1)}, f32[4,3,1,128]{3,2,1,0:T(1,128)S(1)}, u32[]{:S(2)}, u32[]{:S(2)}) %collective-permute-start.6) | collective-permute-done | bytes 6176 | tf_op jit(solution)/shard_map/ppermute | solution.py:23
  50.3 3.3 %collective-permute-done.7 = f32[4,3,1,128]{3,2,1,0:T(1,128)S(1)} collective-permute-done((f32[4,3,1,128]{3,2,1,0:T(1,128)S(1)}, f32[4,3,1,128]{3,2,1,0:T(1,128)S(1)}, u32[]{:S(2)}, u32[]{:S(2)}) %collective-permute-start.7) | collective-permute-done | bytes 6176 | tf_op jit(solution)/shard_map/ppermute | solution.py:23
  53.7 1.9 %collective-permute-start.8 = (f32[4,3,1,128]{3,2,1,0:T(1,128)S(1)}, f32[4,3,1,128]{3,2,1,0:T(1,128)S(1)}, u32[]{:S(2)}, u32[]{:S(2)}) collective-permute-start(f32[4,3,1,128]{3,2,1,0:T(1,128)S(1)} %pad_maximum_fusion), channel_id=1, source_target_pairs={{4,0},{8,4},{12,8},{16,12},{20,16},{24,20},{28,24},{5,1},{9,5},{13... | collective-permute-start | bytes 18440 | tf_op jit(solution)/shard_map/ppermute | solution.py:29
  55.6 3.9 %collective-permute-done.8.ahead = f32[4,3,1,128]{3,2,1,0:T(1,128)S(1)} collective-permute-done((f32[4,3,1,128]{3,2,1,0:T(1,128)S(1)}, f32[4,3,1,128]{3,2,1,0:T(1,128)S(1)}, u32[]{:S(2)}, u32[]{:S(2)}) %collective-permute-start.8) | collective-permute-done | bytes 6176 | tf_op jit(solution)/shard_map/ppermute | solution.py:29
  59.5 0.0 copy-done
  59.5 0.0 copy-done.2
  59.5 0.0 copy-done.3
  59.5 0.6 finish.1
  (7 shorter events, 0.0 us)
Async XLA Ops:
  1.7 17.8 %collective-permute-start = (bf16[2,1,592,128]{3,2,1,0:T(8,128)(2,1)S(1)}, bf16[2,1,592,128]{3,2,1,0:T(8,128)(2,1)S(1)}, u32[]{:S(2)}, u32[]{:S(2)}) collective-permute-start(bf16[2,1,592,128]{3,2,1,0:T(8,128)(2,1)S(1)} %pack.1.own_ref), channel_id=1, source_target_pairs={{0,1},{1,2},{2,3},{3,0},{4,5},{5,6},{6,7},{7,4},{8,9},{9,10},{10,1... | collective-permute-start | bytes 909320 | tf_op jit(solution)/shard_map/ppermute | solution.py:23
  3.0 16.5 %collective-permute-start.1 = (bf16[2,1,592,128]{3,2,1,0:T(8,128)(2,1)S(1)}, bf16[2,1,592,128]{3,2,1,0:T(8,128)(2,1)S(1)}, u32[]{:S(2)}, u32[]{:S(2)}) collective-permute-start(bf16[2,1,592,128]{3,2,1,0:T(8,128)(2,1)S(1)} %pack.1.own_ref), channel_id=1, source_target_pairs={{0,3},{1,0},{2,1},{3,2},{4,7},{5,4},{6,5},{7,6},{8,11},{9,8},{10,9... | collective-permute-start | bytes 909320 | tf_op jit(solution)/shard_map/ppermute | solution.py:23
  5.1 11.0 %collective-permute-start.2 = (bf16[1,1,592,128]{3,2,1,0:T(8,128)(2,1)S(1)}, bf16[1,1,592,128]{3,2,1,0:T(8,128)(2,1)S(1)}, u32[]{:S(2)}, u32[]{:S(2)}) collective-permute-start(bf16[1,1,592,128]{3,2,1,0:T(8,128)(2,1)S(1)} %get-tuple-element.69), channel_id=1, source_target_pairs={{0,4},{4,8},{8,12},{12,16},{16,20},{20,24},{24,28},{1,5},{5,9},{9,... | collective-permute-start | bytes 454664 | tf_op jit(solution)/shard_map/ppermute | solution.py:29
  9.3 7.4 %collective-permute-start.3 = (bf16[1,1,592,128]{3,2,1,0:T(8,128)(2,1)S(1)}, bf16[1,1,592,128]{3,2,1,0:T(8,128)(2,1)S(1)}, u32[]{:S(2)}, u32[]{:S(2)}) collective-permute-start(bf16[1,1,592,128]{3,2,1,0:T(8,128)(2,1)S(1)} %get-tuple-element.68), channel_id=1, source_target_pairs={{4,0},{8,4},{12,8},{16,12},{20,16},{24,20},{28,24},{5,1},{9,5},{13... | collective-permute-start | bytes 454664 | tf_op jit(solution)/shard_map/ppermute | solution.py:29
  19.6 10.9 %collective-permute-start.4 = (bf16[592,256]{1,0:T(8,128)(2,1)S(1)}, bf16[592,256]{1,0:T(8,128)(2,1)S(1)}, u32[]{:S(2)}, u32[]{:S(2)}) collective-permute-start(bf16[592,256]{1,0:T(8,128)(2,1)S(1)} %get-tuple-element.51), channel_id=1, source_target_pairs={{0,4},{4,8},{8,12},{12,16},{16,20},{20,24},{24,28},{1,5},{5,9},{9,... | collective-permute-start | bytes 909320 | tf_op jit(solution)/shard_map/ppermute | solution.py:29
  23.6 9.0 %collective-permute-start.5 = (bf16[592,256]{1,0:T(8,128)(2,1)S(1)}, bf16[592,256]{1,0:T(8,128)(2,1)S(1)}, u32[]{:S(2)}, u32[]{:S(2)}) collective-permute-start(bf16[592,256]{1,0:T(8,128)(2,1)S(1)} %get-tuple-element.52), channel_id=1, source_target_pairs={{4,0},{8,4},{12,8},{16,12},{20,16},{24,20},{28,24},{5,1},{9,5},{13... | collective-permute-start | bytes 909320 | tf_op jit(solution)/shard_map/ppermute | solution.py:29
  32.7 16.7 %copy-start.1 = (f32[2,1,3,128]{3,1,2,0:T(1,128)S(1)}, f32[2,1,3,128]{3,1,2,0:T(1,128)}, u32[]{:S(2)}) copy-start(f32[2,1,3,128]{3,1,2,0:T(1,128)} %param.16) | copy-start | bytes 9220
  32.7 26.8 %copy-start = (f32[2,1,3,128]{3,1,2,0:T(1,128)S(1)}, f32[2,1,3,128]{3,1,2,0:T(1,128)}, u32[]{:S(2)}) copy-start(f32[2,1,3,128]{3,1,2,0:T(1,128)} %param.15) | copy-start | bytes 9220
  32.7 26.8 %copy-start.2 = (f32[1,3,128]{2,0,1:T(1,128)S(1)}, f32[1,3,128]{2,0,1:T(1,128)}, u32[]{:S(2)}) copy-start(f32[1,3,128]{2,0,1:T(1,128)} %param.24) | copy-start | bytes 4612
  32.7 26.8 %copy-start.3 = (f32[1,3,128]{2,0,1:T(1,128)S(1)}, f32[1,3,128]{2,0,1:T(1,128)}, u32[]{:S(2)}) copy-start(f32[1,3,128]{2,0,1:T(1,128)} %param.25) | copy-start | bytes 4612
  47.8 2.5 %collective-permute-start.6 = (f32[4,3,1,128]{3,2,1,0:T(1,128)S(1)}, f32[4,3,1,128]{3,2,1,0:T(1,128)S(1)}, u32[]{:S(2)}, u32[]{:S(2)}) collective-permute-start(f32[4,3,1,128]{3,2,1,0:T(1,128)S(1)} %get-tuple-element.61), channel_id=1, source_target_pairs={{0,3},{1,0},{2,1},{3,2},{4,7},{5,4},{6,5},{7,6},{8,11},{9,8},{10,9... | collective-permute-start | bytes 18440 | tf_op jit(solution)/shard_map/ppermute | solution.py:23
  49.3 4.3 %collective-permute-start.7 = (f32[4,3,1,128]{3,2,1,0:T(1,128)S(1)}, f32[4,3,1,128]{3,2,1,0:T(1,128)S(1)}, u32[]{:S(2)}, u32[]{:S(2)}) collective-permute-start(f32[4,3,1,128]{3,2,1,0:T(1,128)S(1)} %get-tuple-element.62), channel_id=1, source_target_pairs={{0,1},{1,2},{2,3},{3,0},{4,5},{5,6},{6,7},{7,4},{8,9},{9,10},{10,1... | collective-permute-start | bytes 18440 | tf_op jit(solution)/shard_map/ppermute | solution.py:23
  53.7 5.8 %collective-permute-start.8 = (f32[4,3,1,128]{3,2,1,0:T(1,128)S(1)}, f32[4,3,1,128]{3,2,1,0:T(1,128)S(1)}, u32[]{:S(2)}, u32[]{:S(2)}) collective-permute-start(f32[4,3,1,128]{3,2,1,0:T(1,128)S(1)} %pad_maximum_fusion), channel_id=1, source_target_pairs={{4,0},{8,4},{12,8},{16,12},{20,16},{24,20},{28,24},{5,1},{9,5},{13... | collective-permute-start | bytes 18440 | tf_op jit(solution)/shard_map/ppermute | solution.py:29

commit v8 on v7

--- a/solution.py
+++ b/solution.py
@@ -598,6 +598,7 @@
 
     def edge_terms(buffers, step):
         xg, wsc, dsc = buffers[:3]
+        group = 16
         b, first = step // quads, (step % quads) * QUAD
         for s in range(QUAD):
             ln = slice(s * LANES, (s + 1) * LANES)

time: 60.4 us -> 60.2 us (level)
  no operation moved by 1% of the time
where the time goes in v8:
time: 60.2 us; the launch traced here: 59.9 us
  Pallas kernels  28.6 us (48%)
  starting transfers between devices  18.9 us (31%)
  waiting for transfers between devices  10.9 us (18%)
  between operations  0.79 us (1%)
  local copies, waits for them, and re-layouts  0.72 us (1%)
    pallas_call x1, Pallas kernels, energy_part(): call(*ghosts, own, left, right, *pinned(neighbours, counts.reshape(rows,...  14.9 us
    ppermute x5, starting transfers between devices, passed_along(): return lax.ppermute(block, axis, route)  13.9 us
    ppermute x5, waiting for transfers between devices, passed_along(): return lax.ppermute(block, axis, route)  6.6 us
    ppermute x4, starting transfers between devices, shifted(): return lax.ppermute(x, axis, [(i, (i + by) % count) for i in range(count)])  5.02 us
    pallas_call x1, Pallas kernels, local_part(): return call(left, right, own, near, place, xa)[0]  4.96 us
    ppermute x4, waiting for transfers between devices, shifted(): return lax.ppermute(x, axis, [(i, (i + by) % count) for i in range(count)])  4.27 us
    pallas_call x1, Pallas kernels, prepare_part(): call(own, *pinned(neighbours, w_first.T, w_second.T, w_read.T, w_out.resh...  4.21 us
    pallas_call x1, Pallas kernels, ghost_part(): return call(before, after, near, place, xa)[0]  2.82 us
  transfers between devices with their start and end apart: 9, of which 5 were waited for; matrix products, arithmetic and copies ran while one was open for 1% of the time, Pallas kernels for 20%

profile of v8, /device:TPU:3, one launch (start us, length us, event | category | flops | bytes accessed | tf_op | source)
XLA Modules:
  0.0 59.9 jit_solution(14556901196761729974)
XLA Ops:
  0.6 1.0 %pack.1.own_ref = bf16[2,1,592,128]{3,2,1,0:T(8,128)(2,1)S(1)} custom-call(bf16[2,1,576,128]{3,2,1,0:T(8,128)(2,1)} %feat_hbm.1, f32[2,3,1,128]{3,2,1,0:T(1,128)} %bitcast.23), custom_call_target="tpu_custom_call" | custom-call | flops 1000000 | bytes 1048576 | tf_op jit(solution)/shard_map/pack/pallas_call | solution.py:764
  1.7 1.3 %collective-permute-start = (bf16[2,1,592,128]{3,2,1,0:T(8,128)(2,1)S(1)}, bf16[2,1,592,128]{3,2,1,0:T(8,128)(2,1)S(1)}, u32[]{:S(2)}, u32[]{:S(2)}) collective-permute-start(bf16[2,1,592,128]{3,2,1,0:T(8,128)(2,1)S(1)} %pack.1.own_ref), channel_id=1, source_target_pairs={{0,1},{1,2},{2,3},{3,0},{4,5},{5,6},{6,7},{7,4},{8,9},{9,10},{10,1... | collective-permute-start | bytes 909320 | tf_op jit(solution)/shard_map/ppermute | solution.py:23
  3.0 2.1 %collective-permute-start.1 = (bf16[2,1,592,128]{3,2,1,0:T(8,128)(2,1)S(1)}, bf16[2,1,592,128]{3,2,1,0:T(8,128)(2,1)S(1)}, u32[]{:S(2)}, u32[]{:S(2)}) collective-permute-start(bf16[2,1,592,128]{3,2,1,0:T(8,128)(2,1)S(1)} %pack.1.own_ref), channel_id=1, source_target_pairs={{0,3},{1,0},{2,1},{3,2},{4,7},{5,4},{6,5},{7,6},{8,11},{9,8},{10,9... | collective-permute-start | bytes 909320 | tf_op jit(solution)/shard_map/ppermute | solution.py:23
  5.1 4.1 %collective-permute-start.2 = (bf16[1,1,592,128]{3,2,1,0:T(8,128)(2,1)S(1)}, bf16[1,1,592,128]{3,2,1,0:T(8,128)(2,1)S(1)}, u32[]{:S(2)}, u32[]{:S(2)}) collective-permute-start(bf16[1,1,592,128]{3,2,1,0:T(8,128)(2,1)S(1)} %get-tuple-element.69), channel_id=1, source_target_pairs={{0,4},{4,8},{8,12},{12,16},{16,20},{20,24},{24,28},{1,5},{5,9},{9,... | collective-permute-start | bytes 454664 | tf_op jit(solution)/shard_map/ppermute | solution.py:29
  9.3 1.9 %collective-permute-start.3 = (bf16[1,1,592,128]{3,2,1,0:T(8,128)(2,1)S(1)}, bf16[1,1,592,128]{3,2,1,0:T(8,128)(2,1)S(1)}, u32[]{:S(2)}, u32[]{:S(2)}) collective-permute-start(bf16[1,1,592,128]{3,2,1,0:T(8,128)(2,1)S(1)} %get-tuple-element.68), channel_id=1, source_target_pairs={{4,0},{8,4},{12,8},{16,12},{20,16},{24,20},{28,24},{5,1},{9,5},{13... | collective-permute-start | bytes 454664 | tf_op jit(solution)/shard_map/ppermute | solution.py:29
  11.2 0.7 %slice_bitcast_fusion = f32[1,3,1,128]{3,2,1,0:T(1,128)S(1)} fusion(f32[2,1,3,128]{3,1,2,0:T(1,128)} %param.15), kind=kLoop, calls=%fused_computation.2 | loop fusion | bytes 3072 | tf_op jit(solution)/shard_map/slice | solution.py:943
  11.9 4.2 %prepare.1 = (bf16[12,128,512]{2,1,0:T(8,128)(2,1)S(1)}, f32[2,24,128]{2,1,0:T(8,128)S(1)}, bf16[128,64]{1,0:T(8,128)(2,1)S(1)}, bf16[192,192]{1,0:T(8,128)(2,1)...) custom-call(bf16[2,1,592,128]{3,2,1,0:T(8,128)(2,1)S(1)} %pack.1.own, ...), custom_call_target="tpu_custom_call" | custom-call | flops 1811939328 | bytes 1048576 | tf_op jit(solution)/shard_map/prepare/pallas_call | solution.py:746
  16.1 0.0 collective-permute-done.2.prev_ref.prev_own_ref
  16.1 0.6 collective-permute-done.3.next_ref.next_own_ref
  16.7 2.8 %ghost.1.xa = bf16[12,576,512]{2,1,0:T(8,128)(2,1)S(1)} custom-call(bf16[1,1,592,128]{3,2,1,0:T(8,128)(2,1)S(1)} %collective-permute-done.2.prev_ref.prev_own_ref, bf16[1,1,592,128]{3,2,1,0:T(8,128)(2,1)S(1)} %collective-permute-done.3.next_ref.next_own_ref, bf16[12,128,512]{2,1,0:T(8,128)(2,1)S(1)} %get-tuple-element.46.near, ...), custom_call_target="tpu_custom_call" | custom-call | flops 905969664 | bytes 1048576 | tf_op jit(solution)/shard_map/ghost/pallas_call | solution.py:794
  19.5 0.0 collective-permute-done.left_ref
  19.5 0.0 collective-permute-done.1.right_ref
  19.5 0.1 ends.1
  19.6 4.0 %collective-permute-start.4 = (bf16[592,256]{1,0:T(8,128)(2,1)S(1)}, bf16[592,256]{1,0:T(8,128)(2,1)S(1)}, u32[]{:S(2)}, u32[]{:S(2)}) collective-permute-start(bf16[592,256]{1,0:T(8,128)(2,1)S(1)} %get-tuple-element.51), channel_id=1, source_target_pairs={{0,4},{4,8},{8,12},{12,16},{16,20},{20,24},{24,28},{1,5},{5,9},{9,... | collective-permute-start | bytes 909320 | tf_op jit(solution)/shard_map/ppermute | solution.py:29
  23.6 1.9 %collective-permute-start.5 = (bf16[592,256]{1,0:T(8,128)(2,1)S(1)}, bf16[592,256]{1,0:T(8,128)(2,1)S(1)}, u32[]{:S(2)}, u32[]{:S(2)}) collective-permute-start(bf16[592,256]{1,0:T(8,128)(2,1)S(1)} %get-tuple-element.52), channel_id=1, source_target_pairs={{4,0},{8,4},{12,8},{16,12},{20,16},{24,20},{28,24},{5,1},{9,5},{13... | collective-permute-start | bytes 909320 | tf_op jit(solution)/shard_map/ppermute | solution.py:29
  25.6 5.0 %local.1.xl_hbm = bf16[12,576,512]{2,1,0:T(8,128)(2,1)S(1)} custom-call(bf16[2,1,592,128]{3,2,1,0:T(8,128)(2,1)S(1)} %collective-permute-done.left_ref, bf16[2,1,592,128]{3,2,1,0:T(8,128)(2,1)S(1)} %collective-permute-done.1.right_ref, bf16[2,1,592,128]{3,2,1,0:T(8,128)(2,1)S(1)} %pack.1.own_ref, bf16[12,128,512]{2,1,0:T(8,128)(2,1)S(1)} %get-tuple-element.46.near, ...), custom_call_target="tpu_custom_call" | custom-call | flops 3623878656 | bytes 1048576 | tf_op jit(solution)/shard_map/local/pallas_call | solution.py:830
  30.5 0.0 collective-permute-done.4.prev_ref
  30.5 2.1 %collective-permute-done.5.next_ref = bf16[592,256]{1,0:T(8,128)(2,1)S(1)} collective-permute-done((bf16[592,256]{1,0:T(8,128)(2,1)S(1)}, bf16[592,256]{1,0:T(8,128)(2,1)S(1)}, u32[]{:S(2)}, u32[]{:S(2)}) %collective-permute-start.5) | collective-permute-done | bytes 303136 | tf_op jit(solution)/shard_map/ppermute | solution.py:29
  32.7 0.0 copy-start.1
  32.7 0.0 copy-start
  32.7 14.9 %energy.1 = (f32[2,1,1,128]{3,2,1,0:T(1,128)}, f32[4,3,1,128]{3,2,1,0:T(1,128)S(1)}, f32[4,3,1,128]{3,2,1,0:T(1,128)S(1)}, f32[4,3,1,128]{3,2,1,0:T(1,128)S(1)}) custom-call(bf16[592,256]{1,0:T(8,128)(2,1)S(1)} %collective-permute-done.4.prev_ref, bf16[592,256]{1,0:T(8,128)(2,1)S(1)} %collective-permute-done.5.next_ref, ...), custom_call_target="tpu_custom_call" | custom-call | flops 8153726976 | bytes 1048576 | tf_op jit(solution)/shard_map/energy/pallas_call | solution.py:877
  47.6 1.6 %collective-permute-start.6 = (f32[4,3,1,128]{3,2,1,0:T(1,128)S(1)}, f32[4,3,1,128]{3,2,1,0:T(1,128)S(1)}, u32[]{:S(2)}, u32[]{:S(2)}) collective-permute-start(f32[4,3,1,128]{3,2,1,0:T(1,128)S(1)} %get-tuple-element.61), channel_id=1, source_target_pairs={{0,3},{1,0},{2,1},{3,2},{4,7},{5,4},{6,5},{7,6},{8,11},{9,8},{10,9... | collective-permute-start | bytes 18440 | tf_op jit(solution)/shard_map/ppermute | solution.py:23
  49.1 0.0 collective-permute-start.7
  49.1 0.0 copy-done.1
  49.1 0.9 %collective-permute-done.6 = f32[4,3,1,128]{3,2,1,0:T(1,128)S(1)} collective-permute-done((f32[4,3,1,128]{3,2,1,0:T(1,128)S(1)}, f32[4,3,1,128]{3,2,1,0:T(1,128)S(1)}, u32[]{:S(2)}, u32[]{:S(2)}) %collective-permute-start.6) | collective-permute-done | bytes 6176 | tf_op jit(solution)/shard_map/ppermute | solution.py:23
  50.1 3.3 %collective-permute-done.7 = f32[4,3,1,128]{3,2,1,0:T(1,128)S(1)} collective-permute-done((f32[4,3,1,128]{3,2,1,0:T(1,128)S(1)}, f32[4,3,1,128]{3,2,1,0:T(1,128)S(1)}, u32[]{:S(2)}, u32[]{:S(2)}) %collective-permute-start.7) | collective-permute-done | bytes 6176 | tf_op jit(solution)/shard_map/ppermute | solution.py:23
  53.4 1.9 %collective-permute-start.8 = (f32[4,3,1,128]{3,2,1,0:T(1,128)S(1)}, f32[4,3,1,128]{3,2,1,0:T(1,128)S(1)}, u32[]{:S(2)}, u32[]{:S(2)}) collective-permute-start(f32[4,3,1,128]{3,2,1,0:T(1,128)S(1)} %pad_maximum_fusion), channel_id=1, source_target_pairs={{4,0},{8,4},{12,8},{16,12},{20,16},{24,20},{28,24},{5,1},{9,5},{13... | collective-permute-start | bytes 18440 | tf_op jit(solution)/shard_map/ppermute | solution.py:29
  55.4 3.9 %collective-permute-done.8.ahead = f32[4,3,1,128]{3,2,1,0:T(1,128)S(1)} collective-permute-done((f32[4,3,1,128]{3,2,1,0:T(1,128)S(1)}, f32[4,3,1,128]{3,2,1,0:T(1,128)S(1)}, u32[]{:S(2)}, u32[]{:S(2)}) %collective-permute-start.8) | collective-permute-done | bytes 6176 | tf_op jit(solution)/shard_map/ppermute | solution.py:29
  59.3 0.0 copy-done
  59.3 0.0 copy-done.2
  59.3 0.0 copy-done.3
  59.3 0.6 finish.1
  (7 shorter events, 0.0 us)
Async XLA Ops:
  1.7 17.8 %collective-permute-start = (bf16[2,1,592,128]{3,2,1,0:T(8,128)(2,1)S(1)}, bf16[2,1,592,128]{3,2,1,0:T(8,128)(2,1)S(1)}, u32[]{:S(2)}, u32[]{:S(2)}) collective-permute-start(bf16[2,1,592,128]{3,2,1,0:T(8,128)(2,1)S(1)} %pack.1.own_ref), channel_id=1, source_target_pairs={{0,1},{1,2},{2,3},{3,0},{4,5},{5,6},{6,7},{7,4},{8,9},{9,10},{10,1... | collective-permute-start | bytes 909320 | tf_op jit(solution)/shard_map/ppermute | solution.py:23
  3.0 16.5 %collective-permute-start.1 = (bf16[2,1,592,128]{3,2,1,0:T(8,128)(2,1)S(1)}, bf16[2,1,592,128]{3,2,1,0:T(8,128)(2,1)S(1)}, u32[]{:S(2)}, u32[]{:S(2)}) collective-permute-start(bf16[2,1,592,128]{3,2,1,0:T(8,128)(2,1)S(1)} %pack.1.own_ref), channel_id=1, source_target_pairs={{0,3},{1,0},{2,1},{3,2},{4,7},{5,4},{6,5},{7,6},{8,11},{9,8},{10,9... | collective-permute-start | bytes 909320 | tf_op jit(solution)/shard_map/ppermute | solution.py:23
  5.1 11.0 %collective-permute-start.2 = (bf16[1,1,592,128]{3,2,1,0:T(8,128)(2,1)S(1)}, bf16[1,1,592,128]{3,2,1,0:T(8,128)(2,1)S(1)}, u32[]{:S(2)}, u32[]{:S(2)}) collective-permute-start(bf16[1,1,592,128]{3,2,1,0:T(8,128)(2,1)S(1)} %get-tuple-element.69), channel_id=1, source_target_pairs={{0,4},{4,8},{8,12},{12,16},{16,20},{20,24},{24,28},{1,5},{5,9},{9,... | collective-permute-start | bytes 454664 | tf_op jit(solution)/shard_map/ppermute | solution.py:29
  9.3 7.4 %collective-permute-start.3 = (bf16[1,1,592,128]{3,2,1,0:T(8,128)(2,1)S(1)}, bf16[1,1,592,128]{3,2,1,0:T(8,128)(2,1)S(1)}, u32[]{:S(2)}, u32[]{:S(2)}) collective-permute-start(bf16[1,1,592,128]{3,2,1,0:T(8,128)(2,1)S(1)} %get-tuple-element.68), channel_id=1, source_target_pairs={{4,0},{8,4},{12,8},{16,12},{20,16},{24,20},{28,24},{5,1},{9,5},{13... | collective-permute-start | bytes 454664 | tf_op jit(solution)/shard_map/ppermute | solution.py:29
  19.6 10.9 %collective-permute-start.4 = (bf16[592,256]{1,0:T(8,128)(2,1)S(1)}, bf16[592,256]{1,0:T(8,128)(2,1)S(1)}, u32[]{:S(2)}, u32[]{:S(2)}) collective-permute-start(bf16[592,256]{1,0:T(8,128)(2,1)S(1)} %get-tuple-element.51), channel_id=1, source_target_pairs={{0,4},{4,8},{8,12},{12,16},{16,20},{20,24},{24,28},{1,5},{5,9},{9,... | collective-permute-start | bytes 909320 | tf_op jit(solution)/shard_map/ppermute | solution.py:29
  23.6 9.0 %collective-permute-start.5 = (bf16[592,256]{1,0:T(8,128)(2,1)S(1)}, bf16[592,256]{1,0:T(8,128)(2,1)S(1)}, u32[]{:S(2)}, u32[]{:S(2)}) collective-permute-start(bf16[592,256]{1,0:T(8,128)(2,1)S(1)} %get-tuple-element.52), channel_id=1, source_target_pairs={{4,0},{8,4},{12,8},{16,12},{20,16},{24,20},{28,24},{5,1},{9,5},{13... | collective-permute-start | bytes 909320 | tf_op jit(solution)/shard_map/ppermute | solution.py:29
  32.7 16.5 %copy-start.1 = (f32[2,1,3,128]{3,1,2,0:T(1,128)S(1)}, f32[2,1,3,128]{3,1,2,0:T(1,128)}, u32[]{:S(2)}) copy-start(f32[2,1,3,128]{3,1,2,0:T(1,128)} %param.16) | copy-start | bytes 9220
  32.7 26.6 %copy-start = (f32[2,1,3,128]{3,1,2,0:T(1,128)S(1)}, f32[2,1,3,128]{3,1,2,0:T(1,128)}, u32[]{:S(2)}) copy-start(f32[2,1,3,128]{3,1,2,0:T(1,128)} %param.15) | copy-start | bytes 9220
  32.7 26.6 %copy-start.2 = (f32[1,3,128]{2,0,1:T(1,128)S(1)}, f32[1,3,128]{2,0,1:T(1,128)}, u32[]{:S(2)}) copy-start(f32[1,3,128]{2,0,1:T(1,128)} %param.24) | copy-start | bytes 4612
  32.7 26.6 %copy-start.3 = (f32[1,3,128]{2,0,1:T(1,128)S(1)}, f32[1,3,128]{2,0,1:T(1,128)}, u32[]{:S(2)}) copy-start(f32[1,3,128]{2,0,1:T(1,128)} %param.25) | copy-start | bytes 4612
  47.6 2.5 %collective-permute-start.6 = (f32[4,3,1,128]{3,2,1,0:T(1,128)S(1)}, f32[4,3,1,128]{3,2,1,0:T(1,128)S(1)}, u32[]{:S(2)}, u32[]{:S(2)}) collective-permute-start(f32[4,3,1,128]{3,2,1,0:T(1,128)S(1)} %get-tuple-element.61), channel_id=1, source_target_pairs={{0,3},{1,0},{2,1},{3,2},{4,7},{5,4},{6,5},{7,6},{8,11},{9,8},{10,9... | collective-permute-start | bytes 18440 | tf_op jit(solution)/shard_map/ppermute | solution.py:23
  49.1 4.3 %collective-permute-start.7 = (f32[4,3,1,128]{3,2,1,0:T(1,128)S(1)}, f32[4,3,1,128]{3,2,1,0:T(1,128)S(1)}, u32[]{:S(2)}, u32[]{:S(2)}) collective-permute-start(f32[4,3,1,128]{3,2,1,0:T(1,128)S(1)} %get-tuple-element.62), channel_id=1, source_target_pairs={{0,1},{1,2},{2,3},{3,0},{4,5},{5,6},{6,7},{7,4},{8,9},{9,10},{10,1... | collective-permute-start | bytes 18440 | tf_op jit(solution)/shard_map/ppermute | solution.py:23
  53.4 5.8 %collective-permute-start.8 = (f32[4,3,1,128]{3,2,1,0:T(1,128)S(1)}, f32[4,3,1,128]{3,2,1,0:T(1,128)S(1)}, u32[]{:S(2)}, u32[]{:S(2)}) collective-permute-start(f32[4,3,1,128]{3,2,1,0:T(1,128)S(1)} %pad_maximum_fusion), channel_id=1, source_target_pairs={{4,0},{8,4},{12,8},{16,12},{20,16},{24,20},{28,24},{5,1},{9,5},{13... | collective-permute-start | bytes 18440 | tf_op jit(solution)/shard_map/ppermute | solution.py:29
